TPU v7x, 32 devices: a whole 2x2x4 slice. The times are simulated.
32 devices in a mesh: seq: 4 (over z), fsdp: 8 (over y, x, core).
Axes of the slice: x: 2, y: 2, z: 4, core: 2. Of those that a mesh axis runs over, the one named last changes fastest.
Arguments:
- tokens: bfloat16 [16, 2048, 768], P('fsdp', 'seq'), may hold values from -6 to 6
- segment_ids: int32 [16, 2048], P('fsdp', 'seq'), may hold values from 0 to 64, as said below
- cotangent: bfloat16 [16, 2048, 768], P('fsdp', 'seq'), may hold values from -6 to 6
- w_qkv: float32 [768, 2304], P(('seq', 'fsdp')), may hold values from -0.21875 to 0.21875
- w_out: float32 [768, 768], P(('seq', 'fsdp')), may hold values from -0.875 to 0.875
- w_gate: float32 [768, 3072], P(('seq', 'fsdp')), may hold values from -0.21875 to 0.21875
- w_up: float32 [768, 3072], P(('seq', 'fsdp')), may hold values from -0.21875 to 0.21875
- w_down: float32 [3072, 768], P(('seq', 'fsdp')), may hold values from -0.15625 to 0.15625
- norm_params: float32 [4, 768], P(None, ('seq', 'fsdp')), may hold values from -0.5 to 2.4
- first_qkv: float32 [768, 2304], P(('seq', 'fsdp')), may hold values from -0.00021362305 to 0.00021362305
- first_out: float32 [768, 768], P(('seq', 'fsdp')), may hold values from -0.00021362305 to 0.00021362305
- first_gate: float32 [768, 3072], P(('seq', 'fsdp')), may hold values from -0.00021362305 to 0.00021362305
- first_up: float32 [768, 3072], P(('seq', 'fsdp')), may hold values from -0.00021362305 to 0.00021362305
- first_down: float32 [3072, 768], P(('seq', 'fsdp')), may hold values from -0.00021362305 to 0.00021362305
- first_norms: float32 [4, 768], P(None, ('seq', 'fsdp')), may hold values from -0.0008544922 to 0.0008544922
- second_qkv: float32 [768, 2304], P(('seq', 'fsdp')), may hold values from 5.2964664e-11 to 8.474346e-10
- second_out: float32 [768, 768], P(('seq', 'fsdp')), may hold values from 1.0592933e-11 to 8.474346e-11
- second_gate: float32 [768, 3072], P(('seq', 'fsdp')), may hold values from 5.2964664e-11 to 8.474346e-10
- second_up: float32 [768, 3072], P(('seq', 'fsdp')), may hold values from 5.2964664e-11 to 8.474346e-10
- second_down: float32 [3072, 768], P(('seq', 'fsdp')), may hold values from 5.2964664e-11 to 8.474346e-10
- second_norms: float32 [4, 768], P(None, ('seq', 'fsdp')), may hold values from 8.474346e-10 to 1.3558954e-08
Outputs:
- output: bfloat16 [16, 2048, 768], P('fsdp', 'seq')
- input_grad: float32 [16, 2048, 768], P('fsdp', 'seq')
- grad_qkv: float32 [768, 2304], P(('seq', 'fsdp'))
- grad_out: float32 [768, 768], P(('seq', 'fsdp'))
- grad_gate: float32 [768, 3072], P(('seq', 'fsdp'))
- grad_up: float32 [768, 3072], P(('seq', 'fsdp'))
- grad_down: float32 [3072, 768], P(('seq', 'fsdp'))
- grad_norms: float32 [4, 768], P(None, ('seq', 'fsdp'))
- new_qkv: float32 [768, 2304], P(('seq', 'fsdp'))
- new_out: float32 [768, 768], P(('seq', 'fsdp'))
- new_gate: float32 [768, 3072], P(('seq', 'fsdp'))
- new_up: float32 [768, 3072], P(('seq', 'fsdp'))
- new_down: float32 [3072, 768], P(('seq', 'fsdp'))
- new_norms: float32 [4, 768], P(None, ('seq', 'fsdp'))
- new_first_qkv: float32 [768, 2304], P(('seq', 'fsdp'))
- new_first_out: float32 [768, 768], P(('seq', 'fsdp'))
- new_first_gate: float32 [768, 3072], P(('seq', 'fsdp'))
- new_first_up: float32 [768, 3072], P(('seq', 'fsdp'))
- new_first_down: float32 [3072, 768], P(('seq', 'fsdp'))
- new_first_norms: float32 [4, 768], P(None, ('seq', 'fsdp'))
- new_second_qkv: float32 [768, 2304], P(('seq', 'fsdp'))
- new_second_out: float32 [768, 768], P(('seq', 'fsdp'))
- new_second_gate: float32 [768, 3072], P(('seq', 'fsdp'))
- new_second_up: float32 [768, 3072], P(('seq', 'fsdp'))
- new_second_down: float32 [3072, 768], P(('seq', 'fsdp'))
- new_second_norms: float32 [4, 768], P(None, ('seq', 'fsdp'))
- grad_norm: float32 [], replicated
Inputs may be any that keep to these rules, and one draw needn't show every extreme that they name: `segment_ids`: within each sequence the ids start at 0 and rise by 0 or 1 from one position to the next, never above 64.
All inputs are finite; a program needn't handle non-finite values.
Results may differ from a plain program's by a relative error of at most 0.015.
Values may be sent and summed in bfloat16 or wider, within the bound.
A program may use at most 192 MiB of HBM per device.

v0:
```python
import math

import jax
import jax.numpy as jnp
from jax import lax
from jax.sharding import PartitionSpec as P

HEADS = 12
HEAD_DIM = 64
STEP = 10


EPS_NORM = 1e-06
ROPE_BASE = 1000.0
MASKED_SCORE = -1e30
MAX_NORM = 1.0
LEARN_RATE = 0.1
NORM_RATE = 0.6
BETA_ONE = 0.9
BETA_TWO = 0.999
ADAM_EPS = 1e-08
WEIGHT_DECAY = 0.01


def rotate(field, positions, sign_rot):
    shape_in = field.shape
    heads_view = field.reshape(shape_in[:-1] + (HEADS, HEAD_DIM))
    half_dim = HEAD_DIM // 2
    inverse = jnp.exp(
        jnp.arange(half_dim, dtype=jnp.float32) * (-2.0 * math.log(ROPE_BASE) / HEAD_DIM)
    )
    angles = positions[:, None] * inverse[None, :]
    cosine = jnp.cos(angles)[:, None, :]
    sine = jnp.sin(angles)[:, None, :] * sign_rot
    first_half = heads_view[..., :half_dim]
    second_half = heads_view[..., half_dim:]
    turned = jnp.concatenate(
        [first_half * cosine - second_half * sine, second_half * cosine + first_half * sine], -1
    )
    return turned.reshape(shape_in)


def normalize(resid, gain, shift):
    mean_row = jnp.mean(resid, -1, keepdims=True)
    centered = resid - mean_row
    inv_std = lax.rsqrt(jnp.mean(centered * centered, -1, keepdims=True) + EPS_NORM)
    normed = centered * inv_std
    return (normed * gain + shift, normed, inv_std)


def normalize_back(grad_in, normed, inv_std, gain):
    scaled = grad_in * gain
    return inv_std * (
        scaled
        - jnp.mean(scaled, -1, keepdims=True)
        - normed * jnp.mean(scaled * normed, -1, keepdims=True)
    )


def attend(query, keys, values, same_doc, score_scale):
    seq_count, local_len, model_width = query.shape

    def one_head(head_index, carried):
        out_all, log_sums = carried
        col_start = head_index * HEAD_DIM
        query_head = lax.dynamic_slice_in_dim(query, col_start, HEAD_DIM, 2)
        key_head = lax.dynamic_slice_in_dim(keys, col_start, HEAD_DIM, 2)
        value_head = lax.dynamic_slice_in_dim(values, col_start, HEAD_DIM, 2)
        raw_scores = jnp.einsum(
            "sqd,skd->sqk", query_head, key_head, preferred_element_type=jnp.float32
        )
        scores = jnp.where(same_doc, raw_scores * score_scale, MASKED_SCORE)
        row_max = jnp.max(scores, -1, keepdims=True)
        exp_scores = jnp.exp(scores - row_max)
        row_sums = jnp.sum(exp_scores, -1, keepdims=True)
        attn_prob = (exp_scores / row_sums).astype(jnp.bfloat16)
        head_out = jnp.einsum(
            "sqk,skd->sqd", attn_prob, value_head, preferred_element_type=jnp.float32
        )
        out_all = lax.dynamic_update_slice_in_dim(out_all, head_out, col_start, 2)
        log_sums = lax.dynamic_update_index_in_dim(
            log_sums, (row_max + jnp.log(row_sums))[..., 0], head_index, 0
        )
        return (out_all, log_sums)

    start_state = (
        jnp.zeros((seq_count, local_len, model_width), jnp.float32),
        jnp.zeros((HEADS, seq_count, local_len), jnp.float32),
    )
    return lax.fori_loop(0, HEADS, one_head, start_state)


def attend_back(query, keys, values, same_doc, log_sums, grad_attended, score_scale):
    seq_count, local_len, model_width = query.shape
    key_len = keys.shape[1]

    def one_head(head_index, carried):
        dq_all, dk_all, dv_all = carried
        col_start = head_index * HEAD_DIM
        query_head = lax.dynamic_slice_in_dim(query, col_start, HEAD_DIM, 2)
        key_head = lax.dynamic_slice_in_dim(keys, col_start, HEAD_DIM, 2)
        value_head = lax.dynamic_slice_in_dim(values, col_start, HEAD_DIM, 2)
        grad_head = lax.dynamic_slice_in_dim(grad_attended, col_start, HEAD_DIM, 2)
        head_sums = lax.dynamic_index_in_dim(log_sums, head_index, 0, keepdims=False)
        raw_scores = jnp.einsum(
            "sqd,skd->sqk", query_head, key_head, preferred_element_type=jnp.float32
        )
        scores = jnp.where(same_doc, raw_scores * score_scale, MASKED_SCORE)
        attn_prob = jnp.exp(scores - head_sums[..., None])
        grad_prob = jnp.einsum(
            "sqd,skd->sqk", grad_head, value_head, preferred_element_type=jnp.float32
        )
        dv_head = jnp.einsum(
            "sqk,sqd->skd",
            attn_prob.astype(jnp.bfloat16),
            grad_head,
            preferred_element_type=jnp.float32,
        )
        row_dots = jnp.sum(attn_prob * grad_prob, -1, keepdims=True)
        grad_scores = (attn_prob * (grad_prob - row_dots)).astype(jnp.bfloat16)
        dq_head = (
            jnp.einsum("sqk,skd->sqd", grad_scores, key_head, preferred_element_type=jnp.float32)
            * score_scale
        )
        dk_head = (
            jnp.einsum("sqk,sqd->skd", grad_scores, query_head, preferred_element_type=jnp.float32)
            * score_scale
        )
        dq_all = lax.dynamic_update_slice_in_dim(dq_all, dq_head, col_start, 2)
        dk_all = lax.dynamic_update_slice_in_dim(dk_all, dk_head, col_start, 2)
        dv_all = lax.dynamic_update_slice_in_dim(dv_all, dv_head, col_start, 2)
        return (dq_all, dk_all, dv_all)

    start_state = (
        jnp.zeros((seq_count, local_len, model_width), jnp.float32),
        jnp.zeros((seq_count, key_len, model_width), jnp.float32),
        jnp.zeros((seq_count, key_len, model_width), jnp.float32),
    )
    return lax.fori_loop(0, HEADS, one_head, start_state)


def adam_update(weight, gradient, moment_one, moment_two, decay_rate, step_rate, clip_factor):
    clipped = gradient * clip_factor
    first_new = BETA_ONE * moment_one + (1.0 - BETA_ONE) * clipped
    second_new = BETA_TWO * moment_two + (1.0 - BETA_TWO) * clipped * clipped
    first_fix = 1.0 - BETA_ONE**STEP
    second_fix = 1.0 - BETA_TWO**STEP
    direction = (
        first_new / first_fix / (jnp.sqrt(second_new / second_fix) + ADAM_EPS) + decay_rate * weight
    )
    return (weight - step_rate * direction, first_new, second_new)


def per_device(
    tokens,
    segment_ids,
    cotangent,
    w_qkv,
    w_out,
    w_gate,
    w_up,
    w_down,
    norm_params,
    first_qkv,
    first_out,
    first_gate,
    first_up,
    first_down,
    first_norms,
    second_qkv,
    second_out,
    second_gate,
    second_up,
    second_down,
    second_norms,
):
    seq_count, local_len, model_width = tokens.shape
    row_count = seq_count * local_len
    score_scale = 1.0 / math.sqrt(HEAD_DIM)
    lowered_qkv = w_qkv.astype(jnp.bfloat16)
    lowered_out = w_out.astype(jnp.bfloat16)
    lowered_gate = w_gate.astype(jnp.bfloat16)
    lowered_up = w_up.astype(jnp.bfloat16)
    lowered_down = w_down.astype(jnp.bfloat16)
    lowered_norms = norm_params.astype(jnp.bfloat16)
    full_qkv, full_out, full_gate, full_up, full_down, full_norms = (
        lax.all_gather(lowered_qkv, ("seq", "fsdp"), axis=0, tiled=True),
        lax.all_gather(lowered_out, ("seq", "fsdp"), axis=0, tiled=True),
        lax.all_gather(lowered_gate, ("seq", "fsdp"), axis=0, tiled=True),
        lax.all_gather(lowered_up, ("seq", "fsdp"), axis=0, tiled=True),
        lax.all_gather(lowered_down, ("seq", "fsdp"), axis=0, tiled=True),
        lax.all_gather(lowered_norms, ("seq", "fsdp"), axis=1, tiled=True),
    )
    gains = full_norms.astype(jnp.float32)
    gain_one, shift_one, gain_two, shift_two = (gains[0], gains[1], gains[2], gains[3])
    positions = (lax.axis_index("seq") * local_len + jnp.arange(local_len)).astype(jnp.float32)
    flat_rows = tokens.reshape(row_count, model_width)
    projected = jnp.dot(flat_rows, full_qkv, preferred_element_type=jnp.float32).reshape(
        seq_count, local_len, 3 * model_width
    )
    query = rotate(projected[..., :model_width], positions, 1.0).astype(jnp.bfloat16)
    keys_local = rotate(projected[..., model_width : 2 * model_width], positions, 1.0).astype(
        jnp.bfloat16
    )
    values_local = projected[..., 2 * model_width :].astype(jnp.bfloat16)
    keys_all, values_all, key_segments = (
        lax.all_gather(keys_local, "seq", axis=1, tiled=True),
        lax.all_gather(values_local, "seq", axis=1, tiled=True),
        lax.all_gather(segment_ids, "seq", axis=1, tiled=True),
    )
    same_doc = segment_ids[:, :, None] == key_segments[:, None, :]
    attended, log_sums = attend(query, keys_all, values_all, same_doc, score_scale)
    attended_low = attended.astype(jnp.bfloat16).reshape(row_count, model_width)
    resid_one = flat_rows.astype(jnp.float32) + jnp.dot(
        attended_low, full_out, preferred_element_type=jnp.float32
    )
    hidden, normed_one, inv_std_one = normalize(resid_one, gain_one, shift_one)
    hidden_low = hidden.astype(jnp.bfloat16)
    gate_proj = jnp.dot(hidden_low, full_gate, preferred_element_type=jnp.float32)
    up_proj = jnp.dot(hidden_low, full_up, preferred_element_type=jnp.float32)
    sigmoid_gate = jax.nn.sigmoid(gate_proj)
    silu_gate = gate_proj * sigmoid_gate
    mixed_low = (silu_gate * up_proj).astype(jnp.bfloat16)
    resid_two = hidden + jnp.dot(mixed_low, full_down, preferred_element_type=jnp.float32)
    result, normed_two, inv_std_two = normalize(resid_two, gain_two, shift_two)
    output = result.astype(jnp.bfloat16).reshape(seq_count, local_len, model_width)
    back_qkv, back_out, back_gate, back_up, back_down = (
        lax.all_gather(lowered_qkv, ("seq", "fsdp"), axis=0, tiled=True),
        lax.all_gather(lowered_out, ("seq", "fsdp"), axis=0, tiled=True),
        lax.all_gather(lowered_gate, ("seq", "fsdp"), axis=0, tiled=True),
        lax.all_gather(lowered_up, ("seq", "fsdp"), axis=0, tiled=True),
        lax.all_gather(lowered_down, ("seq", "fsdp"), axis=0, tiled=True),
    )
    grad_result = cotangent.reshape(row_count, model_width).astype(jnp.float32)
    d_gain_two = jnp.sum(grad_result * normed_two, 0)
    d_shift_two = jnp.sum(grad_result, 0)
    d_resid_two = normalize_back(grad_result, normed_two, inv_std_two, gain_two)
    d_ff_low = d_resid_two.astype(jnp.bfloat16)
    g_down = jnp.einsum("rf,rd->fd", mixed_low, d_ff_low, preferred_element_type=jnp.float32)
    d_mixed = jnp.einsum("rd,fd->rf", d_ff_low, back_down, preferred_element_type=jnp.float32)
    d_up_low = (d_mixed * silu_gate).astype(jnp.bfloat16)
    d_gate_low = (
        d_mixed * up_proj * sigmoid_gate * (1.0 + gate_proj * (1.0 - sigmoid_gate))
    ).astype(jnp.bfloat16)
    g_gate = jnp.einsum("rd,rf->df", hidden_low, d_gate_low, preferred_element_type=jnp.float32)
    g_up = jnp.einsum("rd,rf->df", hidden_low, d_up_low, preferred_element_type=jnp.float32)
    d_hidden = (
        d_resid_two
        + jnp.einsum("rf,df->rd", d_gate_low, back_gate, preferred_element_type=jnp.float32)
        + jnp.einsum("rf,df->rd", d_up_low, back_up, preferred_element_type=jnp.float32)
    )
    d_gain_one = jnp.sum(d_hidden * normed_one, 0)
    d_shift_one = jnp.sum(d_hidden, 0)
    d_resid_one = normalize_back(d_hidden, normed_one, inv_std_one, gain_one)
    d_branch_low = d_resid_one.astype(jnp.bfloat16)
    g_out = jnp.einsum("rd,re->de", attended_low, d_branch_low, preferred_element_type=jnp.float32)
    d_attended_low = (
        jnp.einsum("re,de->rd", d_branch_low, back_out, preferred_element_type=jnp.float32)
        .astype(jnp.bfloat16)
        .reshape(seq_count, local_len, model_width)
    )
    keys_back, values_back = (
        lax.all_gather(keys_local, "seq", axis=1, tiled=True),
        lax.all_gather(values_local, "seq", axis=1, tiled=True),
    )
    d_query, d_keys, d_values = attend_back(
        query, keys_back, values_back, same_doc, log_sums, d_attended_low, score_scale
    )
    d_keys_local, d_values_local = (
        lax.psum_scatter(
            d_keys.astype(jnp.bfloat16), "seq", scatter_dimension=1, tiled=True
        ).astype(jnp.float32),
        lax.psum_scatter(
            d_values.astype(jnp.bfloat16), "seq", scatter_dimension=1, tiled=True
        ).astype(jnp.float32),
    )
    d_projected_low = (
        jnp.concatenate(
            [
                rotate(d_query, positions, -1.0),
                rotate(d_keys_local, positions, -1.0),
                d_values_local,
            ],
            -1,
        )
        .astype(jnp.bfloat16)
        .reshape(row_count, 3 * model_width)
    )
    g_qkv = jnp.einsum("rd,re->de", flat_rows, d_projected_low, preferred_element_type=jnp.float32)
    input_grad = (
        d_resid_one
        + jnp.einsum("re,de->rd", d_projected_low, back_qkv, preferred_element_type=jnp.float32)
    ).reshape(seq_count, local_len, model_width)
    g_norms = jnp.stack([d_gain_one, d_shift_one, d_gain_two, d_shift_two])
    red_qkv, red_out, red_gate, red_up, red_down, red_norms = (
        lax.psum_scatter(g_qkv, ("seq", "fsdp"), scatter_dimension=0, tiled=True),
        lax.psum_scatter(g_out, ("seq", "fsdp"), scatter_dimension=0, tiled=True),
        lax.psum_scatter(g_gate, ("seq", "fsdp"), scatter_dimension=0, tiled=True),
        lax.psum_scatter(g_up, ("seq", "fsdp"), scatter_dimension=0, tiled=True),
        lax.psum_scatter(g_down, ("seq", "fsdp"), scatter_dimension=0, tiled=True),
        lax.psum_scatter(g_norms, ("seq", "fsdp"), scatter_dimension=1, tiled=True),
    )
    local_squares = (
        jnp.sum(red_qkv * red_qkv)
        + jnp.sum(red_out * red_out)
        + jnp.sum(red_gate * red_gate)
        + jnp.sum(red_up * red_up)
        + jnp.sum(red_down * red_down)
        + jnp.sum(red_norms * red_norms)
    )
    squares_sum = lax.psum(local_squares, ("seq", "fsdp"))
    grad_norm = jnp.sqrt(squares_sum)
    clip_factor = jnp.minimum(1.0, MAX_NORM / (grad_norm + 1e-06))
    new_qkv, mom_qkv, sec_qkv = adam_update(
        w_qkv, red_qkv, first_qkv, second_qkv, WEIGHT_DECAY, LEARN_RATE, clip_factor
    )
    new_out, mom_out, sec_out = adam_update(
        w_out, red_out, first_out, second_out, WEIGHT_DECAY, LEARN_RATE, clip_factor
    )
    new_gate, mom_gate, sec_gate = adam_update(
        w_gate, red_gate, first_gate, second_gate, WEIGHT_DECAY, LEARN_RATE, clip_factor
    )
    new_up, mom_up, sec_up = adam_update(
        w_up, red_up, first_up, second_up, WEIGHT_DECAY, LEARN_RATE, clip_factor
    )
    new_down, mom_down, sec_down = adam_update(
        w_down, red_down, first_down, second_down, WEIGHT_DECAY, LEARN_RATE, clip_factor
    )
    new_norms, mom_norms, sec_norms = adam_update(
        norm_params, red_norms, first_norms, second_norms, 0.0, NORM_RATE, clip_factor
    )
    return (
        output,
        input_grad,
        red_qkv,
        red_out,
        red_gate,
        red_up,
        red_down,
        red_norms,
        new_qkv,
        new_out,
        new_gate,
        new_up,
        new_down,
        new_norms,
        mom_qkv,
        mom_out,
        mom_gate,
        mom_up,
        mom_down,
        mom_norms,
        sec_qkv,
        sec_out,
        sec_gate,
        sec_up,
        sec_down,
        sec_norms,
        grad_norm,
    )


def solution(mesh):
    return jax.shard_map(
        per_device,
        mesh=mesh,
        in_specs=(
            P("fsdp", "seq", None),
            P("fsdp", "seq"),
            P("fsdp", "seq", None),
            P(("seq", "fsdp"), None),
            P(("seq", "fsdp"), None),
            P(("seq", "fsdp"), None),
            P(("seq", "fsdp"), None),
            P(("seq", "fsdp"), None),
            P(None, ("seq", "fsdp")),
            P(("seq", "fsdp"), None),
            P(("seq", "fsdp"), None),
            P(("seq", "fsdp"), None),
            P(("seq", "fsdp"), None),
            P(("seq", "fsdp"), None),
            P(None, ("seq", "fsdp")),
            P(("seq", "fsdp"), None),
            P(("seq", "fsdp"), None),
            P(("seq", "fsdp"), None),
            P(("seq", "fsdp"), None),
            P(("seq", "fsdp"), None),
            P(None, ("seq", "fsdp")),
        ),
        out_specs=(
            P("fsdp", "seq", None),
            P("fsdp", "seq", None),
            P(("seq", "fsdp"), None),
            P(("seq", "fsdp"), None),
            P(("seq", "fsdp"), None),
            P(("seq", "fsdp"), None),
            P(("seq", "fsdp"), None),
            P(None, ("seq", "fsdp")),
            P(("seq", "fsdp"), None),
            P(("seq", "fsdp"), None),
            P(("seq", "fsdp"), None),
            P(("seq", "fsdp"), None),
            P(("seq", "fsdp"), None),
            P(None, ("seq", "fsdp")),
            P(("seq", "fsdp"), None),
            P(("seq", "fsdp"), None),
            P(("seq", "fsdp"), None),
            P(("seq", "fsdp"), None),
            P(("seq", "fsdp"), None),
            P(None, ("seq", "fsdp")),
            P(("seq", "fsdp"), None),
            P(("seq", "fsdp"), None),
            P(("seq", "fsdp"), None),
            P(("seq", "fsdp"), None),
            P(("seq", "fsdp"), None),
            P(None, ("seq", "fsdp")),
            P(),
        ),
        check_vma=False,
    )
```

profile of v0, /device:TPU:0, one launch (start us, length us, event | category | flops | bytes accessed | tf_op | source)
XLA Modules:
  0.0 1893.9 jit_solution(6681185445260502215)
XLA Ops:
  8.9 65.4 %all-gather.9.cloned.1.call-done = bf16[768,2304]{1,0:T(8,128)(2,1)} async-done(((bf16[24,2304]{1,0:T(8,128)(2,1)}), bf16[768,2304]{1,0:T(8,128)(2,1)}) %all-gather.9.cloned.1.call-update) | async-done | bytes 3538960 | tf_op jit(solution)/shard_map/all_gather | solution.py:187
  107.7 15.9 all_gather.36
  123.6 39.1 %all-gather = bf16[32,24,4]{1,2,0:T(4,128)(2,1)S(1)} all-gather(bf16[1,24,4]{1,2,0:T(4,128)(2,1)S(1)} %convert_bitcast_fusion), channel_id=1, replica_groups=mesh['seq'=4,'fsdp'=8] {'seq','fsdp'}, dimensions={0}, use_global_device_ids=true | all-gather | bytes 6336 | tf_op jit(solution)/shard_map/all_gather | solution.py:192
  165.8 34.3 %all-gather.13.cloned.1.call-done = bf16[2,2048,768]{2,1,0:T(8,128)(2,1)} async-done(((bf16[2,512,768]{2,1,0:T(8,128)(2,1)}), bf16[2,2048,768]{2,1,0:T(8,128)(2,1)}) %all-gather.13.cloned.1.call-update) | async-done | bytes 6291472 | tf_op jit(solution)/shard_map/all_gather | solution.py:208
  200.1 8.8 copy.107
  209.0 107.0 %all-gather.11.cloned.1.call-done = bf16[2,2048,768]{1,2,0:T(8,128)(2,1)} async-done(((bf16[2,512,768]{1,2,0:T(8,128)(2,1)}), bf16[2,2048,768]{1,2,0:T(8,128)(2,1)}) %all-gather.11.cloned.1.call-update) | async-done | bytes 6291472 | tf_op jit(solution)/shard_map/all_gather | solution.py:207
  316.0 105.6 %while.34 = (s32[]{:T(128)}, bf16[2,512,768]{1,2,0:T(8,128)(2,1)S(1)}, f32[12,2,512]{2,1,0:T(2,128)S(1)}, bf16[2,512,768]{1,2,0:T(8,128)(2,1)S(1)}, bf16[2,2048,...) while((s32[]{:T(128)}, ...), condition=%wide.region_3.4_spmd.clone, body=%wide.region_0.3_spmd.clone.sunk | while | flops 568327168 | bytes 26704048 | solution.py:90
  429.3 8.7 all-gather.17.cloned.1.call-done
  438.0 10.1 fusion.86
  448.1 55.3 %all-gather.19.cloned.1.call-done = bf16[768,3072]{1,0:T(8,128)(2,1)} async-done(((bf16[24,3072]{1,0:T(8,128)(2,1)}), bf16[768,3072]{1,0:T(8,128)(2,1)}) %all-gather.19.cloned.1.call-update) | async-done | bytes 4718608 | tf_op jit(solution)/shard_map/all_gather | solution.py:190
  503.4 13.4 multiply_convert_fusion.3
  516.8 52.5 %all-gather.21.cloned.1.call-done = bf16[3072,768]{1,0:T(8,128)(2,1)} async-done(((bf16[96,768]{1,0:T(8,128)(2,1)}), bf16[3072,768]{1,0:T(8,128)(2,1)}) %all-gather.21.cloned.1.call-update) | async-done | bytes 4718608 | tf_op jit(solution)/shard_map/all_gather | solution.py:191
  569.3 9.1 fusion.85
  584.5 19.5 %multiply_convert_fusion.1 = (bf16[1024,3072]{1,0:T(8,128)(2,1)}, bf16[1024,3072]{1,0:T(8,128)(2,1)}) fusion(f32[1024,3072]{1,0:T(8,128)} %fusion.86, f32[1024,3072]{1,0:T(8,128)} %get-tuple-element.656, bf16[3072,768]{1,0:T(8,128)(2,1)} %all-gather.21.cloned.1.call-done, f32[1024,768]{1,0:T(8,128)} %get-tuple-element.644), kind=kOutput, calls=%fused_computation.42 | convolution fusion | flops 4873519104 | bytes 45613056 | tf_op jit(solution)/shard_map/rd,fd->rf/dot_general | solution.py:240
  604.0 9.2 fusion.87
  613.3 9.2 multiply_reduce_fusion.1
  635.1 307.3 %while.35 = (s32[]{:T(128)}, f32[2,512,768]{1,2,0:T(8,128)}, bf16[2,2048,768]{1,2,0:T(8,128)(2,1)}, bf16[2,2048,768]{1,2,0:T(8,128)(2,1)}, bf16[2,512,768]{1,2,0...) while((s32[]{:T(128)}, f32[2,512,768]{1,2,0:T(8,128)}, ...), condition=%wide.region_14.15_spmd.clone, body=%wide.region_12.14_spmd.clone.sunk | while | flops 1363475456 | bytes 147109200 | solution.py:139
  948.8 9.9 fusion.88
  960.2 10.5 fusion.89
  972.5 10.2 fusion.65
  982.8 69.4 %reduce-scatter.11.cloned.1.call-done = bf16[2,512,768]{1,2,0:T(8,128)(2,1)} async-done(((bf16[2,2048,768]{1,2,0:T(8,128)(2,1)}), bf16[2,512,768]{1,2,0:T(8,128)(2,1)}) %reduce-scatter.11.cloned.1.call-update) | async-done | bytes 1572880 | tf_op jit(solution)/shard_map/reduce_scatter | solution.py:270
  1055.3 110.5 %reduce-scatter.13.cloned.1.call-done = bf16[2,512,768]{1,2,0:T(8,128)(2,1)} async-done(((bf16[2,2048,768]{1,2,0:T(8,128)(2,1)}), bf16[2,512,768]{1,2,0:T(8,128)(2,1)}) %reduce-scatter.13.cloned.1.call-update) | async-done | bytes 1572880 | tf_op jit(solution)/shard_map/reduce_scatter | solution.py:273
  1165.8 8.6 convolution_bitcast_fusion
  1174.4 8.1 copy.119
  1183.2 41.2 %all-reduce = f32[4,768]{1,0:T(4,128)S(1)} all-reduce(f32[4,768]{1,0:T(4,128)S(1)} %pad_maximum_fusion.2), channel_id=9, replica_groups=mesh['seq'=4,'fsdp'=8] {'seq','fsdp'}, use_global_device_ids=true, to_apply=%region_26.27.clone | all-reduce | flops 3072 | bytes 24576
  1225.1 46.1 %reduce-scatter.15.cloned.1.call-done = f32[24,768]{1,0:T(8,128)} async-done(((f32[768,768]{1,0:T(8,128)}), f32[24,768]{1,0:T(8,128)}) %reduce-scatter.15.cloned.1.call-update) | async-done | bytes 73744 | tf_op jit(solution)/shard_map/reduce_scatter | solution.py:297
  1286.8 126.5 %reduce-scatter.17.cloned.1.call-done = f32[24,3072]{1,0:T(8,128)} async-done(((f32[768,3072]{1,0:T(8,128)}), f32[24,3072]{1,0:T(8,128)}) %reduce-scatter.17.cloned.1.call-update) | async-done | bytes 294928 | tf_op jit(solution)/shard_map/reduce_scatter | solution.py:298
  1415.0 139.3 %reduce-scatter.19.cloned.1.call-done = f32[24,3072]{1,0:T(8,128)} async-done(((f32[768,3072]{1,0:T(8,128)}), f32[24,3072]{1,0:T(8,128)}) %reduce-scatter.19.cloned.1.call-update) | async-done | bytes 294928 | tf_op jit(solution)/shard_map/reduce_scatter | solution.py:299
  1555.9 140.5 %reduce-scatter.21.cloned.1.call-done = f32[96,768]{1,0:T(8,128)} async-done(((f32[3072,768]{1,0:T(8,128)}), f32[96,768]{1,0:T(8,128)}) %reduce-scatter.21.cloned.1.call-update) | async-done | bytes 294928 | tf_op jit(solution)/shard_map/reduce_scatter | solution.py:300
  1698.0 122.7 %reduce-scatter.23.cloned.1.call-done = f32[24,2304]{1,0:T(8,128)} async-done(((f32[768,2304]{1,0:T(8,128)}), f32[24,2304]{1,0:T(8,128)}) %reduce-scatter.23.cloned.1.call-update) | async-done | bytes 221200
  1826.9 9.5 fusion.59
  1836.5 40.0 %psum.7 = f32[]{:T(128)} all-reduce(f32[]{:T(128)S(6)} %add.310), channel_id=1, replica_groups=mesh['seq'=4,'fsdp'=8] {'seq','fsdp'}, use_global_device_ids=true, to_apply=%region_33.34 | all-reduce | flops 1 | bytes 8 | tf_op jit(solution)/shard_map/psum | solution.py:311
  (421 shorter events, 521.4 us)
Async XLA Ops:
  7.2 67.1 %all-gather.9.cloned.1.call-start = ((), (), s32[]{:S(2)}) async-start(), calls=%async_computation.7 | async-start | bytes 3649536 | tf_op jit(solution)/shard_map/all_gather | solution.py:187
  8.9 191.2 %all-gather.13.cloned.1.call-start = ((), (), s32[]{:S(2)}) async-start(), calls=%async_computation.9 | async-start | bytes 7864320 | tf_op jit(solution)/shard_map/all_gather | solution.py:208
  85.6 230.4 %all-gather.11.cloned.1.call-start = ((), (), s32[]{:S(2)}) async-start(), calls=%async_computation.8 | async-start | bytes 7864320 | tf_op jit(solution)/shard_map/all_gather | solution.py:207
  104.5 58.5 %copy-start.2 = (bf16[2,512,768]{2,1,0:T(8,128)(2,1)S(1)}, bf16[2,512,768]{2,1,0:T(8,128)(2,1)}, u32[]{:S(2)}) copy-start(bf16[2,512,768]{2,1,0:T(8,128)(2,1)} %param.27) | copy-start | bytes 4718596
  104.6 318.7 %all-gather.15.cloned.1.call-start = ((), (), s32[]{:S(2)}) async-start(), calls=%async_computation.10 | async-start | bytes 1216512 | tf_op jit(solution)/shard_map/all_gather | solution.py:188
  105.3 332.7 %all-gather.17.cloned.1.call-start = ((), (), s32[]{:S(2)}) async-start(), calls=%async_computation.11 | async-start | bytes 4866048 | tf_op jit(solution)/shard_map/all_gather | solution.py:189
  106.0 397.3 %all-gather.19.cloned.1.call-start = ((), (), s32[]{:S(2)}) async-start(), calls=%async_computation.12 | async-start | bytes 4866048 | tf_op jit(solution)/shard_map/all_gather | solution.py:190
  106.8 462.5 %all-gather.21.cloned.1.call-start = ((), (), s32[]{:S(2)}) async-start(), calls=%async_computation.13 | async-start | bytes 4866048 | tf_op jit(solution)/shard_map/all_gather | solution.py:191
  107.6 944.6 %reduce-scatter.11.cloned.1.call-start = ((), (), s32[]{:S(2)}) async-start(), calls=%async_computation.14 | async-start | bytes 7864320 | tf_op jit(solution)/shard_map/reduce_scatter | solution.py:270
  942.5 223.3 %reduce-scatter.13.cloned.1.call-start = ((), (), s32[]{:S(2)}) async-start(), calls=%async_computation.15 | async-start | bytes 7864320 | tf_op jit(solution)/shard_map/reduce_scatter | solution.py:273
  943.2 328.0 %reduce-scatter.15.cloned.1.call-start = ((), (), s32[]{:S(2)}) async-start(), calls=%async_computation.16 | async-start | bytes 2433024 | tf_op jit(solution)/shard_map/reduce_scatter | solution.py:297
  948.7 464.6 %reduce-scatter.17.cloned.1.call-start = ((), (), s32[]{:S(2)}) async-start(), calls=%async_computation.17 | async-start | bytes 9732096 | tf_op jit(solution)/shard_map/reduce_scatter | solution.py:298
  958.7 595.5 %reduce-scatter.19.cloned.1.call-start = ((), (), s32[]{:S(2)}) async-start(), calls=%async_computation.18 | async-start | bytes 9732096 | tf_op jit(solution)/shard_map/reduce_scatter | solution.py:299
  970.6 725.7 %reduce-scatter.21.cloned.1.call-start = ((), (), s32[]{:S(2)}) async-start(), calls=%async_computation.19 | async-start | bytes 9732096 | tf_op jit(solution)/shard_map/reduce_scatter | solution.py:300
  982.7 71.3 %copy-start.4 = (f32[2,512,768]{1,2,0:T(8,128)S(1)}, f32[2,512,768]{1,2,0:T(8,128)}, u32[]{:S(2)}) copy-start(f32[2,512,768]{1,2,0:T(8,128)} %get-tuple-element.325) | copy-start | bytes 9437188
  982.7 71.3 %copy-start.30 = (f32[512,32]{0,1:T(8,128)S(1)}, f32[512,32]{0,1:T(8,128)}, u32[]{:S(2)}) copy-start(f32[512,32]{0,1:T(8,128)} %copy-done.29) | copy-start | bytes 196612
  982.7 71.3 %copy-start.37 = (f32[512,32]{0,1:T(8,128)S(1)}, f32[512,32]{0,1:T(8,128)}, u32[]{:S(2)}) copy-start(f32[512,32]{0,1:T(8,128)} %get-tuple-element.650) | copy-start | bytes 196612
  982.8 838.0 %reduce-scatter.23.cloned.1.call-start = ((), (), s32[]{:S(2)}) async-start(), calls=%async_computation.20 | async-start | bytes 7299072
  1225.1 652.2 %copy-start.42 = (f32[4,24]{1,0:T(4,128)}, f32[4,24]{1,0:T(4,128)S(1)}, u32[]{:S(2)}) copy-start(f32[4,24]{1,0:T(4,128)S(1)} %get-tuple-element.627) | copy-start | bytes 1156
  1286.8 540.0 %copy-start.15 = (bf16[1024,768]{0,1:T(8,128)(2,1)S(1)}, bf16[1024,768]{0,1:T(8,128)(2,1)}, u32[]{:S(2)}) copy-start(bf16[1024,768]{0,1:T(8,128)(2,1)} %copy.116) | copy-start | bytes 4718596
  1826.8 50.4 %copy-start.41 = (f32[4,24]{1,0:T(4,128)S(1)}, f32[4,24]{1,0:T(4,128)}, u32[]{:S(2)}) copy-start(f32[4,24]{1,0:T(4,128)} %param.33) | copy-start | bytes 1156
  1826.8 50.4 %copy-start.45 = (f32[4,24]{1,0:T(4,128)S(1)}, f32[4,24]{1,0:T(4,128)}, u32[]{:S(2)}) copy-start(f32[4,24]{1,0:T(4,128)} %param.39) | copy-start | bytes 1156
  1826.8 50.4 %copy-start.46 = (f32[4,24]{1,0:T(4,128)S(1)}, f32[4,24]{1,0:T(4,128)}, u32[]{:S(2)}) copy-start(f32[4,24]{1,0:T(4,128)} %param.45) | copy-start | bytes 1156
  1826.9 51.0 %copy-start.27 = (f32[24,2304]{1,0:T(8,128)S(1)}, f32[24,2304]{1,0:T(8,128)}, u32[]{:S(2)}) copy-start(f32[24,2304]{1,0:T(8,128)} %param.28) | copy-start | bytes 663556
  1826.9 51.0 %copy-start.28 = (f32[24,2304]{1,0:T(8,128)S(1)}, f32[24,2304]{1,0:T(8,128)}, u32[]{:S(2)}) copy-start(f32[24,2304]{1,0:T(8,128)} %reduce-scatter.23.cloned.1.call-done) | copy-start | bytes 663556
  1826.9 54.7 %copy-start.18 = (f32[24,3072]{1,0:T(8,128)S(1)}, f32[24,3072]{1,0:T(8,128)}, u32[]{:S(2)}) copy-start(f32[24,3072]{1,0:T(8,128)} %param.30) | copy-start | bytes 884740
  1826.9 54.7 %copy-start.23 = (f32[24,3072]{1,0:T(8,128)S(1)}, f32[24,3072]{1,0:T(8,128)}, u32[]{:S(2)}) copy-start(f32[24,3072]{1,0:T(8,128)} %reduce-scatter.17.cloned.1.call-done) | copy-start | bytes 884740
  1826.9 54.7 %copy-start.31 = (f32[24,3072]{1,0:T(8,128)S(1)}, f32[24,3072]{1,0:T(8,128)}, u32[]{:S(2)}) copy-start(f32[24,3072]{1,0:T(8,128)} %param.36) | copy-start | bytes 884740
  1836.4 47.2 %copy-start.33 = (f32[24,3072]{1,0:T(8,128)S(1)}, f32[24,3072]{1,0:T(8,128)}, u32[]{:S(2)}) copy-start(f32[24,3072]{1,0:T(8,128)} %param.43) | copy-start | bytes 884740
  1836.4 48.3 %copy-start.22 = (f32[96,768]{1,0:T(8,128)S(1)}, f32[96,768]{1,0:T(8,128)}, u32[]{:S(2)}) copy-start(f32[96,768]{1,0:T(8,128)} %param.32) | copy-start | bytes 884740
  1836.4 48.3 %copy-start.25 = (f32[96,768]{1,0:T(8,128)S(1)}, f32[96,768]{1,0:T(8,128)}, u32[]{:S(2)}) copy-start(f32[96,768]{1,0:T(8,128)} %reduce-scatter.21.cloned.1.call-done) | copy-start | bytes 884740
  1836.5 48.2 %copy-start.34 = (f32[96,768]{1,0:T(8,128)S(1)}, f32[96,768]{1,0:T(8,128)}, u32[]{:S(2)}) copy-start(f32[96,768]{1,0:T(8,128)} %param.38) | copy-start | bytes 884740
  (75 other events, 468.1 us)
Sparse Core Ops, SparseCore 0:
  11.5 62.7 all-gather.8
  85.7 114.3 all-gather.12
  202.3 113.6 all-gather.10
  319.3 52.2 all-gather.14
  375.0 62.9 all-gather.16
  441.3 62.0 all-gather.18
  506.8 62.4 all-gather.20
  942.6 109.5 reduce-scatter.10
  1054.5 111.2 reduce-scatter.12
  1171.5 99.6 reduce-scatter.14
  1278.7 134.5 reduce-scatter.16
  1419.6 134.5 reduce-scatter.18
  1561.7 134.5 reduce-scatter.20
  1702.5 118.2 reduce-scatter.22
where the time goes:
time: 1900 us; the launch traced here: 1890 us
  waiting for transfers between devices  1080 us (57%)
  matrix products  441 us (23%)
  other arithmetic  147 us (8%)
  blocking collectives  136 us (7%)
  local copies, waits for them, and re-layouts  68.4 us (4%)
  between operations  20.7 us (1%)
    reduce_scatter x1, waiting for transfers between devices, per_device(): lax.psum_scatter(g_down, ('seq', 'fsdp'), scatter_dimension=0, tiled=True)  140 us
    reduce_scatter x1, waiting for transfers between devices, per_device(): lax.psum_scatter(g_up, ('seq', 'fsdp'), scatter_dimension=0, tiled=True)  139 us
    reduce_scatter x1, waiting for transfers between devices, per_device(): lax.psum_scatter(g_gate, ('seq', 'fsdp'), scatter_dimension=0, tiled=True)  127 us
    dot_general x24, matrix products, one_head(): jnp.einsum('sqd,skd->sqk', query_head, key_head, preferred_element_type=j...  125 us
    unnamed x15, waiting for transfers between devices  124 us
    reduce_scatter x1, waiting for transfers between devices, per_device(): lax.psum_scatter(d_values.astype(jnp.bfloat16), 'seq', scatter_dimension=...  111 us
    all_gather x1, waiting for transfers between devices, per_device(): lax.all_gather(keys_local, 'seq', axis=1, tiled=True)  107 us
    convert_element_type x12, other arithmetic, one_head(): grad_scores = (attn_prob * (grad_prob - row_dots)).astype(jnp.bfloat16)  78.7 us
  transfers between devices with their start and end apart: 14, of which 13 were waited for; matrix products, arithmetic and copies ran while one was open for 13% of the time, Pallas kernels for 0%

commit v1 on v0

--- a/solution.py
+++ b/solution.py
@@ -1,8 +1,11 @@
+import functools
 import math
 
 import jax
 import jax.numpy as jnp
 from jax import lax
+from jax.experimental import pallas as pl
+from jax.experimental.pallas import tpu as pltpu
 from jax.sharding import PartitionSpec as P
 
 HEADS = 12
@@ -360,9 +363,928 @@
     )
 
 
+NT = (((1,), (1,)), ((), ()))
+NN = (((1,), (0,)), ((), ()))
+TN = (((0,), (0,)), ((), ()))
+FAR = 1e30
+CODE_BITS = 7
+MESH_ID = pl.DeviceIdType.MESH
+
+
+def dotf(left, right, dims=NN):
+    return lax.dot_general(left, right, dims, preferred_element_type=jnp.float32)
+
+
+def gather_kernel(seqs, bits, pieces, *refs):
+    gate, up, qkv, out, norm, down = refs[:6]
+    wide_all, down_all = refs[6:8]
+    wide_two, down_two, wide_chip, down_chip = refs[8:12]
+    core_send, core_recv, own_sem, line_send, line_recv, hop_send, hop_recv, swap_send, swap_recv = refs[12:]
+    z = lax.axis_index("seq")
+    f = lax.axis_index("fsdp")
+    core = lax.rem(f, 2)
+    chip = lax.div(f, 2)
+    sibling = {"fsdp": f + 1 - 2 * core}
+
+    def chip_at(mask):
+        at = chip
+        for b in range(bits):
+            if mask & (1 << b):
+                at = at + (1 - 2 * lax.rem(lax.div(chip, 1 << b), 2)) * (1 << b)
+        return at
+
+    def partner(b):
+        return {"fsdp": 2 * chip_at(1 << b) + core}
+
+    barrier = pltpu.get_barrier_semaphore()
+    pl.semaphore_signal(barrier, inc=1, device_id=sibling, device_id_type=MESH_ID)
+    for b in range(bits):
+        pl.semaphore_signal(barrier, inc=1, device_id=partner(b), device_id_type=MESH_ID)
+
+    for way in (1, seqs - 1):
+        pl.semaphore_signal(barrier, inc=1, device_id={"seq": lax.rem(z + way, seqs)}, device_id_type=MESH_ID)
+    rows = gate.shape[0]
+    at = 0
+    for part in (gate, up, qkv, out, norm):
+        wide_two[core, :, at : at + part.shape[1]] = part[...]
+        at += part.shape[1]
+    down_two[core] = down[...]
+    pl.semaphore_wait(barrier, 3 + bits)
+
+    first = [
+        pltpu.make_async_remote_copy(
+            two.at[core], two.at[core], core_send.at[i], core_recv.at[i], device_id=sibling, device_id_type=MESH_ID
+        )
+        for i, two in enumerate((wide_two, down_two))
+    ]
+    for copy in first:
+        copy.start()
+    for copy in first:
+        copy.wait()
+    wide_chip[...] = wide_two[...].reshape(wide_chip.shape).astype(jnp.bfloat16)
+    down_chip[...] = down_two[...].reshape(down_chip.shape).astype(jnp.bfloat16)
+    own = [
+        pltpu.make_async_copy(wide_chip, wide_all.at[z, chip], own_sem.at[0]),
+        pltpu.make_async_copy(down_chip, down_all.at[z, chip], own_sem.at[1]),
+    ]
+    for copy in own:
+        copy.start()
+
+    def columns(p):
+        source, offset, width, _ = pieces[p]
+        half = (down_all if source else wide_all).shape[-1] // 2
+        return pl.ds(pl.multiple_of(core * half + offset, 128), width)
+
+    def block(p, zz, mask):
+        return (down_all if pieces[p][0] else wide_all).at[zz, chip_at(mask), :, columns(p)]
+
+    def own_block(p):
+        return (down_chip if pieces[p][0] else wide_chip).at[:, columns(p)]
+
+    def line_copy(p, zz, way, mine):
+        return pltpu.make_async_remote_copy(
+            own_block(p) if mine else block(p, zz, 0),
+            block(p, zz, 0),
+            line_send.at[p, way, zz],
+            line_recv.at[p, zz],
+            device_id={"seq": z + (1 if way else -1)},
+            device_id_type=MESH_ID,
+        )
+
+    def hop_copy(p, zz, mask, b, mine):
+        return pltpu.make_async_remote_copy(
+            own_block(p) if mine else block(p, zz, mask),
+            block(p, zz, mask),
+            hop_send.at[p, zz, mask | (1 << b)],
+            hop_recv.at[p, zz, mask | (1 << b)],
+            device_id=partner(b),
+            device_id_type=MESH_ID,
+        )
+
+    def swap_copy(p, zz, mask):
+        return pltpu.make_async_remote_copy(
+            block(p, zz, mask),
+            block(p, zz, mask),
+            swap_send.at[p, zz, mask],
+            swap_recv.at[p, zz, mask],
+            device_id=sibling,
+            device_id_type=MESH_ID,
+        )
+
+    def level(p, mask):
+        return max([i for i, b in enumerate(pieces[p][3]) if mask & (1 << b)], default=-1)
+
+    def masks(p):
+        return sorted(range(1 << bits), key=lambda mask: (level(p, mask), mask))
+
+    def pass_on(p, zz, mask, mine=False):
+        for b in pieces[p][3][level(p, mask) + 1 :]:
+            hop_copy(p, zz, mask, b, mine).start()
+        if not mine:
+            swap_copy(p, zz, mask).start()
+
+    def arrived(p, zz, mask):
+        b = pieces[p][3][level(p, mask)]
+        hop_copy(p, zz, mask & ~(1 << b), b, False).wait_recv()
+
+    count = len(pieces)
+    for p in range(count):
+
+        @pl.when(z > 0)
+        def _():
+            line_copy(p, z, 0, True).start()
+
+        @pl.when(z < seqs - 1)
+        def _():
+            line_copy(p, z, 1, True).start()
+
+        pass_on(p, z, 0, True)
+
+    def hops(zz):
+        for level_at in range(bits):
+            for p in range(count):
+                for mask in masks(p):
+                    if level(p, mask) == level_at:
+                        arrived(p, zz, mask)
+                        pass_on(p, zz, mask)
+
+    for distance in range(1, seqs):
+        for way in (1, 0):
+            zz = z - distance if way else z + distance
+
+            @pl.when((zz >= 0) & (zz < seqs))
+            def _():
+                for p in range(count):
+                    line_copy(p, zz, way, False).wait_recv()
+
+                    @pl.when((z < seqs - 1) if way else (z > 0))
+                    def _():
+                        line_copy(p, zz, way, False).start()
+
+                    pass_on(p, zz, 0)
+
+        for way in (1, 0):
+            zz = z - distance + 1 if way else z + distance - 1
+            if distance > 1 or way:
+
+                @pl.when((zz >= 0) & (zz < seqs))
+                def _():
+                    hops(zz)
+
+    for way in (1, 0):
+        zz = z - seqs + 1 if way else z + seqs - 1
+
+        @pl.when((zz >= 0) & (zz < seqs))
+        def _():
+            hops(zz)
+
+    def finish(zz):
+        for p in range(count):
+
+            @pl.when((zz <= z) & (z < seqs - 1))
+            def _():
+                line_copy(p, zz, 1, False).wait_send()
+
+            @pl.when((zz >= z) & (z > 0))
+            def _():
+                line_copy(p, zz, 0, False).wait_send()
+
+            for mask in masks(p):
+                for b in pieces[p][3][level(p, mask) + 1 :]:
+                    hop_copy(p, zz, mask, b, False).wait_send()
+                if mask:
+                    swap_copy(p, zz, mask).wait()
+
+            @pl.when(zz != z)
+            def _():
+                swap_copy(p, zz, 0).wait()
+
+    lax.fori_loop(0, seqs, lambda zz, _: (finish(zz), 0)[1], 0)
+    for copy in own:
+        copy.wait()
+
+
+def gather_all(mesh_shape, gate, up, qkv, out, norm, down):
+    seqs, chips = mesh_shape["seq"], mesh_shape["fsdp"] // 2
+    bits = chips.bit_length() - 1
+    rows, rows_down = gate.shape[0], down.shape[0]
+    wide = sum(part.shape[1] for part in (gate, up, qkv, out, norm))
+    upward, downward = tuple(range(bits)), tuple(reversed(range(bits)))
+    down_load = down.shape[1] // 2 * rows_down // rows
+    cut = max(0, (wide // 2 + down_load) // 2 - down_load) // 128 * 128 + 128
+    pieces = ((0, 0, cut, upward), (1, 0, down.shape[1] // 2, upward), (0, cut, wide // 2 - cut, downward))
+    count = len(pieces)
+    dma = pltpu.SemaphoreType.DMA
+    any_space = pl.BlockSpec(memory_space=pl.ANY)
+    vmem = pl.BlockSpec(memory_space=pltpu.VMEM)
+    return pl.pallas_call(
+        functools.partial(gather_kernel, seqs, bits, pieces),
+        out_shape=[
+            jax.ShapeDtypeStruct((seqs, chips, 2 * rows, wide), jnp.bfloat16),
+            jax.ShapeDtypeStruct((seqs, chips, 2 * rows_down, down.shape[1]), jnp.bfloat16),
+        ],
+        in_specs=[vmem] * 6,
+        out_specs=[any_space] * 2,
+        scratch_shapes=[
+            pltpu.VMEM((2, rows, wide), jnp.float32),
+            pltpu.VMEM((2, rows_down, down.shape[1]), jnp.float32),
+            pltpu.VMEM((2 * rows, wide), jnp.bfloat16),
+            pltpu.VMEM((2 * rows_down, down.shape[1]), jnp.bfloat16),
+            dma((2,)),
+            dma((2,)),
+            dma((2,)),
+            dma((count, 2, seqs)),
+            dma((count, seqs)),
+            dma((count, seqs, chips)),
+            dma((count, seqs, chips)),
+            dma((count, seqs, chips)),
+            dma((count, seqs, chips)),
+        ],
+        compiler_params=pltpu.CompilerParams(collective_id=0, has_side_effects=True, vmem_limit_bytes=48 << 20),
+        name="gather_parameters",
+    )(gate, up, qkv, out, norm, down)
+
+
+def turn(field, cosine, sine):
+    width = field.shape[-1]
+    reps = width // cosine.shape[-1]
+    cosine = jnp.concatenate([cosine] * reps, -1)
+    sine = jnp.concatenate([sine] * reps, -1)
+    lane = lax.broadcasted_iota(jnp.int32, field.shape, 1)
+    half = HEAD_DIM // 2
+    other = jnp.where(
+        lax.rem(lane, HEAD_DIM) < half, pltpu.roll(field, width - half, 1), pltpu.roll(field, half, 1)
+    )
+    return field * cosine + other * sine
+
+
+def project_kernel(x_ref, wq_ref, wk_ref, wv_ref, cos_ref, sin_ref, code_ref, q_ref, kv_ref):
+    x, cosine, sine = x_ref[...], cos_ref[...], sin_ref[...]
+    width = x.shape[-1]
+    query = turn(dotf(x, wq_ref[...]), cosine, sine).astype(jnp.bfloat16)
+    q_ref[...] = query * jnp.bfloat16(1.0 / math.sqrt(HEAD_DIM))
+    kv_ref[:, :width] = turn(dotf(x, wk_ref[...]), cosine, sine).astype(jnp.bfloat16)
+    kv_ref[:, width : 2 * width] = dotf(x, wv_ref[...]).astype(jnp.bfloat16)
+    kv_ref[:, 2 * width :] = code_ref[...]
+
+
+def project(x, wide, first, cosine, sine, code, block=256):
+    rows, width = x.shape
+    weight = lambda n: pl.BlockSpec((width, width), lambda i, n=n: (0, first + n))
+    row = lambda cols: pl.BlockSpec((block, cols), lambda i: (i, 0))
+    return pl.pallas_call(
+        project_kernel,
+        grid=(rows // block,),
+        in_specs=[row(width), weight(0), weight(1), weight(2), row(128), row(128), row(128)],
+        out_specs=[row(width), row(2 * width + 128)],
+        out_shape=[
+            jax.ShapeDtypeStruct((rows, width), jnp.bfloat16),
+            jax.ShapeDtypeStruct((rows, 2 * width + 128), jnp.bfloat16),
+        ],
+        compiler_params=pltpu.CompilerParams(vmem_limit_bytes=48 << 20),
+        name="project",
+    )(x, wide, wide, wide, cosine, sine, code)
+
+
+def attend_kernel(unit, chunk, q_ref, qc_ref, k0, kc0, v0, k1, kc1, v1, p_ref, o_ref, inv_ref, ka, vt, st_ref):
+    part = k0.shape[0]
+    keys = 2 * part
+    rows = q_ref.shape[0]
+    low_k = lax.broadcasted_iota(jnp.int32, (part, 128), 1) < HEAD_DIM
+    for i, (k_ref, kc_ref, v_ref) in enumerate(((k0, kc0, v0), (k1, kc1, v1))):
+        k, kc, v = k_ref[...], kc_ref[...], v_ref[...]
+        one = jnp.ones_like(v)
+        here = slice(i * part, (i + 1) * part)
+        ka[0, here] = jnp.where(low_k, k, kc)
+        ka[1, here] = jnp.where(low_k, kc, k)
+        vt[0, :, here] = jnp.where(low_k, v, one).T
+        vt[1, :, here] = jnp.where(low_k, one, v).T
+    low_q = lax.broadcasted_iota(jnp.int32, (unit, 128), 1) < HEAD_DIM
+    units = [(h, b) for b in range(rows // unit) for h in range(2)]
+    results, before = {}, None
+    for u, now in enumerate([*units, None]):
+        if now is not None:
+            h, b = now
+            q, qc = q_ref[b * unit : (b + 1) * unit], qc_ref[b * unit : (b + 1) * unit]
+            qa = jnp.where(low_q, q, qc) if h == 0 else jnp.where(low_q, qc, q)
+        top = total = None
+        for c in range(keys // chunk):
+            here = slice(c * chunk, (c + 1) * chunk)
+            if now is not None:
+                s = dotf(ka[h, here], qa, NT)
+                st_ref[u % 2, here] = s
+                most = jnp.max(s.reshape(chunk // 8, 8, unit), axis=0)
+                top = most if top is None else jnp.maximum(top, most)
+            if before is not None:
+                hb, bb, row_max = before
+                p = jnp.exp(st_ref[(u - 1) % 2, here] - row_max).astype(jnp.bfloat16)
+                p_ref[hb, here, bb * unit : (bb + 1) * unit] = p
+                d = dotf(vt[hb, :, here], p)
+                total = d if total is None else total + d
+        if before is not None:
+            results[before[:2]] = total.T
+        before = None if now is None else (h, b, jnp.max(top, axis=0, keepdims=True))
+    for b in range(rows // unit):
+        r0, r1 = results[(0, b)], results[(1, b)]
+        inv = 1.0 / pltpu.roll(jnp.where(low_q, r1, r0), HEAD_DIM, 1)
+        inv_ref[b * unit : (b + 1) * unit] = inv
+        o_ref[b * unit : (b + 1) * unit] = (jnp.where(low_q, r0, r1) * inv).astype(jnp.bfloat16)
+
+
+def attend_pallas(q, qc, own, sib, unit=512, chunk=512):
+    rows, width = q.shape
+    pairs = width // 128
+    part = own.shape[0]
+    row = pl.BlockSpec((rows, 128), lambda j: (0, j))
+    kv = [
+        pl.BlockSpec((part, 128), lambda j: (0, j)),
+        pl.BlockSpec((part, 128), lambda j: (0, 2 * pairs)),
+        pl.BlockSpec((part, 128), lambda j: (0, pairs + j)),
+    ]
+    return pl.pallas_call(
+        functools.partial(attend_kernel, unit, chunk),
+        grid=(pairs,),
+        in_specs=[row, pl.BlockSpec((rows, 128), lambda j: (0, 0)), *kv, *kv],
+        out_specs=[pl.BlockSpec((2, 2 * part, rows), lambda j: (j, 0, 0)), row, row],
+        out_shape=[
+            jax.ShapeDtypeStruct((2 * pairs, 2 * part, rows), jnp.bfloat16),
+            jax.ShapeDtypeStruct((rows, width), jnp.bfloat16),
+            jax.ShapeDtypeStruct((rows, width), jnp.float32),
+        ],
+        scratch_shapes=[
+            pltpu.VMEM((2, 2 * part, 128), jnp.bfloat16),
+            pltpu.VMEM((2, 128, 2 * part), jnp.bfloat16),
+            pltpu.VMEM((2, 2 * part, unit), jnp.float32),
+        ],
+        compiler_params=pltpu.CompilerParams(vmem_limit_bytes=56 << 20),
+        name="attend",
+    )(q, qc, own, own, own, sib, sib, sib)
+
+
+def attend_back_kernel(q_ref, k0, v0, k1, v1, p_ref, o_ref, inv_ref, do_ref, dq_ref, own_ref, sib_ref, kt, va, dk, dv):
+    part = k0.shape[0]
+    unit = q_ref.shape[0]
+    lane_k = lax.broadcasted_iota(jnp.int32, (part, 128), 1)
+
+    @pl.when(pl.program_id(1) == 0)
+    def _():
+        for i, (k_ref, v_ref) in enumerate(((k0, v0), (k1, v1))):
+            k, v = k_ref[...], v_ref[...]
+            zero, one = jnp.zeros_like(v), jnp.ones_like(v)
+            here = slice(i * part, (i + 1) * part)
+            kt[0, :, here] = jnp.where(lane_k < HEAD_DIM, k, zero).T
+            kt[1, :, here] = jnp.where(lane_k < HEAD_DIM, zero, k).T
+            va[0, here] = jnp.where(lane_k < HEAD_DIM, v, jnp.where(lane_k < HEAD_DIM + 3, one, zero))
+            va[1, here] = jnp.where(lane_k >= HEAD_DIM, v, jnp.where(lane_k < 3, one, zero))
+        dk[...] = jnp.zeros_like(dk)
+        dv[...] = jnp.zeros_like(dv)
+
+    lane = lax.broadcasted_iota(jnp.int32, (unit, 128), 1)
+    q = q_ref[...]
+    dof = do_ref[...].astype(jnp.float32) * inv_ref[...]
+    prod = dof * o_ref[...].astype(jnp.float32)
+    dob = dof.astype(jnp.bfloat16)
+    zero = jnp.zeros_like(dob)
+    turned = None
+    for h in range(2):
+        mine = lane < HEAD_DIM if h == 0 else lane >= HEAD_DIM
+        base = HEAD_DIM if h == 0 else 0
+        d = -jnp.sum(jnp.where(mine, prod, 0.0), axis=1, keepdims=True)
+        d1 = d.astype(jnp.bfloat16).astype(jnp.float32)
+        d2 = (d - d1).astype(jnp.bfloat16).astype(jnp.float32)
+        d3 = d - d1 - d2
+        extra = jnp.where(
+            lane == base, d1, jnp.where(lane == base + 1, d2, jnp.where(lane == base + 2, d3, 0.0))
+        ).astype(jnp.bfloat16)
+        p = p_ref[h]
+        ds = (p.astype(jnp.float32) * dotf(va[h], jnp.where(mine, dob, extra), NT)).astype(jnp.bfloat16)
+        dv[...] += dotf(p, jnp.where(mine, dob, zero))
+        dk[...] += dotf(ds, jnp.where(mine, q, zero))
+        new = dotf(kt[h], ds)
+        turned = new if turned is None else turned + new
+    dq_ref[...] = turned.T * (1.0 / math.sqrt(HEAD_DIM))
+
+    @pl.when(pl.program_id(1) == pl.num_programs(1) - 1)
+    def _():
+        for i, total in enumerate((dk, dv)):
+            own_ref[i] = total[:part]
+            sib_ref[i] = total[part:].astype(jnp.bfloat16)
+
+
+def attend_back_pallas(q, own, sib, p, o, inv, do, first, pairs, unit=512):
+    rows, width = q.shape
+    all_pairs = width // 128
+    part = own.shape[0]
+    row = pl.BlockSpec((unit, 128), lambda j, i: (i, j + first))
+    kv = [
+        pl.BlockSpec((part, 128), lambda j, i: (0, j + first)),
+        pl.BlockSpec((part, 128), lambda j, i: (0, j + first + all_pairs)),
+    ]
+    return pl.pallas_call(
+        attend_back_kernel,
+        grid=(pairs, rows // unit),
+        in_specs=[row, *kv, *kv, pl.BlockSpec((2, 2 * part, unit), lambda j, i: (j + first, 0, i)), row, row, row],
+        out_specs=[
+            pl.BlockSpec((unit, 128), lambda j, i: (i, j)),
+            pl.BlockSpec((2, part, 128), lambda j, i: (0, 0, j)),
+            pl.BlockSpec((2, part, 128), lambda j, i: (0, 0, j)),
+        ],
+        out_shape=[
+            jax.ShapeDtypeStruct((rows, 128 * pairs), jnp.float32),
+            jax.ShapeDtypeStruct((2, part, 128 * pairs), jnp.float32),
+            jax.ShapeDtypeStruct((2, part, 128 * pairs), jnp.bfloat16),
+        ],
+        scratch_shapes=[
+            pltpu.VMEM((2, 128, 2 * part), jnp.bfloat16),
+            pltpu.VMEM((2, 2 * part, 128), jnp.bfloat16),
+            pltpu.VMEM((2 * part, 128), jnp.float32),
+            pltpu.VMEM((2 * part, 128), jnp.float32),
+        ],
+        compiler_params=pltpu.CompilerParams(vmem_limit_bytes=56 << 20),
+        name="attend_back",
+    )(q, own, own, sib, sib, p, o, inv, do)
+
+
+def mean_row(field):
+    return jnp.mean(field, -1, keepdims=True)
+
+
+def middle_kernel(
+    x_ref, att_ref, cot_ref, wo_ref, wg_ref, wu_ref, wd_ref, norms_ref,
+    out_ref, dr_ref, branch_ref, datt_ref, hid_ref, mixed_ref, dgate_ref, dup_ref, dff_ref, sums_ref,
+    silu_s, slope_s,
+):
+    gain_one, shift_one, gain_two, shift_two = (norms_ref[n : n + 1] for n in range(4))
+    resid_one = x_ref[...].astype(jnp.float32) + dotf(att_ref[...], wo_ref[...])
+    hidden, normed_one, inv_one = normalize(resid_one, gain_one, shift_one)
+    hidden_low = hidden.astype(jnp.bfloat16)
+    hid_ref[...] = hidden_low
+    hidden_units = wd_ref.shape[0]
+    step = 768
+    cuts = [slice(n, n + step) for n in range(0, hidden_units, step)]
+    resid_two = hidden
+    for cut in cuts:
+        gate = dotf(hidden_low, wg_ref[:, cut])
+        up = dotf(hidden_low, wu_ref[:, cut])
+        sig = jax.nn.sigmoid(gate)
+        silu = gate * sig
+        mixed = (silu * up).astype(jnp.bfloat16)
+        silu_s[:, cut] = silu
+        slope_s[:, cut] = up * sig * (1.0 + gate * (1.0 - sig))
+        mixed_ref[:, cut] = mixed
+        resid_two = resid_two + dotf(mixed, wd_ref[cut, :])
+    result, normed_two, inv_two = normalize(resid_two, gain_two, shift_two)
+    out_ref[...] = result.astype(jnp.bfloat16)
+    dy = cot_ref[...].astype(jnp.float32)
+    d_two = normalize_back(dy, normed_two, inv_two, gain_two)
+    d_ff = d_two.astype(jnp.bfloat16)
+    dff_ref[...] = d_ff
+    d_hidden = d_two
+    for cut in cuts:
+        d_mixed = dotf(d_ff, wd_ref[cut, :], NT)
+        d_up = (d_mixed * silu_s[:, cut]).astype(jnp.bfloat16)
+        d_gate = (d_mixed * slope_s[:, cut]).astype(jnp.bfloat16)
+        dup_ref[:, cut] = d_up
+        dgate_ref[:, cut] = d_gate
+        d_hidden = d_hidden + dotf(d_gate, wg_ref[:, cut], NT) + dotf(d_up, wu_ref[:, cut], NT)
+    d_one = normalize_back(d_hidden, normed_one, inv_one, gain_one)
+    dr_ref[...] = d_one
+    branch = d_one.astype(jnp.bfloat16)
+    branch_ref[...] = branch
+    datt_ref[...] = dotf(branch, wo_ref[...], NT).astype(jnp.bfloat16)
+
+    @pl.when(pl.program_id(0) == 0)
+    def _():
+        sums_ref[...] = jnp.zeros_like(sums_ref)
+
+    for n, term in enumerate((d_hidden * normed_one, d_hidden, dy * normed_two, dy)):
+        sums_ref[n : n + 1] += jnp.sum(term, 0, keepdims=True)
+
+
+def middle(x, attended, cotangent, wide, down, norms, block=256):
+    rows, width = x.shape
+    units = down.shape[0]
+    row = lambda cols: pl.BlockSpec((block, cols), lambda i: (i, 0))
+    once = pl.Buffered(1)
+    weight = lambda shape, n: pl.BlockSpec(shape, lambda i: (0, n), pipeline_mode=once)
+    like = lambda cols, dtype: jax.ShapeDtypeStruct((rows, cols), dtype)
+    low = jnp.bfloat16
+    first_out = (2 * units + 3 * width) // width
+    return pl.pallas_call(
+        middle_kernel,
+        grid=(rows // block,),
+        in_specs=[
+            row(width), row(width), row(width),
+            weight((width, width), first_out), weight((width, units), 0), weight((width, units), 1),
+            weight((units, width), 0), weight((8, width), 0),
+        ],
+        out_specs=[
+            row(width), row(width), row(width), row(width), row(width), row(units), row(units), row(units), row(width),
+            pl.BlockSpec((8, width), lambda i: (0, 0)),
+        ],
+        out_shape=[
+            like(width, low), like(width, jnp.float32), like(width, low), like(width, low), like(width, low),
+            like(units, low), like(units, low), like(units, low), like(width, low),
+            jax.ShapeDtypeStruct((8, width), jnp.float32),
+        ],
+        scratch_shapes=[pltpu.VMEM((block, units), jnp.float32), pltpu.VMEM((block, units), jnp.float32)],
+        compiler_params=pltpu.CompilerParams(vmem_limit_bytes=60 << 20),
+        name="middle",
+    )(x, attended, cotangent, wide, wide, wide, down, norms)
+
+
+def grad_wide_kernel(tiles, core_ref, left_ref, right_ref, keep_ref, send_ref):
+    value = dotf(left_ref[...], right_ref[...], TN).astype(jnp.bfloat16)
+
+    @pl.when(pl.program_id(0) < tiles)
+    def _():
+        send_ref[...] = value
+
+    @pl.when(pl.program_id(0) >= tiles)
+    def _():
+        keep_ref[...] = value
+
+
+def grad_wide(core, left, right, tile=512):
+    rows, width = left.shape
+    half = right.shape[1] // 2
+    tiles = half // tile
+    like = jax.ShapeDtypeStruct((width, half), jnp.bfloat16)
+    return pl.pallas_call(
+        functools.partial(grad_wide_kernel, tiles),
+        grid_spec=pltpu.PrefetchScalarGridSpec(
+            num_scalar_prefetch=1,
+            grid=(2 * tiles,),
+            in_specs=[
+                pl.BlockSpec((rows, width), lambda i, c: (0, 0)),
+                pl.BlockSpec(
+                    (rows, tile), lambda i, c: (0, lax.rem(c[0] + 1 + lax.div(i, tiles), 2) * tiles + lax.rem(i, tiles))
+                ),
+            ],
+            out_specs=[
+                pl.BlockSpec((width, tile), lambda i, c: (0, jnp.maximum(i - tiles, 0))),
+                pl.BlockSpec((width, tile), lambda i, c: (0, jnp.minimum(i, tiles - 1))),
+            ],
+        ),
+        out_shape=[like, like],
+        compiler_params=pltpu.CompilerParams(vmem_limit_bytes=48 << 20),
+        name="grad_wide",
+    )(core, left, right)
+
+
+def halves(value, core, keep_ref, send_ref):
+    half = value.shape[1] // 2
+    low, high = value[:, :half].astype(jnp.bfloat16), value[:, half:].astype(jnp.bfloat16)
+    keep_ref[...] = jnp.where(core == 0, low, high)
+    send_ref[...] = jnp.where(core == 0, high, low)
+
+
+def grad_tall_kernel(core_ref, left_ref, right_ref, keep_ref, send_ref):
+    halves(dotf(left_ref[...], right_ref[...], TN), core_ref[0], keep_ref, send_ref)
+
+
+def grad_tall(core, left, right, tile=512):
+    rows, height = left.shape
+    width = right.shape[1]
+    out = pl.BlockSpec((tile, width // 2), lambda i, c: (i, 0))
+    like = jax.ShapeDtypeStruct((height, width // 2), jnp.bfloat16)
+    return pl.pallas_call(
+        grad_tall_kernel,
+        grid_spec=pltpu.PrefetchScalarGridSpec(
+            num_scalar_prefetch=1,
+            grid=(height // tile,),
+            in_specs=[
+                pl.BlockSpec((rows, tile), lambda i, c: (0, i)),
+                pl.BlockSpec((rows, width), lambda i, c: (0, 0)),
+            ],
+            out_specs=[out, out],
+        ),
+        out_shape=[like, like],
+        compiler_params=pltpu.CompilerParams(vmem_limit_bytes=48 << 20),
+        name="grad_tall",
+    )(core, left, right)
+
+
+def grad_out_kernel(core_ref, left_ref, right_ref, sums_ref, keep_ref, send_ref):
+    value = dotf(left_ref[...], right_ref[...], TN)
+    pad = jnp.zeros((NORM_COLS - sums_ref.shape[0], sums_ref.shape[1]), jnp.float32)
+    norms = jnp.concatenate([sums_ref[...], pad], 0).T
+    halves(jnp.concatenate([value, norms], 1), core_ref[0], keep_ref, send_ref)
+
+
+def grad_out(core, left, right, sums):
+    width = left.shape[1]
+    full = lambda array: pl.BlockSpec(array.shape, lambda i, c: (0, 0))
+    half = (width + NORM_COLS) // 2
+    out = pl.BlockSpec((width, half), lambda i, c: (0, 0))
+    like = jax.ShapeDtypeStruct((width, half), jnp.bfloat16)
+    return pl.pallas_call(
+        grad_out_kernel,
+        grid_spec=pltpu.PrefetchScalarGridSpec(
+            num_scalar_prefetch=1, grid=(1,), in_specs=[full(left), full(right), full(sums)], out_specs=[out, out]
+        ),
+        out_shape=[like, like],
+        compiler_params=pltpu.CompilerParams(vmem_limit_bytes=48 << 20),
+        name="grad_out",
+    )(core, left, right, sums)
+
+
+def grad_qkv_kernel(calls, core_ref, x_ref, cos_ref, sin_ref, *refs):
+    parts = [refs[3 * n : 3 * n + 3] for n in range(calls)]
+    dproj_ref, keep_ref, send_ref, total = refs[3 * calls :]
+    join = lambda pieces: jnp.concatenate(pieces, -1)
+    d_query = join([dq[...] for dq, _, _ in parts])
+    d_keys = join([own[0] + got[0].astype(jnp.float32) for _, own, got in parts])
+    d_values = join([own[1] + got[1].astype(jnp.float32) for _, own, got in parts])
+    cosine, sine = cos_ref[...], -sin_ref[...]
+    low = jnp.bfloat16
+    d_projected = join(
+        [turn(d_query, cosine, sine).astype(low), turn(d_keys, cosine, sine).astype(low), d_values.astype(low)]
+    )
+    dproj_ref[...] = d_projected
+    new = dotf(x_ref[...], d_projected, TN)
+
+    @pl.when(pl.program_id(0) == 0)
+    def _():
+        total[...] = new
+
+    @pl.when(pl.program_id(0) > 0)
+    def _():
+        total[...] += new
+
+    @pl.when(pl.program_id(0) == pl.num_programs(0) - 1)
+    def _():
+        halves(total[...], core_ref[0], keep_ref, send_ref)
+
+
+def grad_qkv(core, x, cosine, sine, parts, block=256):
+    rows, width = x.shape
+    row = lambda cols: pl.BlockSpec((block, cols), lambda i, c: (i, 0))
+    specs, arrays = [], []
+    for d_query, own, got in parts:
+        cols = d_query.shape[1]
+        pair = pl.BlockSpec((2, block, cols), lambda i, c: (0, i, 0))
+        specs += [row(cols), pair, pair]
+        arrays += [d_query, own, got]
+    half = pl.BlockSpec((width, 3 * width // 2), lambda i, c: (0, 0))
+    like = jax.ShapeDtypeStruct((width, 3 * width // 2), jnp.bfloat16)
+    return pl.pallas_call(
+        functools.partial(grad_qkv_kernel, len(parts)),
+        grid_spec=pltpu.PrefetchScalarGridSpec(
+            num_scalar_prefetch=1,
+            grid=(rows // block,),
+            in_specs=[row(width), row(128), row(128), *specs],
+            out_specs=[row(3 * width), half, half],
+            scratch_shapes=[pltpu.VMEM((width, 3 * width), jnp.float32)],
+        ),
+        out_shape=[jax.ShapeDtypeStruct((rows, 3 * width), jnp.bfloat16), like, like],
+        compiler_params=pltpu.CompilerParams(vmem_limit_bytes=56 << 20),
+        name="grad_qkv",
+    )(core, x, cosine, sine, *arrays)
+
+
+def grad_input_kernel(dproj_ref, wq_ref, wk_ref, wv_ref, dr_ref, dx_ref):
+    width = dr_ref.shape[1]
+    total = dr_ref[...]
+    for n, w_ref in enumerate((wq_ref, wk_ref, wv_ref)):
+        total = total + dotf(dproj_ref[:, n * width : (n + 1) * width], w_ref[...], NT)
+    dx_ref[...] = total.astype(jnp.bfloat16)
+
+
+def grad_input(d_projected, wide, first, d_resid, block=256):
+    rows, width = d_resid.shape
+    weight = lambda n: pl.BlockSpec((width, width), lambda i, n=n: (0, first + n))
+    row = lambda cols: pl.BlockSpec((block, cols), lambda i: (i, 0))
+    return pl.pallas_call(
+        grad_input_kernel,
+        grid=(rows // block,),
+        in_specs=[row(3 * width), weight(0), weight(1), weight(2), row(width)],
+        out_specs=row(width),
+        out_shape=jax.ShapeDtypeStruct((rows, width), jnp.bfloat16),
+        compiler_params=pltpu.CompilerParams(vmem_limit_bytes=48 << 20),
+        name="grad_input",
+    )(d_projected, wide, wide, wide, d_resid)
+
+
+NORM_COLS = 256
+AXES = ("seq", "fsdp")
+
+
+def pairs_of(shape, move):
+    seqs, line = shape["seq"], shape["fsdp"]
+    found = []
+    for z in range(seqs):
+        for f in range(line):
+            to_z, to_chip, to_core = move(z, f // 2, f % 2)
+            found.append((z * line + f, to_z * line + 2 * to_chip + to_core))
+    return found
+
+
+def send(array, pairs):
+    return lax.ppermute(array, AXES, pairs)
+
+
+def pick(array, index, axis):
+    return lax.dynamic_index_in_dim(array, index, axis, keepdims=False)
+
+
+def add_up(arrays):
+    return sum(array.astype(jnp.float32) for array in arrays)
+
+
+def reduce_scatter(shape, keep, away, downward):
+    seqs, chips = shape["seq"], shape["fsdp"] // 2
+    bits = chips.bit_length() - 1
+    z = lax.axis_index("seq")
+    f = lax.axis_index("fsdp")
+    core, chip = f % 2, f // 2
+    half = keep.shape[1]
+    rows = keep.shape[0] // (seqs * chips)
+    got = send(away, pairs_of(shape, lambda z, p, c: (z, p, 1 - c)))
+    whole = [array.reshape((seqs,) + (2,) * bits + (rows, half)) for array in (keep, got)]
+    left = list(reversed(range(bits)))
+    for b in left if downward else range(bits):
+        axis = 1 + sorted(left, reverse=True).index(b)
+        left = [n for n in left if n != b]
+        mine = (chip >> b) & 1
+        away = add_up([pick(array, 1 - mine, axis) for array in whole]).astype(jnp.bfloat16)
+        got = send(away, pairs_of(shape, lambda z, p, c: (z, p ^ (1 << b), c)))
+        whole = [pick(array, mine, axis) for array in whole] + [got]
+    terms = [add_up([pick(array, z, 0) for array in whole])]
+    for k in range(1, seqs):
+        away = add_up([pick(array, (z + k) % seqs, 0) for array in whole]).astype(jnp.bfloat16)
+        terms.append(send(away, pairs_of(shape, lambda z, p, c: ((z + k) % seqs, p, c))))
+    total = add_up(terms)
+    mine, away = jnp.where(core == 0, 0, rows // 2), jnp.where(core == 0, rows // 2, 0)
+    got = send(
+        lax.dynamic_slice_in_dim(total, away, rows // 2, 0), pairs_of(shape, lambda z, p, c: (z, p, 1 - c))
+    )
+    mine = lax.dynamic_slice_in_dim(total, mine, rows // 2, 0)
+    return jnp.where(core == 0, jnp.concatenate([mine, got], 1), jnp.concatenate([got, mine], 1))
+
+
+def sum_all(shape, value):
+    seqs, chips = shape["seq"], shape["fsdp"] // 2
+    moves = [lambda z, p, c: (z, p, 1 - c)]
+    b = 1
+    while b < chips:
+        moves.append(lambda z, p, c, b=b: (z, p ^ b, c))
+        b *= 2
+    b = 1
+    while b < seqs:
+        moves.append(lambda z, p, c, b=b: (z ^ b, p, c))
+        b *= 2
+    for move in moves:
+        value = value + send(value, pairs_of(shape, move))
+    return value
+
+
+def seg_codes(segments):
+    lane = jnp.arange(128) % HEAD_DIM
+    low, high = lane < CODE_BITS, lane < 2 * CODE_BITS
+    bit = (segments[:, None] >> jnp.where(low, lane, jnp.where(high, lane - CODE_BITS, 0))[None, :]) & 1
+    query = jnp.where(low, bit, jnp.where(high, 1 - bit, 0))
+    keys = jnp.where(low, 1 - bit, jnp.where(high, bit, 0)) * -FAR
+    return query.astype(jnp.bfloat16), keys.astype(jnp.bfloat16)
+
+
+def two_to_a_sequence(
+    shape,
+    tokens, segment_ids, cotangent,
+    w_qkv, w_out, w_gate, w_up, w_down, norm_params,
+    first_qkv, first_out, first_gate, first_up, first_down, first_norms,
+    second_qkv, second_out, second_gate, second_up, second_down, second_norms,
+):
+    seqs = shape["seq"]
+    seq_count, local_len, width = tokens.shape
+    rows = seq_count * local_len
+    group = seqs // seq_count
+    units = w_gate.shape[1]
+    z = lax.axis_index("seq")
+    f = lax.axis_index("fsdp")
+    core = f % 2
+
+    def there(turn_at):
+        def move(z, p, c):
+            at = (c * seq_count + (z + turn_at) % seq_count) * group + z // seq_count
+            return (at // 2, p, at % 2)
+
+        return pairs_of(shape, move)
+
+    out_pairs = [there(t) for t in range(seq_count)]
+    back_pairs = [[(to, at) for at, to in pairs] for pairs in out_pairs]
+
+    def to_sequences(array):
+        return jnp.concatenate(
+            [send(pick(array, (z + t) % seq_count, 0), out_pairs[t]) for t in range(seq_count)], 0
+        )
+
+    def from_sequences(array):
+        got = jnp.stack(
+            [send(array[t * local_len : (t + 1) * local_len], back_pairs[t]) for t in range(seq_count)]
+        )
+        return jnp.roll(got, z % seq_count, 0)
+
+    x = to_sequences(tokens)
+    segments = to_sequences(segment_ids)
+    dy = to_sequences(cotangent)
+    q_code, k_code = seg_codes(segments)
+    at = z * 2 + core
+    within = jnp.concatenate(
+        [((at // group - t) % seq_count) * local_len + jnp.arange(local_len) for t in range(seq_count)]
+    )
+    positions = ((at % group) * rows + within).astype(jnp.float32)
+    half_dim = HEAD_DIM // 2
+    inverse = jnp.exp(jnp.arange(half_dim, dtype=jnp.float32) * (-2.0 * math.log(ROPE_BASE) / HEAD_DIM))
+    angles = positions[:, None] * inverse[None, :]
+    cosine, sine = jnp.cos(angles), jnp.sin(angles)
+    cosine = jnp.concatenate([cosine] * 4, 1)
+    sine = jnp.concatenate([-sine, sine, -sine, sine], 1)
+
+    norm_rows = jnp.pad(norm_params.T, ((0, 0), (0, NORM_COLS - norm_params.shape[0])))
+    wide, down = gather_all(shape, w_gate, w_up, w_qkv, w_out, norm_rows, w_down)
+    wide = wide.reshape(width, wide.shape[-1])
+    down = down.reshape(units, width)
+    norms = jnp.pad(wide[:, -NORM_COLS : 4 - NORM_COLS].T.astype(jnp.float32), ((0, 4), (0, 0)))
+    first_block = 2 * units // width
+
+    sibling = pairs_of(shape, lambda z, p, c: (z, p, 1 - c))
+    query, own = project(x, wide, first_block, cosine, sine, k_code)
+    sib = send(own, sibling)
+    probs, attended, inverse_sums = attend_pallas(query, q_code, own, sib)
+    (
+        result, d_resid_one, d_branch, d_attended, hidden_low, mixed, d_gate, d_up, d_ff, sums,
+    ) = middle(x, attended, dy, wide, down, norms)
+    output = from_sequences(result)
+
+    core_id = core.astype(jnp.int32).reshape(1)
+    scatter = functools.partial(reduce_scatter, shape)
+    red_down = scatter(*grad_tall(core_id, mixed, d_ff), False)
+    red_gate = scatter(*grad_wide(core_id, hidden_low, d_gate), True)
+    red_up = scatter(*grad_wide(core_id, hidden_low, d_up), False)
+    red_out = scatter(*grad_out(core_id, attended, d_branch, sums), True)
+    red_norms = red_out[:, width : width + norm_params.shape[0]].T
+    red_out = red_out[:, :width]
+
+    parts = []
+    for first, count in ((0, 2), (2, 2), (4, 2)):
+        d_query, d_own, d_sib = attend_back_pallas(
+            query, own, sib, probs, attended, inverse_sums, d_attended, first, count
+        )
+        parts.append((d_query, d_own, send(d_sib, sibling)))
+    d_projected, keep, away = grad_qkv(core_id, x, cosine, sine, parts)
+    red_qkv = scatter(keep, away, True)
+    d_x = grad_input(d_projected, wide, first_block, d_resid_one)
+    input_grad = from_sequences(d_x).astype(jnp.float32)
+
+    reduced = (red_qkv, red_out, red_gate, red_up, red_down, red_norms)
+    squares = sum(jnp.sum(grad * grad) for grad in reduced)
+    grad_norm = jnp.sqrt(sum_all(shape, squares.reshape(1))[0])
+    clip_factor = jnp.minimum(1.0, MAX_NORM / (grad_norm + 1e-06))
+    weights = (w_qkv, w_out, w_gate, w_up, w_down, norm_params)
+    firsts = (first_qkv, first_out, first_gate, first_up, first_down, first_norms)
+    seconds = (second_qkv, second_out, second_gate, second_up, second_down, second_norms)
+    updated = [
+        adam_update(
+            weight,
+            grad,
+            first,
+            second,
+            0.0 if weight is norm_params else WEIGHT_DECAY,
+            NORM_RATE if weight is norm_params else LEARN_RATE,
+            clip_factor,
+        )
+        for weight, grad, first, second in zip(weights, reduced, firsts, seconds)
+    ]
+    return (
+        output,
+        input_grad,
+        *reduced,
+        *(new for new, _, _ in updated),
+        *(new for _, new, _ in updated),
+        *(new for _, _, new in updated),
+        grad_norm,
+    )
+
+
+def device_program(shape, *arrays):
+    tokens, w_gate, w_down = arrays[0], arrays[5], arrays[7]
+    seqs, line = shape["seq"], shape["fsdp"]
+    seq_count, local_len, width = tokens.shape
+    fits = (
+        seqs == 2 * seq_count
+        and line & (line - 1) == 0
+        and line >= 4
+        and (seq_count * local_len) % 512 == 0
+        and w_gate.shape[0] % 8 == 0
+        and w_down.shape[0] % 8 == 0
+    )
+    return two_to_a_sequence(shape, *arrays) if fits else per_device(*arrays)
+
+
 def solution(mesh):
     return jax.shard_map(
-        per_device,
+        functools.partial(device_program, dict(mesh.shape)),
         mesh=mesh,
         in_specs=(
             P("fsdp", "seq", None),

time: 1900 us -> 628 us (0.33)
  waiting for transfers between devices: 1080 us -> 85.3 us
  matrix products: 441 us -> 0 us
  Pallas kernels: 0 us -> 341 us
  blocking collectives: 136 us -> 0 us
  starting transfers between devices: 0.58 us -> 101 us
  other arithmetic: 147 us -> 55.2 us
  local copies, waits for them, and re-layouts: 68.4 us -> 26.1 us
    reduce_scatter x6 -> x0, waiting for transfers between devices: 632 us -> none  [the longest x1 140 us: per_device(): lax.psum_scatter(g_down, ('seq', 'fsdp'), scatter_dimension=0, tiled=True)]
    dot_general x99 -> x0, matrix products: 441 us -> none  [the longest x24 125 us: one_head(): jnp.einsum('sqd,skd->sqk', query_head, key_head, preferred_element_type=j...]
    pallas_call x0 -> x13, Pallas kernels: none -> 341 us  [the longest x1 101 us: gather_all(): pl.pallas_call(functools.partial(gather_kernel, seqs, bits, pieces), out_...]
    all_gather x7 -> x0, waiting for transfers between devices: 323 us -> none  [the longest x1 107 us: per_device(): lax.all_gather(keys_local, 'seq', axis=1, tiled=True)]
    unnamed x15 -> x0, waiting for transfers between devices: 124 us -> none
    ppermute x0 -> x54, starting transfers between devices: none -> 101 us  [send(): return lax.ppermute(array, AXES, pairs)]
    ppermute x0 -> x54, waiting for transfers between devices: none -> 85.3 us  [send(): return lax.ppermute(array, AXES, pairs)]
    convert_element_type x19, other arithmetic: 84.7 us -> 26 us  [the longest x10 14.6 us: reduce_scatter(): add_up([pick(array, 1 - mine, axis) for array in whole])]
  transfers between devices with their start and end apart: 14 -> 54, of which waited for: 13 -> 15; matrix products, arithmetic and copies ran while one was open for 13% -> 9% of each run, Pallas kernels for 0% -> 37%
where the time goes in v1:
time: 628 us; the launch traced here: 619 us
  Pallas kernels  341 us (54%)
  starting transfers between devices  101 us (16%)
  waiting for transfers between devices  85.3 us (14%)
  other arithmetic  55.2 us (9%)
  local copies, waits for them, and re-layouts  26.1 us (4%)
  between operations  10.8 us (2%)
    pallas_call x1, Pallas kernels, gather_all(): pl.pallas_call(functools.partial(gather_kernel, seqs, bits, pieces), out_...  101 us
    ppermute x54, starting transfers between devices, send(): return lax.ppermute(array, AXES, pairs)  101 us
    ppermute x54, waiting for transfers between devices, send(): return lax.ppermute(array, AXES, pairs)  85.3 us
    pallas_call x3, Pallas kernels, attend_back_pallas(): pl.pallas_call(attend_back_kernel, grid=(pairs, rows // unit), in_specs=[...  79.8 us
    pallas_call x1, Pallas kernels, middle(): pl.pallas_call(middle_kernel, grid=(rows // block,), in_specs=[row(width)...  53.2 us
    pallas_call x1, Pallas kernels, attend_pallas(): pl.pallas_call(functools.partial(attend_kernel, unit, chunk), grid=(pairs...  47.2 us
    pallas_call x2, Pallas kernels, grad_wide(): pl.pallas_call(functools.partial(grad_wide_kernel, tiles), grid_spec=pltp...  19.2 us
    unnamed x105, local copies, waits for them, and re-layouts  17 us
  transfers between devices with their start and end apart: 54, of which 15 were waited for; matrix products, arithmetic and copies ran while one was open for 9% of the time, Pallas kernels for 37%

profile of v1, /device:TPU:0, one launch (start us, length us, event | category | flops | bytes accessed | tf_op | source)
XLA Modules:
  0.0 619.2 jit_solution(15761982342215919421)
XLA Ops:
  3.3 7.4 %collective-permute-start = (bf16[512,768]{1,0:T(8,128)(2,1)}, bf16[512,768]{1,0:T(8,128)(2,1)}, u32[]{:S(2)}, u32[]{:S(2)}) collective-permute-start(bf16[512,768]{1,0:T(8,128)(2,1)} %get-tuple-element.233), channel_id=1, source_target_pairs={{0,0},{1,16},{2,2},{3,18},{4,4},{5,20},{6,6},{7,22},{8,8},{9,24},{... | collective-permute-start | bytes 2359304 | tf_op jit(solution)/shard_map/ppermute | solution.py:1084
  10.7 3.0 collective-permute-start.1
  17.8 101.2 %gather_parameters.1 = (bf16[4,4,48,9472]{3,2,1,0:T(8,128)(2,1)}, bf16[4,4,192,768]{3,2,1,0:T(8,128)(2,1)S(1)}) custom-call(f32[24,3072]{1,0:T(8,128)S(1)} %copy-done.19, f32[24,3072]{1,0:T(8,128)S(1)} %copy-done.17, f32[24,2304]{1,0:T(8,128)S(1)} %copy-done.21, f32[24,768]{1,0:T(8,128)S(1)} %copy-done.23, f32[24,256]{1,0:T(8,128)S(1)} %pad.10.refs_4_, ...), custom_call_target="tpu_custom_call" | custom-call | tf_op jit(solution)/shard_map/gather_parameters/pallas_call | solution.py:580
  122.7 8.4 %project.1 = (bf16[1024,768]{1,0:T(8,128)(2,1)S(1)}, bf16[1024,1664]{1,0:T(8,128)(2,1)}) custom-call(bf16[1024,768]{1,0:T(8,128)(2,1)S(1)} %constant_dynamic-update-slice_fusion.x_ref, bf16[768,9472]{1,0:T(8,128)(2,1)} %bitcast.261, bf16[768,9472]{1,0:T(8,128)(2,1)} %bitcast.262, bf16[768,9472]{1,0:T(8,128)(2,1)} %bitcast.263, ...), custom_call_target="tpu_custom_call" | custom-call | tf_op jit(solution)/shard_map/project/pallas_call | solution.py:635
  136.9 13.4 %collective-permute-done.6 = bf16[512,768]{1,0:T(8,128)(2,1)} collective-permute-done((bf16[512,768]{1,0:T(8,128)(2,1)S(1)}, bf16[512,768]{1,0:T(8,128)(2,1)}, u32[]{:S(2)}, u32[]{:S(2)}) %collective-permute-start.6) | collective-permute-done | bytes 786464 | tf_op jit(solution)/shard_map/ppermute | solution.py:1084
  152.7 47.2 %attend.1 = (bf16[12,2048,1024]{2,1,0:T(8,128)(2,1)}, bf16[1024,768]{1,0:T(8,128)(2,1)}, f32[1024,768]{1,0:T(8,128)}) custom-call(bf16[1024,768]{1,0:T(8,128)(2,1)} %copy-done.1, bf16[1024,128]{1,0:T(8,128)(2,1)} %select_convert_fusion.qc_ref, bf16[1024,1664]{1,0:T(8,128)(2,1)} %get-tuple-element.67.k0.kc0.v0, ...), custom_call_target="tpu_custom_call" | custom-call | tf_op jit(solution)/shard_map/attend/pallas_call | solution.py:704
  199.9 53.2 %middle.1 = (bf16[1024,768]{1,0:T(8,128)(2,1)}, f32[1024,768]{1,0:T(8,128)}, bf16[1024,768]{1,0:T(8,128)(2,1)}, bf16[1024,768]{1,0:T(8,128)(2,1)}, bf16[1024,768...) custom-call(bf16[1024,768]{1,0:T(8,128)(2,1)} %copy-done.2, ...), custom_call_target="tpu_custom_call" | custom-call | tf_op jit(solution)/shard_map/middle/pallas_call | solution.py:873
  256.6 13.8 %collective-permute-start.21 = (bf16[768,512]{1,0:T(8,128)(2,1)S(1)}, bf16[768,512]{1,0:T(8,128)(2,1)}, u32[]{:S(2)}, u32[]{:S(2)}) collective-permute-start(bf16[768,512]{1,0:T(8,128)(2,1)S(1)} %get-tuple-element.90), channel_id=1, source_target_pairs={{0,1},{1,0},{2,3},{3,2},{4,5},{5,4},{6,7},{7,6},{8,9},{9,8},{10,11... | collective-permute-start | bytes 2359304 | tf_op jit(solution)/shard_map/ppermute | solution.py:1084
  270.4 34.5 %attend_back.5 = (f32[1024,256]{1,0:T(8,128)}, f32[2,1024,256]{2,1,0:T(8,128)}, bf16[2,1024,256]{2,1,0:T(8,128)(2,1)}) custom-call(bf16[1024,768]{1,0:T(8,128)(2,1)} %copy-done.1, bf16[1024,1664]{1,0:T(8,128)(2,1)} %get-tuple-element.67.k0.kc0.v0, bf16[1024,1664]{1,0:T(8,128)(2,1)} %get-tuple-element.67.k0.kc0.v0, ...), custom_call_target="tpu_custom_call" | custom-call | tf_op jit(solution)/shard_map/attend_back/pallas_call | solution.py:783
  306.2 7.4 %collective-permute-start.7 = (bf16[512,768]{1,0:T(8,128)(2,1)}, bf16[512,768]{1,0:T(8,128)(2,1)}, u32[]{:S(2)}, u32[]{:S(2)}) collective-permute-start(bf16[512,768]{1,0:T(8,128)(2,1)} %get-tuple-element.229), channel_id=1, source_target_pairs={{0,0},{16,1},{2,2},{18,3},{4,4},{20,5},{6,6},{22,7},{8,8},{24,9},{... | collective-permute-start | bytes 2359304 | tf_op jit(solution)/shard_map/ppermute | solution.py:1084
  313.7 8.9 %collective-permute-start.8 = (bf16[512,768]{1,0:T(8,128)(2,1)}, bf16[512,768]{1,0:T(8,128)(2,1)}, u32[]{:S(2)}, u32[]{:S(2)}) collective-permute-start(bf16[512,768]{1,0:T(8,128)(2,1)} %get-tuple-element.228), channel_id=1, source_target_pairs={{8,0},{24,1},{10,2},{26,3},{12,4},{28,5},{14,6},{30,7},{0,8},{16,9... | collective-permute-start | bytes 2359304 | tf_op jit(solution)/shard_map/ppermute | solution.py:1084
  325.4 9.0 %grad_tall.1 = (bf16[3072,384]{1,0:T(8,128)(2,1)S(1)}, bf16[3072,384]{1,0:T(8,128)(2,1)}) custom-call(s32[1]{0:T(128)} %bitcast.12.core_ref, bf16[1024,3072]{1,0:T(8,128)(2,1)} %get-tuple-element.98.left_ref, bf16[1024,768]{1,0:T(8,128)(2,1)S(1)} %copy-done.15), custom_call_target="tpu_custom_call" | custom-call | tf_op jit(solution)/shard_map/grad_tall/pallas_call | solution.py:951
  335.8 22.6 %attend_back.4 = (f32[1024,256]{1,0:T(8,128)}, f32[2,1024,256]{2,1,0:T(8,128)}, bf16[2,1024,256]{2,1,0:T(8,128)(2,1)}) custom-call(bf16[1024,768]{1,0:T(8,128)(2,1)} %copy-done.1, bf16[1024,1664]{1,0:T(8,128)(2,1)} %get-tuple-element.67.k0.kc0.v0, bf16[1024,1664]{1,0:T(8,128)(2,1)} %get-tuple-element.67.k0.kc0.v0, ...), custom_call_target="tpu_custom_call" | custom-call | tf_op jit(solution)/shard_map/attend_back/pallas_call | solution.py:783
  358.5 22.6 %attend_back.3 = (f32[1024,256]{1,0:T(8,128)}, f32[2,1024,256]{2,1,0:T(8,128)}, bf16[2,1024,256]{2,1,0:T(8,128)(2,1)}) custom-call(bf16[1024,768]{1,0:T(8,128)(2,1)} %copy-done.1, bf16[1024,1664]{1,0:T(8,128)(2,1)} %get-tuple-element.67.k0.kc0.v0, bf16[1024,1664]{1,0:T(8,128)(2,1)} %get-tuple-element.67.k0.kc0.v0, ...), custom_call_target="tpu_custom_call" | custom-call | tf_op jit(solution)/shard_map/attend_back/pallas_call | solution.py:783
  381.8 9.5 %grad_wide.3 = (bf16[768,1536]{1,0:T(8,128)(2,1)S(1)}, bf16[768,1536]{1,0:T(8,128)(2,1)}) custom-call(s32[1]{0:T(128)} %bitcast.12.core_ref, bf16[1024,768]{1,0:T(8,128)(2,1)S(1)} %copy-done.3, bf16[1024,3072]{1,0:T(8,128)(2,1)} %get-tuple-element.95.right_ref), custom_call_target="tpu_custom_call" | custom-call | tf_op jit(solution)/shard_map/grad_wide/pallas_call | solution.py:913
  395.5 9.7 %grad_wide.2 = (bf16[768,1536]{1,0:T(8,128)(2,1)S(1)}, bf16[768,1536]{1,0:T(8,128)(2,1)}) custom-call(s32[1]{0:T(128)} %bitcast.12.core_ref, bf16[1024,768]{1,0:T(8,128)(2,1)S(1)} %copy-done.3, bf16[1024,3072]{1,0:T(8,128)(2,1)} %get-tuple-element.92.right_ref), custom_call_target="tpu_custom_call" | custom-call | tf_op jit(solution)/shard_map/grad_wide/pallas_call | solution.py:913
  412.9 14.6 %grad_qkv.1 = (bf16[1024,2304]{1,0:T(8,128)(2,1)}, bf16[768,1152]{1,0:T(8,128)(2,1)}, bf16[768,1152]{1,0:T(8,128)(2,1)}) custom-call(s32[1]{0:T(128)} %bitcast.12.core_ref, bf16[1024,768]{1,0:T(8,128)(2,1)} %copy-done.2, f32[1024,128]{1,0:T(8,128)} %copy-done.5, f32[1024,128]{1,0:T(8,128)} %copy-done.4, f32[1024,256]{1,0:T(8,128)} %get-tuple-element.74.refs_0_, ...), custom_call_target="tpu_custom_call" | custom-call | tf_op jit(solution)/shard_map/grad_qkv/pallas_call | solution.py:1031
  429.3 3.9 fusion.5
  433.2 7.1 %grad_input.1 = bf16[1024,768]{1,0:T(8,128)(2,1)S(1)} custom-call(bf16[1024,2304]{1,0:T(8,128)(2,1)} %get-tuple-element.83.dproj_ref, bf16[768,9472]{1,0:T(8,128)(2,1)} %bitcast.268, bf16[768,9472]{1,0:T(8,128)(2,1)} %bitcast.269, bf16[768,9472]{1,0:T(8,128)(2,1)} %bitcast.270, f32[1024,768]{1,0:T(8,128)S(1)} %copy-done.7), custom_call_target="tpu_custom_call" | custom-call | tf_op jit(solution)/shard_map/grad_input/pallas_call | solution.py:1058
  442.6 7.8 %collective-permute-start.12 = (bf16[512,768]{1,0:T(8,128)(2,1)}, bf16[512,768]{1,0:T(8,128)(2,1)}, u32[]{:S(2)}, u32[]{:S(2)}) collective-permute-start(bf16[512,768]{1,0:T(8,128)(2,1)} %get-tuple-element.227), channel_id=1, source_target_pairs={{0,0},{16,1},{2,2},{18,3},{4,4},{20,5},{6,6},{22,7},{8,8},{24,9},{... | collective-permute-start | bytes 2359304 | tf_op jit(solution)/shard_map/ppermute | solution.py:1084
  466.9 15.6 %collective-permute-done.13 = bf16[512,768]{1,0:T(8,128)(2,1)S(1)} collective-permute-done((bf16[512,768]{1,0:T(8,128)(2,1)}, bf16[512,768]{1,0:T(8,128)(2,1)S(1)}, u32[]{:S(2)}, u32[]{:S(2)}) %collective-permute-start.13) | collective-permute-done | bytes 786464 | tf_op jit(solution)/shard_map/ppermute | solution.py:1084
  482.4 4.0 fusion.2
  488.8 17.3 %collective-permute-done.36 = bf16[4,2,48,1536]{3,2,1,0:T(8,128)(2,1)S(1)} collective-permute-done((bf16[4,2,48,1536]{3,2,1,0:T(8,128)(2,1)S(1)}, bf16[4,2,48,1536]{3,2,1,0:T(8,128)(2,1)S(1)}, u32[]{:S(2)}, u32[]{:S(2)}) %collective-permute-start.36) | collective-permute-done | bytes 1179680 | tf_op jit(solution)/shard_map/ppermute | solution.py:1084
  514.6 8.0 %collective-permute-done.44 = bf16[4,192,384]{2,1,0:T(8,128)(2,1)S(1)} collective-permute-done((bf16[4,192,384]{2,1,0:T(8,128)(2,1)S(1)}, bf16[4,192,384]{2,1,0:T(8,128)(2,1)S(1)}, u32[]{:S(2)}, u32[]{:S(2)}) %collective-permute-start.44) | collective-permute-done | bytes 589856 | tf_op jit(solution)/shard_map/ppermute | solution.py:1084
  524.9 5.3 collective-permute-done.37
  540.6 4.3 collective-permute-done.18
  548.0 3.4 collective-permute-start.39
  552.5 3.8 collective-permute-start.33
  557.4 4.5 collective-permute-done.31
  562.5 8.0 %collective-permute-done.32 = bf16[48,1536]{1,0:T(8,128)(2,1)S(1)} collective-permute-done((bf16[48,1536]{1,0:T(8,128)(2,1)S(1)}, bf16[48,1536]{1,0:T(8,128)(2,1)S(1)}, u32[]{:S(2)}, u32[]{:S(2)}) %collective-permute-start.32) | collective-permute-done | bytes 147488 | tf_op jit(solution)/shard_map/ppermute | solution.py:1084
  595.9 4.1 collective-permute-start.52
  600.9 4.5 collective-permute-start.53
  (260 shorter events, 120.2 us)
Async XLA Ops:
  3.3 118.1 %collective-permute-start = (bf16[512,768]{1,0:T(8,128)(2,1)}, bf16[512,768]{1,0:T(8,128)(2,1)}, u32[]{:S(2)}, u32[]{:S(2)}) collective-permute-start(bf16[512,768]{1,0:T(8,128)(2,1)} %get-tuple-element.233), channel_id=1, source_target_pairs={{0,0},{1,16},{2,2},{3,18},{4,4},{5,20},{6,6},{7,22},{8,8},{9,24},{... | collective-permute-start | bytes 2359304 | tf_op jit(solution)/shard_map/ppermute | solution.py:1084
  10.7 111.9 %collective-permute-start.1 = (bf16[512,768]{1,0:T(8,128)(2,1)}, bf16[512,768]{1,0:T(8,128)(2,1)S(1)}, u32[]{:S(2)}, u32[]{:S(2)}) collective-permute-start(bf16[512,768]{1,0:T(8,128)(2,1)} %get-tuple-element.232), channel_id=1, source_target_pairs={{0,8},{1,24},{2,10},{3,26},{4,12},{5,28},{6,14},{7,30},{8,0},{9,16... | collective-permute-start | bytes 2359304 | tf_op jit(solution)/shard_map/ppermute | solution.py:1084
  13.8 107.4 %collective-permute-start.2 = (s32[512]{0:T(512)S(1)}, s32[512]{0:T(512)S(1)}, u32[]{:S(2)}, u32[]{:S(2)}) collective-permute-start(s32[512]{0:T(512)S(1)} %bitcast.278), channel_id=1, source_target_pairs={{0,0},{1,16},{2,2},{3,18},{4,4},{5,20},{6,6},{7,22},{8,8},{9,24},{... | collective-permute-start | bytes 6152 | tf_op jit(solution)/shard_map/ppermute | solution.py:1084
  14.4 106.8 %collective-permute-start.3 = (s32[512]{0:T(512)S(1)}, s32[512]{0:T(512)S(1)}, u32[]{:S(2)}, u32[]{:S(2)}) collective-permute-start(s32[512]{0:T(512)S(1)} %bitcast.277), channel_id=1, source_target_pairs={{0,8},{1,24},{2,10},{3,26},{4,12},{5,28},{6,14},{7,30},{8,0},{9,16... | collective-permute-start | bytes 6152 | tf_op jit(solution)/shard_map/ppermute | solution.py:1084
  131.2 21.5 %collective-permute-start.4 = (bf16[1024,1664]{1,0:T(8,128)(2,1)}, bf16[1024,1664]{1,0:T(8,128)(2,1)}, u32[]{:S(2)}, u32[]{:S(2)}) collective-permute-start(bf16[1024,1664]{1,0:T(8,128)(2,1)} %get-tuple-element.67.k0.kc0.v0), channel_id=1, source_target_pairs={{0,1},{1,0},{2,3},{3,2},{4,5},{5,4},{6,7},{7,6},{8,9},{9,8},{10,11... | collective-permute-start | bytes 10223624 | tf_op jit(solution)/shard_map/ppermute | solution.py:1084
  256.6 66.0 %collective-permute-start.21 = (bf16[768,512]{1,0:T(8,128)(2,1)S(1)}, bf16[768,512]{1,0:T(8,128)(2,1)}, u32[]{:S(2)}, u32[]{:S(2)}) collective-permute-start(bf16[768,512]{1,0:T(8,128)(2,1)S(1)} %get-tuple-element.90), channel_id=1, source_target_pairs={{0,1},{1,0},{2,3},{3,2},{4,5},{5,4},{6,7},{7,6},{8,9},{9,8},{10,11... | collective-permute-start | bytes 2359304 | tf_op jit(solution)/shard_map/ppermute | solution.py:1084
  305.0 89.3 %collective-permute-start.11 = (bf16[2,1024,256]{2,1,0:T(8,128)(2,1)}, bf16[2,1024,256]{2,1,0:T(8,128)(2,1)}, u32[]{:S(2)}, u32[]{:S(2)}) collective-permute-start(bf16[2,1024,256]{2,1,0:T(8,128)(2,1)} %get-tuple-element.82), channel_id=1, source_target_pairs={{0,1},{1,0},{2,3},{3,2},{4,5},{5,4},{6,7},{7,6},{8,9},{9,8},{10,11... | collective-permute-start | bytes 3145736 | tf_op jit(solution)/shard_map/ppermute | solution.py:1084
  306.2 74.9 %collective-permute-start.7 = (bf16[512,768]{1,0:T(8,128)(2,1)}, bf16[512,768]{1,0:T(8,128)(2,1)}, u32[]{:S(2)}, u32[]{:S(2)}) collective-permute-start(bf16[512,768]{1,0:T(8,128)(2,1)} %get-tuple-element.229), channel_id=1, source_target_pairs={{0,0},{16,1},{2,2},{18,3},{4,4},{20,5},{6,6},{22,7},{8,8},{24,9},{... | collective-permute-start | bytes 2359304 | tf_op jit(solution)/shard_map/ppermute | solution.py:1084
  313.7 68.0 %collective-permute-start.8 = (bf16[512,768]{1,0:T(8,128)(2,1)}, bf16[512,768]{1,0:T(8,128)(2,1)}, u32[]{:S(2)}, u32[]{:S(2)}) collective-permute-start(bf16[512,768]{1,0:T(8,128)(2,1)} %get-tuple-element.228), channel_id=1, source_target_pairs={{8,0},{24,1},{10,2},{26,3},{12,4},{28,5},{14,6},{30,7},{0,8},{16,9... | collective-permute-start | bytes 2359304 | tf_op jit(solution)/shard_map/ppermute | solution.py:1084
  324.5 68.2 %collective-permute-start.22 = (bf16[4,2,48,512]{3,2,1,0:T(8,128)(2,1)}, bf16[4,2,48,512]{3,2,1,0:T(8,128)(2,1)}, u32[]{:S(2)}, u32[]{:S(2)}) collective-permute-start(bf16[4,2,48,512]{3,2,1,0:T(8,128)(2,1)} %fusion.17), channel_id=1, source_target_pairs={{0,4},{1,5},{2,6},{3,7},{4,0},{5,1},{6,2},{7,3},{8,12},{9,13},{10,... | collective-permute-start | bytes 1179656 | tf_op jit(solution)/shard_map/ppermute | solution.py:1084
  335.8 117.7 %collective-permute-start.42 = (bf16[3072,384]{1,0:T(8,128)(2,1)}, bf16[3072,384]{1,0:T(8,128)(2,1)}, u32[]{:S(2)}, u32[]{:S(2)}) collective-permute-start(bf16[3072,384]{1,0:T(8,128)(2,1)} %get-tuple-element.101), channel_id=1, source_target_pairs={{0,1},{1,0},{2,3},{3,2},{4,5},{5,4},{6,7},{7,6},{8,9},{9,8},{10,11... | collective-permute-start | bytes 7077896 | tf_op jit(solution)/shard_map/ppermute | solution.py:1084
  381.1 26.6 %collective-permute-start.10 = (bf16[2,1024,256]{2,1,0:T(8,128)(2,1)}, bf16[2,1024,256]{2,1,0:T(8,128)(2,1)}, u32[]{:S(2)}, u32[]{:S(2)}) collective-permute-start(bf16[2,1024,256]{2,1,0:T(8,128)(2,1)} %get-tuple-element.79), channel_id=1, source_target_pairs={{0,1},{1,0},{2,3},{3,2},{4,5},{5,4},{6,7},{7,6},{8,9},{9,8},{10,11... | collective-permute-start | bytes 3145736 | tf_op jit(solution)/shard_map/ppermute | solution.py:1084
  381.7 26.1 %collective-permute-start.9 = (bf16[2,1024,256]{2,1,0:T(8,128)(2,1)}, bf16[2,1024,256]{2,1,0:T(8,128)(2,1)}, u32[]{:S(2)}, u32[]{:S(2)}) collective-permute-start(bf16[2,1024,256]{2,1,0:T(8,128)(2,1)} %get-tuple-element.76), channel_id=1, source_target_pairs={{0,1},{1,0},{2,3},{3,2},{4,5},{5,4},{6,7},{7,6},{8,9},{9,8},{10,11... | collective-permute-start | bytes 3145736 | tf_op jit(solution)/shard_map/ppermute | solution.py:1084
  392.7 63.6 %collective-permute-start.35 = (bf16[768,1536]{1,0:T(8,128)(2,1)}, bf16[768,1536]{1,0:T(8,128)(2,1)}, u32[]{:S(2)}, u32[]{:S(2)}) collective-permute-start(bf16[768,1536]{1,0:T(8,128)(2,1)} %get-tuple-element.97), channel_id=1, source_target_pairs={{0,1},{1,0},{2,3},{3,2},{4,5},{5,4},{6,7},{7,6},{8,9},{9,8},{10,11... | collective-permute-start | bytes 7077896 | tf_op jit(solution)/shard_map/ppermute | solution.py:1084
  406.6 52.5 %collective-permute-start.28 = (bf16[768,1536]{1,0:T(8,128)(2,1)}, bf16[768,1536]{1,0:T(8,128)(2,1)}, u32[]{:S(2)}, u32[]{:S(2)}) collective-permute-start(bf16[768,1536]{1,0:T(8,128)(2,1)} %get-tuple-element.94), channel_id=1, source_target_pairs={{0,1},{1,0},{2,3},{3,2},{4,5},{5,4},{6,7},{7,6},{8,9},{9,8},{10,11... | collective-permute-start | bytes 7077896 | tf_op jit(solution)/shard_map/ppermute | solution.py:1084
  407.7 19.8 %collective-permute-start.24 = (bf16[48,512]{1,0:T(8,128)(2,1)S(1)}, bf16[48,512]{1,0:T(8,128)(2,1)S(1)}, u32[]{:S(2)}, u32[]{:S(2)}) collective-permute-start(bf16[48,512]{1,0:T(8,128)(2,1)S(1)} %get-tuple-element.223), channel_id=1, source_target_pairs={{0,8},{1,9},{2,10},{3,11},{4,12},{5,13},{6,14},{7,15},{8,16},{9,17... | collective-permute-start | bytes 147464 | tf_op jit(solution)/shard_map/ppermute | solution.py:1084
  407.8 19.8 %collective-permute-start.25 = (bf16[48,512]{1,0:T(8,128)(2,1)S(1)}, bf16[48,512]{1,0:T(8,128)(2,1)S(1)}, u32[]{:S(2)}, u32[]{:S(2)}) collective-permute-start(bf16[48,512]{1,0:T(8,128)(2,1)S(1)} %get-tuple-element.225), channel_id=1, source_target_pairs={{0,16},{1,17},{2,18},{3,19},{4,20},{5,21},{6,22},{7,23},{8,24},{9,... | collective-permute-start | bytes 147464 | tf_op jit(solution)/shard_map/ppermute | solution.py:1084
  427.6 34.4 %collective-permute-start.14 = (bf16[768,1152]{1,0:T(8,128)(2,1)}, bf16[768,1152]{1,0:T(8,128)(2,1)}, u32[]{:S(2)}, u32[]{:S(2)}) collective-permute-start(bf16[768,1152]{1,0:T(8,128)(2,1)} %get-tuple-element.86), channel_id=1, source_target_pairs={{0,1},{1,0},{2,3},{3,2},{4,5},{5,4},{6,7},{7,6},{8,9},{9,8},{10,11... | collective-permute-start | bytes 5308424 | tf_op jit(solution)/shard_map/ppermute | solution.py:1084
  442.6 22.0 %collective-permute-start.12 = (bf16[512,768]{1,0:T(8,128)(2,1)}, bf16[512,768]{1,0:T(8,128)(2,1)}, u32[]{:S(2)}, u32[]{:S(2)}) collective-permute-start(bf16[512,768]{1,0:T(8,128)(2,1)} %get-tuple-element.227), channel_id=1, source_target_pairs={{0,0},{16,1},{2,2},{18,3},{4,4},{20,5},{6,6},{22,7},{8,8},{24,9},{... | collective-permute-start | bytes 2359304 | tf_op jit(solution)/shard_map/ppermute | solution.py:1084
  453.5 29.0 %collective-permute-start.13 = (bf16[512,768]{1,0:T(8,128)(2,1)}, bf16[512,768]{1,0:T(8,128)(2,1)S(1)}, u32[]{:S(2)}, u32[]{:S(2)}) collective-permute-start(bf16[512,768]{1,0:T(8,128)(2,1)} %get-tuple-element.226), channel_id=1, source_target_pairs={{8,0},{24,1},{10,2},{26,3},{12,4},{28,5},{14,6},{30,7},{0,8},{16,9... | collective-permute-start | bytes 2359304 | tf_op jit(solution)/shard_map/ppermute | solution.py:1084
  456.3 30.1 %collective-permute-start.43 = (bf16[4,2,192,384]{3,2,1,0:T(8,128)(2,1)S(1)}, bf16[4,2,192,384]{3,2,1,0:T(8,128)(2,1)S(1)}, u32[]{:S(2)}, u32[]{:S(2)}) collective-permute-start(bf16[4,2,192,384]{3,2,1,0:T(8,128)(2,1)S(1)} %fusion.9), channel_id=1, source_target_pairs={{0,2},{1,3},{2,0},{3,1},{4,6},{5,7},{6,4},{7,5},{8,10},{9,11},{10,... | collective-permute-start | bytes 3538952 | tf_op jit(solution)/shard_map/ppermute | solution.py:1084
  459.2 47.0 %collective-permute-start.36 = (bf16[4,2,48,1536]{3,2,1,0:T(8,128)(2,1)S(1)}, bf16[4,2,48,1536]{3,2,1,0:T(8,128)(2,1)S(1)}, u32[]{:S(2)}, u32[]{:S(2)}) collective-permute-start(bf16[4,2,48,1536]{3,2,1,0:T(8,128)(2,1)S(1)} %fusion.8), channel_id=1, source_target_pairs={{0,2},{1,3},{2,0},{3,1},{4,6},{5,7},{6,4},{7,5},{8,10},{9,11},{10,... | collective-permute-start | bytes 3538952 | tf_op jit(solution)/shard_map/ppermute | solution.py:1084
  462.0 50.2 %collective-permute-start.29 = (bf16[4,2,48,1536]{3,2,1,0:T(8,128)(2,1)S(1)}, bf16[4,2,48,1536]{3,2,1,0:T(8,128)(2,1)S(1)}, u32[]{:S(2)}, u32[]{:S(2)}) collective-permute-start(bf16[4,2,48,1536]{3,2,1,0:T(8,128)(2,1)S(1)} %fusion.7), channel_id=1, source_target_pairs={{0,4},{1,5},{2,6},{3,7},{4,0},{5,1},{6,2},{7,3},{8,12},{9,13},{10,... | collective-permute-start | bytes 3538952 | tf_op jit(solution)/shard_map/ppermute | solution.py:1084
  464.6 45.4 %collective-permute-start.15 = (bf16[4,2,48,1152]{3,2,1,0:T(8,128)(2,1)S(1)}, bf16[4,2,48,1152]{3,2,1,0:T(8,128)(2,1)S(1)}, u32[]{:S(2)}, u32[]{:S(2)}) collective-permute-start(bf16[4,2,48,1152]{3,2,1,0:T(8,128)(2,1)S(1)} %fusion.13), channel_id=1, source_target_pairs={{0,4},{1,5},{2,6},{3,7},{4,0},{5,1},{6,2},{7,3},{8,12},{9,13},{10,... | collective-permute-start | bytes 2654216 | tf_op jit(solution)/shard_map/ppermute | solution.py:1084
  487.8 34.8 %collective-permute-start.44 = (bf16[4,192,384]{2,1,0:T(8,128)(2,1)S(1)}, bf16[4,192,384]{2,1,0:T(8,128)(2,1)S(1)}, u32[]{:S(2)}, u32[]{:S(2)}) collective-permute-start(bf16[4,192,384]{2,1,0:T(8,128)(2,1)S(1)} %fusion.10), channel_id=1, source_target_pairs={{0,4},{1,5},{2,6},{3,7},{4,0},{5,1},{6,2},{7,3},{8,12},{9,13},{10,... | collective-permute-start | bytes 1769480 | tf_op jit(solution)/shard_map/ppermute | solution.py:1084
  507.5 22.8 %collective-permute-start.37 = (bf16[4,48,1536]{2,1,0:T(8,128)(2,1)S(1)}, bf16[4,48,1536]{2,1,0:T(8,128)(2,1)S(1)}, u32[]{:S(2)}, u32[]{:S(2)}) collective-permute-start(bf16[4,48,1536]{2,1,0:T(8,128)(2,1)S(1)} %fusion.11), channel_id=1, source_target_pairs={{0,4},{1,5},{2,6},{3,7},{4,0},{5,1},{6,2},{7,3},{8,12},{9,13},{10,... | collective-permute-start | bytes 1769480 | tf_op jit(solution)/shard_map/ppermute | solution.py:1084
  511.1 20.4 %collective-permute-start.16 = (bf16[4,48,1152]{2,1,0:T(8,128)(2,1)S(1)}, bf16[4,48,1152]{2,1,0:T(8,128)(2,1)S(1)}, u32[]{:S(2)}, u32[]{:S(2)}) collective-permute-start(bf16[4,48,1152]{2,1,0:T(8,128)(2,1)S(1)} %fusion.14), channel_id=1, source_target_pairs={{0,2},{1,3},{2,0},{3,1},{4,6},{5,7},{6,4},{7,5},{8,10},{9,11},{10,... | collective-permute-start | bytes 1327112 | tf_op jit(solution)/shard_map/ppermute | solution.py:1084
  513.5 21.9 %collective-permute-start.30 = (bf16[4,48,1536]{2,1,0:T(8,128)(2,1)S(1)}, bf16[4,48,1536]{2,1,0:T(8,128)(2,1)S(1)}, u32[]{:S(2)}, u32[]{:S(2)}) collective-permute-start(bf16[4,48,1536]{2,1,0:T(8,128)(2,1)S(1)} %fusion.12), channel_id=1, source_target_pairs={{0,2},{1,3},{2,0},{3,1},{4,6},{5,7},{6,4},{7,5},{8,10},{9,11},{10,... | collective-permute-start | bytes 1769480 | tf_op jit(solution)/shard_map/ppermute | solution.py:1084
  523.9 28.5 %collective-permute-start.45 = (bf16[192,384]{1,0:T(8,128)(2,1)S(1)}, bf16[192,384]{1,0:T(8,128)(2,1)S(1)}, u32[]{:S(2)}, u32[]{:S(2)}) collective-permute-start(bf16[192,384]{1,0:T(8,128)(2,1)S(1)} %get-tuple-element.211), channel_id=1, source_target_pairs={{0,8},{1,9},{2,10},{3,11},{4,12},{5,13},{6,14},{7,15},{8,16},{9,17... | collective-permute-start | bytes 442376 | tf_op jit(solution)/shard_map/ppermute | solution.py:1084
  524.9 27.5 %collective-permute-start.46 = (bf16[192,384]{1,0:T(8,128)(2,1)S(1)}, bf16[192,384]{1,0:T(8,128)(2,1)S(1)}, u32[]{:S(2)}, u32[]{:S(2)}) collective-permute-start(bf16[192,384]{1,0:T(8,128)(2,1)S(1)} %get-tuple-element.213), channel_id=1, source_target_pairs={{0,16},{1,17},{2,18},{3,19},{4,20},{5,21},{6,22},{7,23},{8,24},{9,... | collective-permute-start | bytes 442376 | tf_op jit(solution)/shard_map/ppermute | solution.py:1084
  545.0 27.2 %collective-permute-start.38 = (bf16[48,1536]{1,0:T(8,128)(2,1)S(1)}, bf16[48,1536]{1,0:T(8,128)(2,1)S(1)}, u32[]{:S(2)}, u32[]{:S(2)}) collective-permute-start(bf16[48,1536]{1,0:T(8,128)(2,1)S(1)} %get-tuple-element.214), channel_id=1, source_target_pairs={{0,8},{1,9},{2,10},{3,11},{4,12},{5,13},{6,14},{7,15},{8,16},{9,17... | collective-permute-start | bytes 442376 | tf_op jit(solution)/shard_map/ppermute | solution.py:1084
  548.0 24.3 %collective-permute-start.39 = (bf16[48,1536]{1,0:T(8,128)(2,1)S(1)}, bf16[48,1536]{1,0:T(8,128)(2,1)S(1)}, u32[]{:S(2)}, u32[]{:S(2)}) collective-permute-start(bf16[48,1536]{1,0:T(8,128)(2,1)S(1)} %get-tuple-element.216), channel_id=1, source_target_pairs={{0,16},{1,17},{2,18},{3,19},{4,20},{5,21},{6,22},{7,23},{8,24},{9,... | collective-permute-start | bytes 442376 | tf_op jit(solution)/shard_map/ppermute | solution.py:1084
  (70 other events, 987.1 us)

commit v2 on v1

--- a/solution.py
+++ b/solution.py
@@ -603,6 +603,322 @@
         compiler_params=pltpu.CompilerParams(collective_id=0, has_side_effects=True, vmem_limit_bytes=48 << 20),
         name="gather_parameters",
     )(gate, up, qkv, out, norm, down)
+
+
+def place():
+    f = lax.axis_index("fsdp")
+    return lax.axis_index("seq"), lax.div(f, 2), lax.rem(f, 2)
+
+
+def chip_at(chip, mask):
+    at, b = chip, 0
+    while mask >> b:
+        if (mask >> b) & 1:
+            at = at + (1 - 2 * lax.rem(lax.div(chip, 1 << b), 2)) * (1 << b)
+        b += 1
+    return at
+
+
+def greet(seqs, bits):
+    z, chip, core = place()
+    barrier = pltpu.get_barrier_semaphore()
+    peers = [{"fsdp": 2 * chip + 1 - core}]
+    peers += [{"fsdp": 2 * chip_at(chip, 1 << b) + core} for b in range(bits)]
+    peers += [{"seq": lax.rem(z + k, seqs)} for k in range(1, seqs)]
+    for peer in peers:
+        pl.semaphore_signal(barrier, inc=1, device_id=peer, device_id_type=MESH_ID)
+    pl.semaphore_wait(barrier, len(peers))
+
+
+def hop_masks(order, stage):
+    gone = sum(1 << b for b in order[:stage])
+    return [m for m in range(1 << len(order)) if (m >> order[stage]) & 1 and not m & gone]
+
+
+def hop_slot(order, stage, mask):
+    return [m ^ (1 << order[stage]) for m in hop_masks(order, stage)].index(mask)
+
+
+def reducer_scratch(seqs, bits, pieces, rows, width):
+    dma = pltpu.SemaphoreType.DMA
+    chips = 1 << bits
+    low = jnp.bfloat16
+    hops = [
+        pltpu.VMEM((seqs, len(hop_masks(order, stage)), rows, cols), low)
+        for _, cols, order in pieces
+        for stage in range(bits)
+    ]
+    most = max(1, chips // 2)
+    return [
+        pltpu.VMEM((seqs, chips, rows, width), low),
+        pltpu.VMEM((seqs, rows, width), low),
+        pltpu.VMEM((2, rows // 2, width), jnp.float32),
+        pltpu.VMEM((rows // 2, width), jnp.float32),
+        dma((2, seqs, chips)),
+        dma((2, len(pieces), bits, seqs, most)),
+        dma((2, seqs)),
+        dma((2,)),
+        *hops,
+    ]
+
+
+def reducer(seqs, bits, pieces, away, keep, got, line, halves_ref, swapped, core_sem, hop_sem, line_sem, swap_sem, *hops):
+    z, chip, core = place()
+    rows = keep.shape[2]
+    half = rows // 2
+    sibling = {"fsdp": 2 * chip + 1 - core}
+    masks = range(1 << bits)
+    hop = lambda p, stage: hops[p * bits + stage]
+
+    def remote(source, target, sems, index, device):
+        return pltpu.make_async_remote_copy(
+            source, target, sems.at[(0, *index)], sems.at[(1, *index)], device_id=device, device_id_type=MESH_ID
+        )
+
+    def core_copy(zz, mask):
+        at = chip_at(chip, mask)
+        return remote(away.at[zz, at], got.at[zz, at], core_sem, (zz, at), sibling)
+
+    def hop_copy(p, stage, zz, mask):
+        start, cols, order = pieces[p]
+        slot = hop_slot(order, stage, mask ^ (1 << order[stage]))
+        return remote(
+            got.at[zz, chip_at(chip, mask), :, pl.ds(start, cols)],
+            hop(p, stage).at[zz, slot],
+            hop_sem,
+            (p, stage, zz, slot),
+            {"fsdp": 2 * chip_at(chip, 1 << order[stage]) + core},
+        )
+
+    def line_copy(zz, source):
+        return remote(got.at[zz, chip], line.at[source], line_sem, (source,), {"seq": zz})
+
+    def total(p, zz, mask, stages):
+        start, cols, order = pieces[p]
+        at = chip_at(chip, mask)
+        where = (zz, at, slice(None), pl.ds(start, cols))
+        value = keep[where].astype(jnp.float32) + got[where].astype(jnp.float32)
+        for stage in range(stages):
+            value = value + hop(p, stage)[zz, hop_slot(order, stage, mask)].astype(jnp.float32)
+        return value
+
+    def start():
+        for k in range(1, seqs + 1):
+            zz = lax.rem(z + k, seqs)
+            for mask in reversed(masks):
+                core_copy(zz, mask).start()
+
+    def come(p, stage, zz):
+        for mask in hop_masks(pieces[p][2], stage):
+            hop_copy(p, stage, zz, mask).wait_recv()
+
+    def stage_of(stage, zz):
+        if stage == 0:
+            for mask in masks:
+                core_copy(zz, mask).wait_recv()
+        for p, (first, cols, order) in enumerate(pieces):
+            if stage:
+                come(p, stage - 1, zz)
+            for mask in hop_masks(order, stage):
+                got[zz, chip_at(chip, mask), :, pl.ds(first, cols)] = total(p, zz, mask, stage).astype(jnp.bfloat16)
+                hop_copy(p, stage, zz, mask).start()
+
+    def line_of(zz):
+        for p, (first, cols, _) in enumerate(pieces):
+            come(p, bits - 1, zz)
+            got[zz, chip, :, pl.ds(first, cols)] = total(p, zz, 0, bits).astype(jnp.bfloat16)
+        line_copy(zz, z).start()
+
+    def finish():
+        for p in range(len(pieces)):
+            come(p, bits - 1, z)
+        for k in range(1, seqs):
+            source = lax.rem(z + k, seqs)
+            line_copy(z, source).wait_recv()
+        for p, (first, cols, _) in enumerate(pieces):
+            value = total(p, z, 0, bits)
+            for k in range(1, seqs):
+                value = value + line[lax.rem(z + k, seqs), :, pl.ds(first, cols)].astype(jnp.float32)
+            halves_ref[0, :, pl.ds(first, cols)] = value[:half]
+            halves_ref[1, :, pl.ds(first, cols)] = value[half:]
+        swap = remote(halves_ref.at[1 - core], swapped, swap_sem, (), sibling)
+        swap.start()
+        for zz in range(seqs):
+            for mask in masks:
+                core_copy(zz, mask).wait_send()
+            for p, (_, _, order) in enumerate(pieces):
+                for stage in range(bits):
+                    for mask in hop_masks(order, stage):
+                        hop_copy(p, stage, zz, mask).wait_send()
+        for k in range(1, seqs):
+            line_copy(lax.rem(z + k, seqs), z).wait_send()
+        swap.wait()
+
+    def own(k):
+        return lax.rem(z + k, seqs)
+
+    return start, stage_of, line_of, finish, own
+
+
+def attend_back_kernel(
+    seqs, bits, pieces, plan,
+    q_ref, k0, v0, k1, v1, p_ref, o_ref, inv_ref, do_ref, keep_hbm, away_hbm,
+    dq_ref, own_ref, sib_ref, sum_ref,
+    kt, va, dk, dv, sib, sib_sem, keep, keep_sem, *shared,
+):
+    part = k0.shape[0]
+    unit = q_ref.shape[0]
+    j, i = pl.program_id(0), pl.program_id(1)
+    count = pl.num_programs(1)
+    step = j * count + i
+    z, chip, core = place()
+    lane_k = lax.broadcasted_iota(jnp.int32, (part, 128), 1)
+    start, stage_of, line_of, finish, own = reducer(seqs, bits, pieces, away_hbm, keep, *shared)
+    keep_copy = pltpu.make_async_copy(keep_hbm, keep, keep_sem)
+
+    def sib_copy(pair):
+        return pltpu.make_async_remote_copy(
+            sib.at[lax.rem(pair, 2)],
+            sib_ref.at[:, :, pl.ds(pl.multiple_of(pair * 128, 128), 128)],
+            sib_sem.at[0, pair],
+            sib_sem.at[1, pair],
+            device_id={"fsdp": 2 * chip + 1 - core},
+            device_id_type=MESH_ID,
+        )
+
+    @pl.when(step == 0)
+    def _():
+        keep_copy.start()
+        greet(seqs, bits)
+        start()
+        keep_copy.wait()
+
+    for at, tasks in plan.items():
+
+        @pl.when(step == at)
+        def _():
+            for kind, k in tasks:
+                if kind < bits:
+                    stage_of(kind, own(k))
+                else:
+                    line_of(own(k))
+
+    @pl.when(i == 0)
+    def _():
+        for n, (k_ref, v_ref) in enumerate(((k0, v0), (k1, v1))):
+            k, v = k_ref[...], v_ref[...]
+            zero, one = jnp.zeros_like(v), jnp.ones_like(v)
+            here = slice(n * part, (n + 1) * part)
+            kt[0, :, here] = jnp.where(lane_k < HEAD_DIM, k, zero).T
+            kt[1, :, here] = jnp.where(lane_k < HEAD_DIM, zero, k).T
+            va[0, here] = jnp.where(lane_k < HEAD_DIM, v, jnp.where(lane_k < HEAD_DIM + 3, one, zero))
+            va[1, here] = jnp.where(lane_k >= HEAD_DIM, v, jnp.where(lane_k < 3, one, zero))
+        dk[...] = jnp.zeros_like(dk)
+        dv[...] = jnp.zeros_like(dv)
+
+    lane = lax.broadcasted_iota(jnp.int32, (unit, 128), 1)
+    q = q_ref[...]
+    dof = do_ref[...].astype(jnp.float32) * inv_ref[...]
+    prod = dof * o_ref[...].astype(jnp.float32)
+    dob = dof.astype(jnp.bfloat16)
+    zero = jnp.zeros_like(dob)
+    turned = None
+    for h in range(2):
+        mine = lane < HEAD_DIM if h == 0 else lane >= HEAD_DIM
+        base = HEAD_DIM if h == 0 else 0
+        d = -jnp.sum(jnp.where(mine, prod, 0.0), axis=1, keepdims=True)
+        d1 = d.astype(jnp.bfloat16).astype(jnp.float32)
+        d2 = (d - d1).astype(jnp.bfloat16).astype(jnp.float32)
+        d3 = d - d1 - d2
+        extra = jnp.where(
+            lane == base, d1, jnp.where(lane == base + 1, d2, jnp.where(lane == base + 2, d3, 0.0))
+        ).astype(jnp.bfloat16)
+        p = p_ref[h]
+        ds = (p.astype(jnp.float32) * dotf(va[h], jnp.where(mine, dob, extra), NT)).astype(jnp.bfloat16)
+        dv[...] += dotf(p, jnp.where(mine, dob, zero))
+        dk[...] += dotf(ds, jnp.where(mine, q, zero))
+        new = dotf(kt[h], ds)
+        turned = new if turned is None else turned + new
+    dq_ref[...] = turned.T * (1.0 / math.sqrt(HEAD_DIM))
+
+    @pl.when(i == count - 1)
+    def _():
+        @pl.when(j >= 2)
+        def _():
+            sib_copy(j - 2).wait_send()
+
+        for n, total in enumerate((dk, dv)):
+            own_ref[n] = total[:part]
+            sib[lax.rem(j, 2), n] = total[part:].astype(jnp.bfloat16)
+        sib_copy(j).start()
+
+    @pl.when(step == pl.num_programs(0) * count - 1)
+    def _():
+        finish()
+        halves_ref, swapped = shared[2], shared[3]
+        sum_ref[core] = halves_ref[core]
+        sum_ref[1 - core] = swapped[...]
+        pairs = pl.num_programs(0)
+        for back in (1, 0):
+            sib_copy(pairs - 1 - back).wait_send()
+        lax.fori_loop(0, pairs, lambda pair, _: (sib_copy(pair).wait_recv(), 0)[1], 0)
+
+
+def attend_back_pallas(shape, q, own, sib, p, o, inv, do, keep, away, plan, unit=512):
+    seqs, bits = shape["seq"], (shape["fsdp"] // 2).bit_length() - 1
+    rows, width = q.shape
+    pairs = width // 128
+    part = own.shape[0]
+    low = jnp.bfloat16
+    keep, away = (array.reshape(seqs, 1 << bits, -1, array.shape[1]) for array in (keep, away))
+    sum_rows, sum_cols = keep.shape[2:]
+    pieces = halves_of(sum_cols, bits)
+    row = pl.BlockSpec((unit, 128), lambda j, i: (i, j))
+    kv = [
+        pl.BlockSpec((part, 128), lambda j, i: (0, j)),
+        pl.BlockSpec((part, 128), lambda j, i: (0, j + pairs)),
+    ]
+    any_space = pl.BlockSpec(memory_space=pl.ANY)
+    dma = pltpu.SemaphoreType.DMA
+    return pl.pallas_call(
+        functools.partial(attend_back_kernel, seqs, bits, pieces, plan),
+        grid=(pairs, rows // unit),
+        in_specs=[
+            row, *kv, *kv, pl.BlockSpec((2, 2 * part, unit), lambda j, i: (j, 0, i)), row, row, row, any_space, any_space
+        ],
+        out_specs=[
+            row,
+            pl.BlockSpec((2, part, 128), lambda j, i: (0, 0, j)),
+            any_space,
+            pl.BlockSpec((2, sum_rows // 2, sum_cols), lambda j, i: (0, 0, 0)),
+        ],
+        out_shape=[
+            jax.ShapeDtypeStruct((rows, width), jnp.float32),
+            jax.ShapeDtypeStruct((2, part, width), jnp.float32),
+            jax.ShapeDtypeStruct((2, part, width), low),
+            jax.ShapeDtypeStruct((2, sum_rows // 2, sum_cols), jnp.float32),
+        ],
+        scratch_shapes=[
+            pltpu.VMEM((2, 128, 2 * part), low),
+            pltpu.VMEM((2, 2 * part, 128), low),
+            pltpu.VMEM((2 * part, 128), jnp.float32),
+            pltpu.VMEM((2 * part, 128), jnp.float32),
+            pltpu.VMEM((2, 2, part, 128), low),
+            dma((2, pairs)),
+            pltpu.VMEM(keep.shape, low),
+            dma,
+            *reducer_scratch(seqs, bits, pieces, sum_rows, sum_cols),
+        ],
+        compiler_params=pltpu.CompilerParams(
+            collective_id=1, has_side_effects=True, vmem_limit_bytes=62 << 20
+        ),
+        name="attend_back",
+    )(q, own, own, sib, sib, p, o, inv, do, keep, away)
+
+
+def halves_of(cols, bits):
+    cut = cols // 256 * 128
+    return ((0, cut, tuple(range(bits))), (cut, cols - cut, tuple(reversed(range(bits)))))
 
 
 def turn(field, cosine, sine):
@@ -721,90 +1037,6 @@
     )(q, qc, own, own, own, sib, sib, sib)
 
 
-def attend_back_kernel(q_ref, k0, v0, k1, v1, p_ref, o_ref, inv_ref, do_ref, dq_ref, own_ref, sib_ref, kt, va, dk, dv):
-    part = k0.shape[0]
-    unit = q_ref.shape[0]
-    lane_k = lax.broadcasted_iota(jnp.int32, (part, 128), 1)
-
-    @pl.when(pl.program_id(1) == 0)
-    def _():
-        for i, (k_ref, v_ref) in enumerate(((k0, v0), (k1, v1))):
-            k, v = k_ref[...], v_ref[...]
-            zero, one = jnp.zeros_like(v), jnp.ones_like(v)
-            here = slice(i * part, (i + 1) * part)
-            kt[0, :, here] = jnp.where(lane_k < HEAD_DIM, k, zero).T
-            kt[1, :, here] = jnp.where(lane_k < HEAD_DIM, zero, k).T
-            va[0, here] = jnp.where(lane_k < HEAD_DIM, v, jnp.where(lane_k < HEAD_DIM + 3, one, zero))
-            va[1, here] = jnp.where(lane_k >= HEAD_DIM, v, jnp.where(lane_k < 3, one, zero))
-        dk[...] = jnp.zeros_like(dk)
-        dv[...] = jnp.zeros_like(dv)
-
-    lane = lax.broadcasted_iota(jnp.int32, (unit, 128), 1)
-    q = q_ref[...]
-    dof = do_ref[...].astype(jnp.float32) * inv_ref[...]
-    prod = dof * o_ref[...].astype(jnp.float32)
-    dob = dof.astype(jnp.bfloat16)
-    zero = jnp.zeros_like(dob)
-    turned = None
-    for h in range(2):
-        mine = lane < HEAD_DIM if h == 0 else lane >= HEAD_DIM
-        base = HEAD_DIM if h == 0 else 0
-        d = -jnp.sum(jnp.where(mine, prod, 0.0), axis=1, keepdims=True)
-        d1 = d.astype(jnp.bfloat16).astype(jnp.float32)
-        d2 = (d - d1).astype(jnp.bfloat16).astype(jnp.float32)
-        d3 = d - d1 - d2
-        extra = jnp.where(
-            lane == base, d1, jnp.where(lane == base + 1, d2, jnp.where(lane == base + 2, d3, 0.0))
-        ).astype(jnp.bfloat16)
-        p = p_ref[h]
-        ds = (p.astype(jnp.float32) * dotf(va[h], jnp.where(mine, dob, extra), NT)).astype(jnp.bfloat16)
-        dv[...] += dotf(p, jnp.where(mine, dob, zero))
-        dk[...] += dotf(ds, jnp.where(mine, q, zero))
-        new = dotf(kt[h], ds)
-        turned = new if turned is None else turned + new
-    dq_ref[...] = turned.T * (1.0 / math.sqrt(HEAD_DIM))
-
-    @pl.when(pl.program_id(1) == pl.num_programs(1) - 1)
-    def _():
-        for i, total in enumerate((dk, dv)):
-            own_ref[i] = total[:part]
-            sib_ref[i] = total[part:].astype(jnp.bfloat16)
-
-
-def attend_back_pallas(q, own, sib, p, o, inv, do, first, pairs, unit=512):
-    rows, width = q.shape
-    all_pairs = width // 128
-    part = own.shape[0]
-    row = pl.BlockSpec((unit, 128), lambda j, i: (i, j + first))
-    kv = [
-        pl.BlockSpec((part, 128), lambda j, i: (0, j + first)),
-        pl.BlockSpec((part, 128), lambda j, i: (0, j + first + all_pairs)),
-    ]
-    return pl.pallas_call(
-        attend_back_kernel,
-        grid=(pairs, rows // unit),
-        in_specs=[row, *kv, *kv, pl.BlockSpec((2, 2 * part, unit), lambda j, i: (j + first, 0, i)), row, row, row],
-        out_specs=[
-            pl.BlockSpec((unit, 128), lambda j, i: (i, j)),
-            pl.BlockSpec((2, part, 128), lambda j, i: (0, 0, j)),
-            pl.BlockSpec((2, part, 128), lambda j, i: (0, 0, j)),
-        ],
-        out_shape=[
-            jax.ShapeDtypeStruct((rows, 128 * pairs), jnp.float32),
-            jax.ShapeDtypeStruct((2, part, 128 * pairs), jnp.float32),
-            jax.ShapeDtypeStruct((2, part, 128 * pairs), jnp.bfloat16),
-        ],
-        scratch_shapes=[
-            pltpu.VMEM((2, 128, 2 * part), jnp.bfloat16),
-            pltpu.VMEM((2, 2 * part, 128), jnp.bfloat16),
-            pltpu.VMEM((2 * part, 128), jnp.float32),
-            pltpu.VMEM((2 * part, 128), jnp.float32),
-        ],
-        compiler_params=pltpu.CompilerParams(vmem_limit_bytes=56 << 20),
-        name="attend_back",
-    )(q, own, own, sib, sib, p, o, inv, do)
-
-
 def mean_row(field):
     return jnp.mean(field, -1, keepdims=True)
 
@@ -893,7 +1125,8 @@
     )(x, attended, cotangent, wide, wide, wide, down, norms)
 
 
-def grad_wide_kernel(tiles, core_ref, left_ref, right_ref, keep_ref, send_ref):
+def grad_wide_kernel(tiles, core_ref, left_ref, right_ref, *refs):
+    keep_ref, send_ref = refs[-2:]
     value = dotf(left_ref[...], right_ref[...], TN).astype(jnp.bfloat16)
 
     @pl.when(pl.program_id(0) < tiles)
@@ -905,11 +1138,12 @@
         keep_ref[...] = value
 
 
-def grad_wide(core, left, right, tile=512):
+def grad_wide(core, left, right, held, offset, tile=512):
     rows, width = left.shape
     half = right.shape[1] // 2
     tiles = half // tile
-    like = jax.ShapeDtypeStruct((width, half), jnp.bfloat16)
+    first = offset // tile
+    like = jax.ShapeDtypeStruct(held[0].shape, jnp.bfloat16)
     return pl.pallas_call(
         functools.partial(grad_wide_kernel, tiles),
         grid_spec=pltpu.PrefetchScalarGridSpec(
@@ -920,16 +1154,19 @@
                 pl.BlockSpec(
                     (rows, tile), lambda i, c: (0, lax.rem(c[0] + 1 + lax.div(i, tiles), 2) * tiles + lax.rem(i, tiles))
                 ),
+                pl.BlockSpec(memory_space=pl.ANY),
+                pl.BlockSpec(memory_space=pl.ANY),
             ],
             out_specs=[
-                pl.BlockSpec((width, tile), lambda i, c: (0, jnp.maximum(i - tiles, 0))),
-                pl.BlockSpec((width, tile), lambda i, c: (0, jnp.minimum(i, tiles - 1))),
+                pl.BlockSpec((width, tile), lambda i, c: (0, first + jnp.maximum(i - tiles, 0))),
+                pl.BlockSpec((width, tile), lambda i, c: (0, first + jnp.minimum(i, tiles - 1))),
             ],
         ),
         out_shape=[like, like],
+        input_output_aliases={3: 0, 4: 1},
         compiler_params=pltpu.CompilerParams(vmem_limit_bytes=48 << 20),
         name="grad_wide",
-    )(core, left, right)
+    )(core, left, right, *held)
 
 
 def halves(value, core, keep_ref, send_ref):
@@ -939,23 +1176,45 @@
     send_ref[...] = jnp.where(core == 0, high, low)
 
 
-def grad_tall_kernel(core_ref, left_ref, right_ref, keep_ref, send_ref):
-    halves(dotf(left_ref[...], right_ref[...], TN), core_ref[0], keep_ref, send_ref)
-
-
-def grad_tall(core, left, right, tile=512):
-    rows, height = left.shape
+def grad_tall_kernel(rows, core_ref, left_ref, right_ref, keep_ref, send_ref):
+    value = dotf(left_ref[...], right_ref[...], TN)
+    half = value.shape[1] // 2
+    turns = keep_ref.shape[1] // half
+    core = core_ref[0]
+    for n, part in enumerate((value[:, :half], value[:, half:])):
+        wide = jnp.concatenate(
+            [
+                jnp.concatenate([part[(b * turns + a) * rows : (b * turns + a + 1) * rows] for a in range(turns)], 1)
+                for b in range(part.shape[0] // (turns * rows))
+            ],
+            0,
+        ).astype(jnp.bfloat16)
+
+        @pl.when(core == n)
+        def _():
+            keep_ref[...] = wide
+
+        @pl.when(core != n)
+        def _():
+            send_ref[...] = wide
+
+
+def grad_tall(core, left, right, rows, cols, tile=384):
+    depth, height = left.shape
     width = right.shape[1]
-    out = pl.BlockSpec((tile, width // 2), lambda i, c: (i, 0))
-    like = jax.ShapeDtypeStruct((height, width // 2), jnp.bfloat16)
+    devices = height // (rows * (height // width))
+    fold = height // (devices * rows)
+    tile_rows = tile // fold
+    out = pl.BlockSpec((tile_rows, fold * width // 2), lambda i, c: (i, 0))
+    like = jax.ShapeDtypeStruct((height // fold, cols), jnp.bfloat16)
     return pl.pallas_call(
-        grad_tall_kernel,
+        functools.partial(grad_tall_kernel, rows),
         grid_spec=pltpu.PrefetchScalarGridSpec(
             num_scalar_prefetch=1,
             grid=(height // tile,),
             in_specs=[
-                pl.BlockSpec((rows, tile), lambda i, c: (0, i)),
-                pl.BlockSpec((rows, width), lambda i, c: (0, 0)),
+                pl.BlockSpec((depth, tile), lambda i, c: (0, i)),
+                pl.BlockSpec((depth, width), lambda i, c: (0, 0)),
             ],
             out_specs=[out, out],
         ),
@@ -965,28 +1224,33 @@
     )(core, left, right)
 
 
-def grad_out_kernel(core_ref, left_ref, right_ref, sums_ref, keep_ref, send_ref):
+def grad_out_kernel(core_ref, left_ref, right_ref, sums_ref, _keep, _send, keep_ref, send_ref):
     value = dotf(left_ref[...], right_ref[...], TN)
     pad = jnp.zeros((NORM_COLS - sums_ref.shape[0], sums_ref.shape[1]), jnp.float32)
     norms = jnp.concatenate([sums_ref[...], pad], 0).T
     halves(jnp.concatenate([value, norms], 1), core_ref[0], keep_ref, send_ref)
 
 
-def grad_out(core, left, right, sums):
+def grad_out(core, left, right, sums, held, offset):
     width = left.shape[1]
     full = lambda array: pl.BlockSpec(array.shape, lambda i, c: (0, 0))
     half = (width + NORM_COLS) // 2
-    out = pl.BlockSpec((width, half), lambda i, c: (0, 0))
-    like = jax.ShapeDtypeStruct((width, half), jnp.bfloat16)
+    out = pl.BlockSpec((width, half), lambda i, c: (0, offset // half))
+    like = jax.ShapeDtypeStruct(held[0].shape, jnp.bfloat16)
+    any_space = pl.BlockSpec(memory_space=pl.ANY)
     return pl.pallas_call(
         grad_out_kernel,
         grid_spec=pltpu.PrefetchScalarGridSpec(
-            num_scalar_prefetch=1, grid=(1,), in_specs=[full(left), full(right), full(sums)], out_specs=[out, out]
+            num_scalar_prefetch=1,
+            grid=(1,),
+            in_specs=[full(left), full(right), full(sums), any_space, any_space],
+            out_specs=[out, out],
         ),
         out_shape=[like, like],
+        input_output_aliases={4: 0, 5: 1},
         compiler_params=pltpu.CompilerParams(vmem_limit_bytes=48 << 20),
         name="grad_out",
-    )(core, left, right, sums)
+    )(core, left, right, sums, *held)
 
 
 def grad_qkv_kernel(calls, core_ref, x_ref, cos_ref, sin_ref, *refs):
@@ -1067,6 +1331,7 @@
 
 
 NORM_COLS = 256
+PLAN = {1: ((0, 1),), 2: ((0, 2),), 4: ((0, 3), (1, 1)), 6: ((0, 0), (1, 2)), 8: ((1, 3), (2, 1)), 9: ((2, 2),), 10: ((1, 0),), 11: ((2, 3),)}
 AXES = ("seq", "fsdp")
 
 
@@ -1219,19 +1484,31 @@
 
     core_id = core.astype(jnp.int32).reshape(1)
     scatter = functools.partial(reduce_scatter, shape)
-    red_down = scatter(*grad_tall(core_id, mixed, d_ff), False)
-    red_gate = scatter(*grad_wide(core_id, hidden_low, d_gate), True)
-    red_up = scatter(*grad_wide(core_id, hidden_low, d_up), False)
-    red_out = scatter(*grad_out(core_id, attended, d_branch, sums), True)
+    own_rows = w_gate.shape[0]
+    half_tall, half_wide, half_out = units * width // 2 // width, units // 2, (width + NORM_COLS) // 2
+    cols = half_tall + 2 * half_wide + half_out
+    held = grad_tall(core_id, mixed, d_ff, own_rows, cols)
+    held = grad_wide(core_id, hidden_low, d_gate, held, half_tall)
+    held = grad_wide(core_id, hidden_low, d_up, held, half_tall + half_wide)
+    held = grad_out(core_id, attended, d_branch, sums, held, half_tall + 2 * half_wide)
+    d_query, d_own, d_got, reduced_sums = attend_back_pallas(
+        shape, query, own, sib, probs, attended, inverse_sums, d_attended, *held, PLAN
+    )
+    parts = [(d_query, d_own, d_got)]
+    columns = lambda first, count: jnp.concatenate([reduced_sums[n, :, first : first + count] for n in range(2)], 1)
+    red_down = jnp.concatenate(
+        [
+            reduced_sums[n, :, :half_tall].reshape(own_rows, -1, width // 2).transpose(1, 0, 2).reshape(-1, width // 2)
+            for n in range(2)
+        ],
+        1,
+    )
+    red_gate = columns(half_tall, half_wide)
+    red_up = columns(half_tall + half_wide, half_wide)
+    red_out = columns(half_tall + 2 * half_wide, half_out)
     red_norms = red_out[:, width : width + norm_params.shape[0]].T
     red_out = red_out[:, :width]
 
-    parts = []
-    for first, count in ((0, 2), (2, 2), (4, 2)):
-        d_query, d_own, d_sib = attend_back_pallas(
-            query, own, sib, probs, attended, inverse_sums, d_attended, first, count
-        )
-        parts.append((d_query, d_own, send(d_sib, sibling)))
     d_projected, keep, away = grad_qkv(core_id, x, cosine, sine, parts)
     red_qkv = scatter(keep, away, True)
     d_x = grad_input(d_projected, wide, first_block, d_resid_one)

time: 628 us -> 560 us (0.89)
  starting transfers between devices: 101 us -> 48.5 us
  Pallas kernels: 341 us -> 384 us
  waiting for transfers between devices: 85.3 us -> 51.6 us
  other arithmetic: 55.2 us -> 33.4 us
    ppermute x54 -> x23, starting transfers between devices: 101 us -> 48.5 us  [send(): return lax.ppermute(array, AXES, pairs)]
    pallas_call x4 -> x2, Pallas kernels: 88.8 us -> 129 us  [the longest x1 118 us: attend_back_pallas(): pl.pallas_call(functools.partial(attend_back_kernel, seqs, bits, pieces,...]
    ppermute x54 -> x23, waiting for transfers between devices: 85.3 us -> 51.6 us  [send(): return lax.ppermute(array, AXES, pairs)]
    convert_element_type x10 -> x2, other arithmetic: 14.6 us -> 3.61 us  [reduce_scatter(): add_up([pick(array, 1 - mine, axis) for array in whole])]
    unnamed x105 -> x100, local copies, waits for them, and re-layouts: 17 us -> 7.61 us
  transfers between devices with their start and end apart: 54 -> 23, of which waited for: 15 -> 9; matrix products, arithmetic and copies ran while one was open for 9% -> 8% of each run, Pallas kernels for 37% -> 20%
where the time goes in v2:
time: 560 us; the launch traced here: 552 us
  Pallas kernels  384 us (69%)
  waiting for transfers between devices  51.6 us (9%)
  starting transfers between devices  48.5 us (9%)
  other arithmetic  33.4 us (6%)
  local copies, waits for them, and re-layouts  24.3 us (4%)
  between operations  9.91 us (2%)
    pallas_call x1, Pallas kernels, attend_back_pallas(): pl.pallas_call(functools.partial(attend_back_kernel, seqs, bits, pieces,...  118 us
    pallas_call x1, Pallas kernels, gather_all(): pl.pallas_call(functools.partial(gather_kernel, seqs, bits, pieces), out_...  101 us
    pallas_call x1, Pallas kernels, middle(): pl.pallas_call(middle_kernel, grid=(rows // block,), in_specs=[row(width)...  53 us
    ppermute x23, waiting for transfers between devices, send(): return lax.ppermute(array, AXES, pairs)  51.6 us
    ppermute x23, starting transfers between devices, send(): return lax.ppermute(array, AXES, pairs)  48.5 us
    pallas_call x1, Pallas kernels, attend_pallas(): pl.pallas_call(functools.partial(attend_kernel, unit, chunk), grid=(pairs...  47.2 us
    pallas_call x2, Pallas kernels, grad_wide(): pl.pallas_call(functools.partial(grad_wide_kernel, tiles), grid_spec=pltp...  20.7 us
    pallas_call x1, Pallas kernels, grad_qkv(): pl.pallas_call(functools.partial(grad_qkv_kernel, len(parts)), grid_spec=...  14.6 us
  transfers between devices with their start and end apart: 23, of which 9 were waited for; matrix products, arithmetic and copies ran while one was open for 8% of the time, Pallas kernels for 20%

profile of v2, /device:TPU:0, one launch (start us, length us, event | category | flops | bytes accessed | tf_op | source)
XLA Modules:
  0.0 551.5 jit_solution(10740333086806011109)
XLA Ops:
  0.7 2.6 dynamic-slice_bitcast_fusion.2
  3.3 7.4 %collective-permute-start = (bf16[512,768]{1,0:T(8,128)(2,1)}, bf16[512,768]{1,0:T(8,128)(2,1)}, u32[]{:S(2)}, u32[]{:S(2)}) collective-permute-start(bf16[512,768]{1,0:T(8,128)(2,1)} %get-tuple-element.184), channel_id=1, source_target_pairs={{0,0},{1,16},{2,2},{3,18},{4,4},{5,20},{6,6},{7,22},{8,8},{9,24},{... | collective-permute-start | bytes 2359304 | tf_op jit(solution)/shard_map/ppermute | solution.py:1349
  10.8 3.0 collective-permute-start.1
  17.8 101.2 %gather_parameters.1 = (bf16[4,4,48,9472]{3,2,1,0:T(8,128)(2,1)}, bf16[4,4,192,768]{3,2,1,0:T(8,128)(2,1)S(1)}) custom-call(f32[24,3072]{1,0:T(8,128)S(1)} %copy-done.10, f32[24,3072]{1,0:T(8,128)S(1)} %copy-done.11, f32[24,2304]{1,0:T(8,128)S(1)} %copy-done.15, f32[24,768]{1,0:T(8,128)S(1)} %copy-done.17, f32[24,256]{1,0:T(8,128)S(1)} %pad.10.refs_4_, ...), custom_call_target="tpu_custom_call" | custom-call | tf_op jit(solution)/shard_map/gather_parameters/pallas_call | solution.py:580
  119.1 2.1 copy-done.6
  122.7 8.6 %project.1 = (bf16[1024,768]{1,0:T(8,128)(2,1)S(1)}, bf16[1024,1664]{1,0:T(8,128)(2,1)}) custom-call(bf16[1024,768]{1,0:T(8,128)(2,1)S(1)} %constant_dynamic-update-slice_fusion.x_ref, bf16[768,9472]{1,0:T(8,128)(2,1)} %bitcast.94, bf16[768,9472]{1,0:T(8,128)(2,1)} %bitcast.95, bf16[768,9472]{1,0:T(8,128)(2,1)} %bitcast.96, ...), custom_call_target="tpu_custom_call" | custom-call | tf_op jit(solution)/shard_map/project/pallas_call | solution.py:951
  137.7 14.2 %collective-permute-done.6 = bf16[512,768]{1,0:T(8,128)(2,1)S(1)} collective-permute-done((bf16[512,768]{1,0:T(8,128)(2,1)S(1)}, bf16[512,768]{1,0:T(8,128)(2,1)S(1)}, u32[]{:S(2)}, u32[]{:S(2)}) %collective-permute-start.6) | collective-permute-done | bytes 786464 | tf_op jit(solution)/shard_map/ppermute | solution.py:1349
  151.9 2.4 pad_maximum_fusion.cot_ref
  154.3 47.2 %attend.1 = (bf16[12,2048,1024]{2,1,0:T(8,128)(2,1)}, bf16[1024,768]{1,0:T(8,128)(2,1)}, f32[1024,768]{1,0:T(8,128)}) custom-call(bf16[1024,768]{1,0:T(8,128)(2,1)} %copy-done.3, bf16[1024,128]{1,0:T(8,128)(2,1)} %select_convert_fusion.qc_ref, bf16[1024,1664]{1,0:T(8,128)(2,1)} %get-tuple-element.62.k0.kc0.v0, ...), custom_call_target="tpu_custom_call" | custom-call | tf_op jit(solution)/shard_map/attend/pallas_call | solution.py:1020
  201.5 53.0 %middle.1 = (bf16[1024,768]{1,0:T(8,128)(2,1)}, f32[1024,768]{1,0:T(8,128)}, bf16[1024,768]{1,0:T(8,128)(2,1)}, bf16[1024,768]{1,0:T(8,128)(2,1)}, bf16[1024,768...) custom-call(bf16[1024,768]{1,0:T(8,128)(2,1)} %copy-done, ...), custom_call_target="tpu_custom_call" | custom-call | tf_op jit(solution)/shard_map/middle/pallas_call | solution.py:1105
  255.9 10.9 %grad_tall.1 = (bf16[768,5120]{1,0:T(8,128)(2,1)}, bf16[768,5120]{1,0:T(8,128)(2,1)}) custom-call(s32[1]{0:T(128)} %bitcast.12.core_ref, bf16[1024,3072]{1,0:T(8,128)(2,1)} %get-tuple-element.74.left_ref, bf16[1024,768]{1,0:T(8,128)(2,1)S(1)} %copy-done.9), custom_call_target="tpu_custom_call" | custom-call | tf_op jit(solution)/shard_map/grad_tall/pallas_call | solution.py:1210
  266.8 10.1 %grad_wide.2 = (bf16[768,5120]{1,0:T(8,128)(2,1)}, bf16[768,5120]{1,0:T(8,128)(2,1)}) custom-call(s32[1]{0:T(128)} %bitcast.12.core_ref, bf16[1024,768]{1,0:T(8,128)(2,1)S(1)} %copy-done.2, bf16[1024,3072]{1,0:T(8,128)(2,1)} %get-tuple-element.73.right_ref, ...), custom_call_target="tpu_custom_call", output_to_operand_aliasing={{0}: (3, {}), {1}: (4, {})} | custom-call | tf_op jit(solution)/shard_map/grad_wide/pallas_call | solution.py:1147
  276.9 10.6 %grad_wide.3 = (bf16[768,5120]{1,0:T(8,128)(2,1)}, bf16[768,5120]{1,0:T(8,128)(2,1)}) custom-call(s32[1]{0:T(128)} %bitcast.12.core_ref, bf16[1024,768]{1,0:T(8,128)(2,1)S(1)} %copy-done.2, bf16[1024,3072]{1,0:T(8,128)(2,1)} %get-tuple-element.72.right_ref, ...), custom_call_target="tpu_custom_call", output_to_operand_aliasing={{0}: (3, {}), {1}: (4, {})} | custom-call | tf_op jit(solution)/shard_map/grad_wide/pallas_call | solution.py:1147
  287.5 2.7 grad_out.1
  290.2 117.9 %attend_back.1 = (f32[1024,768]{1,0:T(8,128)}, f32[2,1024,768]{2,1,0:T(8,128)}, bf16[2,1024,768]{2,1,0:T(8,128)(2,1)}, f32[2,24,5120]{2,1,0:T(8,128)}) custom-call(bf16[1024,768]{1,0:T(8,128)(2,1)} %copy-done.3, bf16[1024,1664]{1,0:T(8,128)(2,1)} %get-tuple-element.62.k0.kc0.v0, bf16[1024,1664]{1,0:T(8,128)(2,1)} %get-tuple-element.62.k0.kc0.v0, ...), custom_call_target="tpu_custom_call" | custom-call | tf_op jit(solution)/shard_map/attend_back/pallas_call | solution.py:883
  408.1 14.6 %grad_qkv.1 = (bf16[1024,2304]{1,0:T(8,128)(2,1)}, bf16[768,1152]{1,0:T(8,128)(2,1)}, bf16[768,1152]{1,0:T(8,128)(2,1)}) custom-call(s32[1]{0:T(128)} %bitcast.12.core_ref, bf16[1024,768]{1,0:T(8,128)(2,1)} %copy-done, f32[1024,128]{1,0:T(8,128)} %copy-done.5, f32[1024,128]{1,0:T(8,128)} %copy-done.4, f32[1024,768]{1,0:T(8,128)} %get-tuple-element.84.refs_0_, ...), custom_call_target="tpu_custom_call" | custom-call | tf_op jit(solution)/shard_map/grad_qkv/pallas_call | solution.py:1295
  425.2 2.7 fusion.31
  427.9 7.4 %collective-permute-start.7 = (bf16[512,768]{1,0:T(8,128)(2,1)}, bf16[512,768]{1,0:T(8,128)(2,1)}, u32[]{:S(2)}, u32[]{:S(2)}) collective-permute-start(bf16[512,768]{1,0:T(8,128)(2,1)} %get-tuple-element.180), channel_id=1, source_target_pairs={{0,0},{16,1},{2,2},{18,3},{4,4},{20,5},{6,6},{22,7},{8,8},{24,9},{... | collective-permute-start | bytes 2359304 | tf_op jit(solution)/shard_map/ppermute | solution.py:1349
  436.2 7.1 %grad_input.1 = bf16[1024,768]{1,0:T(8,128)(2,1)S(1)} custom-call(bf16[1024,2304]{1,0:T(8,128)(2,1)} %get-tuple-element.87.dproj_ref, bf16[768,9472]{1,0:T(8,128)(2,1)} %bitcast.101, bf16[768,9472]{1,0:T(8,128)(2,1)} %bitcast.102, bf16[768,9472]{1,0:T(8,128)(2,1)} %bitcast.103, f32[1024,768]{1,0:T(8,128)S(1)} %copy-done.7), custom_call_target="tpu_custom_call" | custom-call | tf_op jit(solution)/shard_map/grad_input/pallas_call | solution.py:1322
  444.6 7.6 %collective-permute-start.9 = (bf16[512,768]{1,0:T(8,128)(2,1)}, bf16[512,768]{1,0:T(8,128)(2,1)}, u32[]{:S(2)}, u32[]{:S(2)}) collective-permute-start(bf16[512,768]{1,0:T(8,128)(2,1)} %get-tuple-element.178), channel_id=1, source_target_pairs={{0,0},{16,1},{2,2},{18,3},{4,4},{20,5},{6,6},{22,7},{8,8},{24,9},{... | collective-permute-start | bytes 2359304 | tf_op jit(solution)/shard_map/ppermute | solution.py:1349
  453.4 2.3 fusion.7
  465.5 7.6 %collective-permute-done.12 = bf16[4,2,48,1152]{3,2,1,0:T(8,128)(2,1)} collective-permute-done((bf16[4,2,48,1152]{3,2,1,0:T(8,128)(2,1)}, bf16[4,2,48,1152]{3,2,1,0:T(8,128)(2,1)}, u32[]{:S(2)}, u32[]{:S(2)}) %collective-permute-start.12) | collective-permute-done | bytes 884768 | tf_op jit(solution)/shard_map/ppermute | solution.py:1349
  474.5 2.0 collective-permute-start.13
  480.2 2.7 collective-permute-done.13
  484.3 2.0 collective-permute-start.15
  486.4 3.9 fusion.5
  491.6 19.6 %collective-permute-done.15 = bf16[48,1152]{1,0:T(8,128)(2,1)S(1)} collective-permute-done((bf16[48,1152]{1,0:T(8,128)(2,1)S(1)}, bf16[48,1152]{1,0:T(8,128)(2,1)S(1)}, u32[]{:S(2)}, u32[]{:S(2)}) %collective-permute-start.15) | collective-permute-done | bytes 110624 | tf_op jit(solution)/shard_map/ppermute | solution.py:1349
  512.4 4.5 fusion.2
  523.6 3.2 collective-permute-start.19
  527.8 3.0 collective-permute-start.20
  533.3 2.2 collective-permute-done.21
  537.5 3.1 collective-permute-done.22
  (180 shorter events, 52.3 us)
Async XLA Ops:
  3.3 118.1 %collective-permute-start = (bf16[512,768]{1,0:T(8,128)(2,1)}, bf16[512,768]{1,0:T(8,128)(2,1)}, u32[]{:S(2)}, u32[]{:S(2)}) collective-permute-start(bf16[512,768]{1,0:T(8,128)(2,1)} %get-tuple-element.184), channel_id=1, source_target_pairs={{0,0},{1,16},{2,2},{3,18},{4,4},{5,20},{6,6},{7,22},{8,8},{9,24},{... | collective-permute-start | bytes 2359304 | tf_op jit(solution)/shard_map/ppermute | solution.py:1349
  10.8 111.8 %collective-permute-start.1 = (bf16[512,768]{1,0:T(8,128)(2,1)}, bf16[512,768]{1,0:T(8,128)(2,1)S(1)}, u32[]{:S(2)}, u32[]{:S(2)}) collective-permute-start(bf16[512,768]{1,0:T(8,128)(2,1)} %get-tuple-element.183), channel_id=1, source_target_pairs={{0,8},{1,24},{2,10},{3,26},{4,12},{5,28},{6,14},{7,30},{8,0},{9,16... | collective-permute-start | bytes 2359304 | tf_op jit(solution)/shard_map/ppermute | solution.py:1349
  13.8 107.4 %collective-permute-start.3 = (s32[512]{0:T(512)S(1)}, s32[512]{0:T(512)S(1)}, u32[]{:S(2)}, u32[]{:S(2)}) collective-permute-start(s32[512]{0:T(512)S(1)} %bitcast.116), channel_id=1, source_target_pairs={{0,8},{1,24},{2,10},{3,26},{4,12},{5,28},{6,14},{7,30},{8,0},{9,16... | collective-permute-start | bytes 6152 | tf_op jit(solution)/shard_map/ppermute | solution.py:1349
  13.9 107.3 %collective-permute-start.2 = (s32[512]{0:T(512)S(1)}, s32[512]{0:T(512)S(1)}, u32[]{:S(2)}, u32[]{:S(2)}) collective-permute-start(s32[512]{0:T(512)S(1)} %bitcast.115), channel_id=1, source_target_pairs={{0,0},{1,16},{2,2},{3,18},{4,4},{5,20},{6,6},{7,22},{8,8},{9,24},{... | collective-permute-start | bytes 6152 | tf_op jit(solution)/shard_map/ppermute | solution.py:1349
  17.1 105.6 %copy-start.5 = (f32[1024,128]{1,0:T(8,128)}, f32[1024,128]{1,0:T(8,128)S(1)}, u32[]{:S(2)}) copy-start(f32[1024,128]{1,0:T(8,128)S(1)} %pad_maximum_fusion.1.cos_ref) | copy-start | bytes 1572868
  17.6 105.1 %copy-start.4 = (f32[1024,128]{1,0:T(8,128)}, f32[1024,128]{1,0:T(8,128)S(1)}, u32[]{:S(2)}) copy-start(f32[1024,128]{1,0:T(8,128)S(1)} %pad_maximum_fusion.2.sin_ref) | copy-start | bytes 1572868
  131.3 23.0 %collective-permute-start.4 = (bf16[1024,1664]{1,0:T(8,128)(2,1)}, bf16[1024,1664]{1,0:T(8,128)(2,1)}, u32[]{:S(2)}, u32[]{:S(2)}) collective-permute-start(bf16[1024,1664]{1,0:T(8,128)(2,1)} %get-tuple-element.62.k0.kc0.v0), channel_id=1, source_target_pairs={{0,1},{1,0},{2,3},{3,2},{4,5},{5,4},{6,7},{7,6},{8,9},{9,8},{10,11... | collective-permute-start | bytes 10223624 | tf_op jit(solution)/shard_map/ppermute | solution.py:1349
  131.8 20.2 %collective-permute-start.6 = (bf16[512,768]{1,0:T(8,128)(2,1)S(1)}, bf16[512,768]{1,0:T(8,128)(2,1)S(1)}, u32[]{:S(2)}, u32[]{:S(2)}) collective-permute-start(bf16[512,768]{1,0:T(8,128)(2,1)S(1)} %get-tuple-element.182), channel_id=1, source_target_pairs={{0,8},{1,24},{2,10},{3,26},{4,12},{5,28},{6,14},{7,30},{8,0},{9,16... | collective-permute-start | bytes 2359304 | tf_op jit(solution)/shard_map/ppermute | solution.py:1349
  133.4 18.6 %collective-permute-start.5 = (bf16[512,768]{1,0:T(8,128)(2,1)S(1)}, bf16[512,768]{1,0:T(8,128)(2,1)}, u32[]{:S(2)}, u32[]{:S(2)}) collective-permute-start(bf16[512,768]{1,0:T(8,128)(2,1)S(1)} %get-tuple-element.181), channel_id=1, source_target_pairs={{0,0},{1,16},{2,2},{3,18},{4,4},{5,20},{6,6},{7,22},{8,8},{9,24},{... | collective-permute-start | bytes 2359304 | tf_op jit(solution)/shard_map/ppermute | solution.py:1349
  422.7 30.7 %collective-permute-start.11 = (bf16[768,1152]{1,0:T(8,128)(2,1)}, bf16[768,1152]{1,0:T(8,128)(2,1)}, u32[]{:S(2)}, u32[]{:S(2)}) collective-permute-start(bf16[768,1152]{1,0:T(8,128)(2,1)} %get-tuple-element.90), channel_id=1, source_target_pairs={{0,1},{1,0},{2,3},{3,2},{4,5},{5,4},{6,7},{7,6},{8,9},{9,8},{10,11... | collective-permute-start | bytes 5308424 | tf_op jit(solution)/shard_map/ppermute | solution.py:1349
  427.9 56.4 %collective-permute-start.7 = (bf16[512,768]{1,0:T(8,128)(2,1)}, bf16[512,768]{1,0:T(8,128)(2,1)}, u32[]{:S(2)}, u32[]{:S(2)}) collective-permute-start(bf16[512,768]{1,0:T(8,128)(2,1)} %get-tuple-element.180), channel_id=1, source_target_pairs={{0,0},{16,1},{2,2},{18,3},{4,4},{20,5},{6,6},{22,7},{8,8},{24,9},{... | collective-permute-start | bytes 2359304 | tf_op jit(solution)/shard_map/ppermute | solution.py:1349
  435.3 51.0 %collective-permute-start.8 = (bf16[512,768]{1,0:T(8,128)(2,1)}, bf16[512,768]{1,0:T(8,128)(2,1)}, u32[]{:S(2)}, u32[]{:S(2)}) collective-permute-start(bf16[512,768]{1,0:T(8,128)(2,1)} %get-tuple-element.179), channel_id=1, source_target_pairs={{8,0},{24,1},{10,2},{26,3},{12,4},{28,5},{14,6},{30,7},{0,8},{16,9... | collective-permute-start | bytes 2359304 | tf_op jit(solution)/shard_map/ppermute | solution.py:1349
  444.6 67.7 %collective-permute-start.9 = (bf16[512,768]{1,0:T(8,128)(2,1)}, bf16[512,768]{1,0:T(8,128)(2,1)}, u32[]{:S(2)}, u32[]{:S(2)}) collective-permute-start(bf16[512,768]{1,0:T(8,128)(2,1)} %get-tuple-element.178), channel_id=1, source_target_pairs={{0,0},{16,1},{2,2},{18,3},{4,4},{20,5},{6,6},{22,7},{8,8},{24,9},{... | collective-permute-start | bytes 2359304 | tf_op jit(solution)/shard_map/ppermute | solution.py:1349
  452.2 60.2 %collective-permute-start.10 = (bf16[512,768]{1,0:T(8,128)(2,1)}, bf16[512,768]{1,0:T(8,128)(2,1)}, u32[]{:S(2)}, u32[]{:S(2)}) collective-permute-start(bf16[512,768]{1,0:T(8,128)(2,1)} %get-tuple-element.177), channel_id=1, source_target_pairs={{8,0},{24,1},{10,2},{26,3},{12,4},{28,5},{14,6},{30,7},{0,8},{16,9... | collective-permute-start | bytes 2359304 | tf_op jit(solution)/shard_map/ppermute | solution.py:1349
  455.7 17.5 %collective-permute-start.12 = (bf16[4,2,48,1152]{3,2,1,0:T(8,128)(2,1)}, bf16[4,2,48,1152]{3,2,1,0:T(8,128)(2,1)}, u32[]{:S(2)}, u32[]{:S(2)}) collective-permute-start(bf16[4,2,48,1152]{3,2,1,0:T(8,128)(2,1)} %fusion.7), channel_id=1, source_target_pairs={{0,4},{1,5},{2,6},{3,7},{4,0},{5,1},{6,2},{7,3},{8,12},{9,13},{10,... | collective-permute-start | bytes 2654216 | tf_op jit(solution)/shard_map/ppermute | solution.py:1349
  465.5 79.8 %copy-start.37 = (f32[24,768]{1,0:T(8,128)}, f32[24,768]{1,0:T(8,128)S(1)}, u32[]{:S(2)}) copy-start(f32[24,768]{1,0:T(8,128)S(1)} %get-tuple-element.171) | copy-start | bytes 221188
  474.5 8.4 %collective-permute-start.13 = (bf16[4,48,1152]{2,1,0:T(8,128)(2,1)S(1)}, bf16[4,48,1152]{2,1,0:T(8,128)(2,1)S(1)}, u32[]{:S(2)}, u32[]{:S(2)}) collective-permute-start(bf16[4,48,1152]{2,1,0:T(8,128)(2,1)S(1)} %fusion.8), channel_id=1, source_target_pairs={{0,2},{1,3},{2,0},{3,1},{4,6},{5,7},{6,4},{7,5},{8,10},{9,11},{10,... | collective-permute-start | bytes 1327112 | tf_op jit(solution)/shard_map/ppermute | solution.py:1349
  477.8 69.1 %copy-start.21 = (f32[24,3072]{1,0:T(8,128)}, f32[24,3072]{1,0:T(8,128)S(1)}, u32[]{:S(2)}) copy-start(f32[24,3072]{1,0:T(8,128)S(1)} %get-tuple-element.169) | copy-start | bytes 884740
  478.5 69.5 %copy-start.22 = (f32[24,3072]{1,0:T(8,128)}, f32[24,3072]{1,0:T(8,128)S(1)}, u32[]{:S(2)}) copy-start(f32[24,3072]{1,0:T(8,128)S(1)} %get-tuple-element.167) | copy-start | bytes 884740
  480.2 68.9 %copy-start.23 = (f32[96,768]{1,0:T(8,128)}, f32[96,768]{1,0:T(8,128)S(1)}, u32[]{:S(2)}) copy-start(f32[96,768]{1,0:T(8,128)S(1)} %get-tuple-element.165) | copy-start | bytes 884740
  484.3 7.3 %collective-permute-start.16 = (bf16[48,1152]{1,0:T(8,128)(2,1)S(1)}, bf16[48,1152]{1,0:T(8,128)(2,1)S(1)}, u32[]{:S(2)}, u32[]{:S(2)}) collective-permute-start(bf16[48,1152]{1,0:T(8,128)(2,1)S(1)} %get-tuple-element.175), channel_id=1, source_target_pairs={{0,24},{1,25},{2,26},{3,27},{4,28},{5,29},{6,30},{7,31},{8,0},{9,1... | collective-permute-start | bytes 331784 | tf_op jit(solution)/shard_map/ppermute | solution.py:1349
  484.3 26.9 %collective-permute-start.15 = (bf16[48,1152]{1,0:T(8,128)(2,1)S(1)}, bf16[48,1152]{1,0:T(8,128)(2,1)S(1)}, u32[]{:S(2)}, u32[]{:S(2)}) collective-permute-start(bf16[48,1152]{1,0:T(8,128)(2,1)S(1)} %get-tuple-element.176), channel_id=1, source_target_pairs={{0,16},{1,17},{2,18},{3,19},{4,20},{5,21},{6,22},{7,23},{8,24},{9,... | collective-permute-start | bytes 331784 | tf_op jit(solution)/shard_map/ppermute | solution.py:1349
  486.3 24.9 %collective-permute-start.14 = (bf16[48,1152]{1,0:T(8,128)(2,1)S(1)}, bf16[48,1152]{1,0:T(8,128)(2,1)S(1)}, u32[]{:S(2)}, u32[]{:S(2)}) collective-permute-start(bf16[48,1152]{1,0:T(8,128)(2,1)S(1)} %get-tuple-element.174), channel_id=1, source_target_pairs={{0,8},{1,9},{2,10},{3,11},{4,12},{5,13},{6,14},{7,15},{8,16},{9,17... | collective-permute-start | bytes 331784 | tf_op jit(solution)/shard_map/ppermute | solution.py:1349
  512.3 4.7 collective-permute-start.17
  512.4 30.9 %copy-start.16 = (f32[24,2304]{1,0:T(8,128)S(1)}, f32[24,2304]{1,0:T(8,128)}, u32[]{:S(2)}) copy-start(f32[24,2304]{1,0:T(8,128)} %refs_2_.1) | copy-start | bytes 663556
  512.4 30.9 %copy-start.38 = (f32[24,2304]{1,0:T(8,128)S(1)}, f32[24,2304]{1,0:T(8,128)}, u32[]{:S(2)}) copy-start(f32[24,2304]{1,0:T(8,128)} %param.32) | copy-start | bytes 663556
  517.7 30.4 %copy-start.25 = (f32[24,2304]{1,0:T(8,128)}, f32[24,2304]{1,0:T(8,128)S(1)}, u32[]{:S(2)}) copy-start(f32[24,2304]{1,0:T(8,128)S(1)} %get-tuple-element.173) | copy-start | bytes 663556
  521.6 1.4 collective-permute-start.18
  523.6 3.6 collective-permute-start.19
  527.8 3.6 collective-permute-start.20
  532.0 3.6 collective-permute-start.21
  536.2 4.5 collective-permute-start.22
  (38 other events, 441.8 us)

commit v3 on v2

--- a/solution.py
+++ b/solution.py
@@ -619,15 +619,86 @@
     return at
 
 
-def greet(seqs, bits):
-    z, chip, core = place()
+def greet(peers):
     barrier = pltpu.get_barrier_semaphore()
-    peers = [{"fsdp": 2 * chip + 1 - core}]
-    peers += [{"fsdp": 2 * chip_at(chip, 1 << b) + core} for b in range(bits)]
-    peers += [{"seq": lax.rem(z + k, seqs)} for k in range(1, seqs)]
     for peer in peers:
         pl.semaphore_signal(barrier, inc=1, device_id=peer, device_id_type=MESH_ID)
     pl.semaphore_wait(barrier, len(peers))
+
+
+def column_peers(seqs):
+    z, chip, core = place()
+    return [{"seq": lax.rem(z + k, seqs), "fsdp": 2 * chip + c} for k in range(1, seqs) for c in range(2)]
+
+
+def plane_peers(line):
+    f = lax.axis_index("fsdp")
+    return [{"fsdp": lax.rem(f + k, line)} for k in range(1, line)]
+
+
+def sum_peers(bits):
+    z, chip, core = place()
+    return [{"fsdp": 2 * chip + 1 - core}] + [{"fsdp": 2 * chip_at(chip, 1 << b) + core} for b in range(bits)]
+
+
+def returns(seqs, seq_count, source, target, sems, rows):
+    z, chip, core = place()
+    group = seqs // seq_count
+    at = z * 2 + core
+    number = lax.div(at, group)
+    slot = lax.rem(number, seq_count)
+    to_core = lax.div(number, seq_count)
+    local_len = target.shape[1]
+    subs = local_len // rows
+
+    def copies(n):
+        t, sub = divmod(n, subs)
+        to_z = lax.rem(at, group) * seq_count + lax.rem(slot - t + seq_count, seq_count)
+        mine = (to_z == z) & (to_core == core)
+        here = target.at[slot, pl.ds(sub * rows, rows)]
+        remote = pltpu.make_async_remote_copy(
+            source(n), here, sems.at[0, n], sems.at[1, slot * subs + sub],
+            device_id={"seq": to_z, "fsdp": 2 * chip + to_core}, device_id_type=MESH_ID,
+        )
+        return mine, remote, pltpu.make_async_copy(source(n), here, sems.at[2, n])
+
+    def begin(n):
+        mine, remote, local = copies(n)
+
+        @pl.when(mine)
+        def _():
+            local.start()
+
+        @pl.when(jnp.logical_not(mine))
+        def _():
+            remote.start()
+
+    def end():
+        for n in range(seq_count * subs):
+            mine, remote, local = copies(n)
+
+            @pl.when(mine)
+            def _():
+                local.wait()
+
+            @pl.when(jnp.logical_not(mine))
+            def _():
+                remote.wait_send()
+
+        for s in range(seq_count):
+            came = (core * seq_count + s) * group + lax.div(z, seq_count)
+            other = jnp.logical_not((lax.div(came, 2) == z) & (lax.rem(came, 2) == core))
+            for sub in range(subs):
+
+                @pl.when(other)
+                def _():
+                    here = target.at[s, pl.ds(sub * rows, rows)]
+                    pltpu.make_async_remote_copy(
+                        source(0), here, sems.at[0, 0], sems.at[1, s * subs + sub],
+                        device_id={"seq": z, "fsdp": 2 * chip + 1 - core}, device_id_type=MESH_ID,
+                    ).wait_recv()
+
+    return begin, end
 
 
 def hop_masks(order, stage):
@@ -762,9 +833,9 @@
 
 def attend_back_kernel(
     seqs, bits, pieces, plan,
-    q_ref, k0, v0, k1, v1, p_ref, o_ref, inv_ref, do_ref, keep_hbm, away_hbm,
-    dq_ref, own_ref, sib_ref, sum_ref,
-    kt, va, dk, dv, sib, sib_sem, keep, keep_sem, *shared,
+    q_ref, k0, v0, k1, v1, p_ref, o_ref, inv_ref, do_ref, keep_hbm, away_hbm, result_hbm,
+    dq_ref, own_ref, sib_ref, sum_ref, output_hbm,
+    kt, va, dk, dv, sib, sib_sem, keep, keep_sem, back_sem, *shared,
 ):
     part = k0.shape[0]
     unit = q_ref.shape[0]
@@ -775,6 +846,10 @@
     lane_k = lax.broadcasted_iota(jnp.int32, (part, 128), 1)
     start, stage_of, line_of, finish, own = reducer(seqs, bits, pieces, away_hbm, keep, *shared)
     keep_copy = pltpu.make_async_copy(keep_hbm, keep, keep_sem)
+    seq_count, local_len = output_hbm.shape[:2]
+    back_begin, back_end = returns(
+        seqs, seq_count, lambda n: result_hbm.at[pl.ds(n * local_len, local_len)], output_hbm, back_sem, local_len
+    )
 
     def sib_copy(pair):
         return pltpu.make_async_remote_copy(
@@ -789,8 +864,10 @@
     @pl.when(step == 0)
     def _():
         keep_copy.start()
-        greet(seqs, bits)
+        greet(sum_peers(bits) + column_peers(seqs))
         start()
+        for n in range(seq_count):
+            back_begin(n)
         keep_copy.wait()
 
     for at, tasks in plan.items():
@@ -855,6 +932,7 @@
     @pl.when(step == pl.num_programs(0) * count - 1)
     def _():
         finish()
+        back_end()
         halves_ref, swapped = shared[2], shared[3]
         sum_ref[core] = halves_ref[core]
         sum_ref[1 - core] = swapped[...]
@@ -864,7 +942,7 @@
         lax.fori_loop(0, pairs, lambda pair, _: (sib_copy(pair).wait_recv(), 0)[1], 0)
 
 
-def attend_back_pallas(shape, q, own, sib, p, o, inv, do, keep, away, plan, unit=512):
+def attend_back_pallas(shape, q, own, sib, p, o, inv, do, keep, away, result, seq_count, plan, unit=512):
     seqs, bits = shape["seq"], (shape["fsdp"] // 2).bit_length() - 1
     rows, width = q.shape
     pairs = width // 128
@@ -884,19 +962,22 @@
         functools.partial(attend_back_kernel, seqs, bits, pieces, plan),
         grid=(pairs, rows // unit),
         in_specs=[
-            row, *kv, *kv, pl.BlockSpec((2, 2 * part, unit), lambda j, i: (j, 0, i)), row, row, row, any_space, any_space
+            row, *kv, *kv, pl.BlockSpec((2, 2 * part, unit), lambda j, i: (j, 0, i)), row, row, row,
+            any_space, any_space, any_space,
         ],
         out_specs=[
             row,
             pl.BlockSpec((2, part, 128), lambda j, i: (0, 0, j)),
             any_space,
             pl.BlockSpec((2, sum_rows // 2, sum_cols), lambda j, i: (0, 0, 0)),
+            any_space,
         ],
         out_shape=[
             jax.ShapeDtypeStruct((rows, width), jnp.float32),
             jax.ShapeDtypeStruct((2, part, width), jnp.float32),
             jax.ShapeDtypeStruct((2, part, width), low),
             jax.ShapeDtypeStruct((2, sum_rows // 2, sum_cols), jnp.float32),
+            jax.ShapeDtypeStruct((seq_count, rows // seq_count, width), low),
         ],
         scratch_shapes=[
             pltpu.VMEM((2, 128, 2 * part), low),
@@ -907,13 +988,210 @@
             dma((2, pairs)),
             pltpu.VMEM(keep.shape, low),
             dma,
+            dma((3, seq_count)),
             *reducer_scratch(seqs, bits, pieces, sum_rows, sum_cols),
         ],
         compiler_params=pltpu.CompilerParams(
             collective_id=1, has_side_effects=True, vmem_limit_bytes=62 << 20
         ),
         name="attend_back",
-    )(q, own, own, sib, sib, p, o, inv, do, keep, away)
+    )(q, own, own, sib, sib, p, o, inv, do, keep, away, result)
+
+
+def tail_kernel(
+    seqs, bits, pieces,
+    cos_ref, sin_ref, dq_ref, own_ref, got_ref, wq_ref, wk_ref, wv_ref, dr_ref, x_ref, sum_ref,
+    back_ref, qsum_ref, square_ref,
+    dproj, dx, keep, away, plane, line_sum, back_sem, plane_sem, total_sem, *shared,
+):
+    z, chip, core = place()
+    f = 2 * chip + core
+    line = 2 << bits
+    block, width = dr_ref.shape
+    i = pl.program_id(0)
+    blocks = dx.shape[0]
+    low = jnp.bfloat16
+    start, stage_of, line_of, finish, own = reducer(seqs, bits, pieces, away, keep, *shared)
+    back_begin, back_end = returns(seqs, back_ref.shape[0], lambda n: dx.at[n], back_ref, back_sem, block)
+
+    @pl.when(i == 0)
+    def _():
+        greet(plane_peers(line) + column_peers(seqs))
+
+    cosine, sine = cos_ref[...], -sin_ref[...]
+    grads = (
+        turn(dq_ref[...], cosine, sine).astype(low),
+        turn(own_ref[0] + got_ref[0].astype(jnp.float32), cosine, sine).astype(low),
+        (own_ref[1] + got_ref[1].astype(jnp.float32)).astype(low),
+    )
+    value = dr_ref[...]
+    rows = pl.ds(pl.multiple_of(i * block, block), block)
+    for n, (grad, w_ref) in enumerate(zip(grads, (wq_ref, wk_ref, wv_ref))):
+        dproj[rows, n * width : (n + 1) * width] = grad
+        value = value + dotf(grad, w_ref[...], NT)
+    dx[i] = value.astype(low)
+    for n in range(blocks):
+
+        @pl.when(i == n)
+        def _():
+            back_begin(n)
+
+    @pl.when(i == blocks - 1)
+    def _():
+        half = keep.shape[-1]
+        tile = 384
+        for target, side in ((away, 1 - core), (keep, core)):
+            for n in range(half // tile):
+                cols = pl.ds(pl.multiple_of(side * half + n * tile, 128), tile)
+                grad = dotf(x_ref[...], dproj[:, cols], TN).astype(low)
+                target[:, :, :, n * tile : (n + 1) * tile] = grad.reshape(target.shape[:3] + (tile,))
+            if target is away:
+                start()
+        order = [*range(1, seqs), 0]
+        for k in order:
+            stage_of(0, own(k))
+        for stage in range(1, bits):
+            for k in order:
+                stage_of(stage, own(k))
+        for k in order[:-1]:
+            line_of(own(k))
+        finish()
+        halves_ref, swapped = shared[2], shared[3]
+        qsum_ref[core] = halves_ref[core]
+        qsum_ref[1 - core] = swapped[...]
+        squares = jnp.sum(jnp.square(sum_ref[...])) + jnp.sum(jnp.square(qsum_ref[...]))
+        plane[f] = jnp.zeros(plane.shape[1:], jnp.float32) + squares
+
+        def plane_copy(to, source):
+            return pltpu.make_async_remote_copy(
+                plane.at[source], plane.at[source], plane_sem.at[0, to], plane_sem.at[1, source],
+                device_id={"fsdp": to}, device_id_type=MESH_ID,
+            )
+
+        def total_copy(to, source):
+            return pltpu.make_async_remote_copy(
+                line_sum.at[source], line_sum.at[source], total_sem.at[0, to], total_sem.at[1, source],
+                device_id={"seq": to}, device_id_type=MESH_ID,
+            )
+
+        for k in range(1, line):
+            plane_copy(lax.rem(f + k, line), f).start()
+        for k in range(1, line):
+            plane_copy(lax.rem(f + k, line), lax.rem(f + k, line)).wait_recv()
+        line_sum[z] = sum(plane[n] for n in range(line))
+        for k in range(1, seqs):
+            total_copy(lax.rem(z + k, seqs), z).start()
+        for k in range(1, seqs):
+            total_copy(lax.rem(z + k, seqs), lax.rem(z + k, seqs)).wait_recv()
+        square_ref[...] = sum(line_sum[n] for n in range(seqs))
+        for k in range(1, line):
+            plane_copy(lax.rem(f + k, line), f).wait_send()
+        for k in range(1, seqs):
+            total_copy(lax.rem(z + k, seqs), z).wait_send()
+        back_end()
+
+
+def tail(shape, cosine, sine, d_query, own, got, wide, first, d_resid, x, sums, seq_count, block=256):
+    seqs, line = shape["seq"], shape["fsdp"]
+    bits = (line // 2).bit_length() - 1
+    rows, width = x.shape
+    low = jnp.bfloat16
+    sum_rows, sum_cols = width // (seqs * line // 2), 3 * width // 2
+    pieces = halves_of(sum_cols, bits)
+    dma = pltpu.SemaphoreType.DMA
+    row = lambda cols: pl.BlockSpec((block, cols), lambda i: (i, 0))
+    pair = pl.BlockSpec((2, block, width), lambda i: (0, i, 0))
+    once = pl.Buffered(1)
+    weight = lambda n: pl.BlockSpec((width, width), lambda i, n=n: (0, first + n), pipeline_mode=once)
+    blocks = rows // block
+    return pl.pallas_call(
+        functools.partial(tail_kernel, seqs, bits, pieces),
+        grid=(blocks,),
+        in_specs=[
+            row(128), row(128), row(width), pair, pair, weight(0), weight(1), weight(2), row(width),
+            pl.BlockSpec(x.shape, lambda i: (0, 0), pipeline_mode=once),
+            pl.BlockSpec(sums.shape, lambda i: (0, 0, 0), pipeline_mode=once),
+        ],
+        out_specs=[
+            pl.BlockSpec(memory_space=pl.ANY),
+            pl.BlockSpec((2, sum_rows // 2, sum_cols), lambda i: (0, 0, 0)),
+            pl.BlockSpec((8, 128), lambda i: (0, 0)),
+        ],
+        out_shape=[
+            jax.ShapeDtypeStruct((seq_count, rows // seq_count, width), low),
+            jax.ShapeDtypeStruct((2, sum_rows // 2, sum_cols), jnp.float32),
+            jax.ShapeDtypeStruct((8, 128), jnp.float32),
+        ],
+        scratch_shapes=[
+            pltpu.VMEM((rows, 3 * width), low),
+            pltpu.VMEM((blocks, block, width), low),
+            pltpu.VMEM((seqs, 1 << bits, sum_rows, sum_cols), low),
+            pltpu.VMEM((seqs, 1 << bits, sum_rows, sum_cols), low),
+            pltpu.VMEM((line, 8, 128), jnp.float32),
+            pltpu.VMEM((seqs, 8, 128), jnp.float32),
+            dma((3, blocks)),
+            dma((2, line)),
+            dma((2, seqs)),
+            *reducer_scratch(seqs, bits, pieces, sum_rows, sum_cols),
+        ],
+        compiler_params=pltpu.CompilerParams(collective_id=2, has_side_effects=True, vmem_limit_bytes=60 << 20),
+        name="tail",
+    )(cosine, sine, d_query, own, got, wide, wide, wide, d_resid, x, sums)
+
+
+def adam_kernel(sum_ref, qsum_ref, square_ref, back_ref, *refs):
+    states, outs = refs[:18], refs[18:]
+    back_out, norm_out = outs[24:]
+    back_out[...] = back_ref[...].astype(jnp.float32)
+    norm = jnp.sqrt(square_ref[0:1, 0:1])
+    norm_out[...] = norm
+    clip = jnp.minimum(1.0, MAX_NORM / (norm + 1e-06))
+    rows, units = states[2].shape
+    width = states[1].shape[1]
+    tall, wide, out = units // 2, units // 2, (width + NORM_COLS) // 2
+    at = tall + 2 * wide
+    take = lambda first, count: jnp.concatenate([sum_ref[n, :, first : first + count] for n in range(2)], 1)
+    fold = states[4].shape[0] // rows
+    red_out = take(at, out)
+    norms = red_out[:, width : width + 128].T[: states[5].shape[0]]
+    grads = (
+        jnp.concatenate([qsum_ref[0], qsum_ref[1]], 1),
+        red_out[:, :width],
+        take(tall, wide),
+        take(tall + wide, wide),
+        jnp.concatenate(
+            [
+                jnp.concatenate([sum_ref[n, :, a * (width // 2) : (a + 1) * (width // 2)] for n in range(2)], 1)
+                for a in range(fold)
+            ],
+            0,
+        ),
+        norms,
+    )
+    for n, grad in enumerate(grads):
+        rates = (0.0, NORM_RATE) if n == 5 else (WEIGHT_DECAY, LEARN_RATE)
+        outs[n][...] = grad
+        new, first, second = adam_update(
+            states[n][...], grad, states[6 + n][...], states[12 + n][...], *rates, clip
+        )
+        outs[6 + n][...] = new
+        outs[12 + n][...] = first
+        outs[18 + n][...] = second
+
+
+def adam(sums, qsums, squares, back, states):
+    like = lambda array: jax.ShapeDtypeStruct(array.shape, jnp.float32)
+    vmem = pl.BlockSpec(memory_space=pltpu.VMEM)
+    outs = [like(array) for array in states[:6]] * 4
+    outs += [like(back), jax.ShapeDtypeStruct((1, 1), jnp.float32)]
+    return pl.pallas_call(
+        adam_kernel,
+        in_specs=[vmem] * (4 + len(states)),
+        out_specs=[vmem] * len(outs),
+        out_shape=outs,
+        compiler_params=pltpu.CompilerParams(vmem_limit_bytes=56 << 20),
+        name="adam",
+    )(sums, qsums, squares, back, *states)
 
 
 def halves_of(cols, bits):
@@ -1253,83 +1531,6 @@
     )(core, left, right, sums, *held)
 
 
-def grad_qkv_kernel(calls, core_ref, x_ref, cos_ref, sin_ref, *refs):
-    parts = [refs[3 * n : 3 * n + 3] for n in range(calls)]
-    dproj_ref, keep_ref, send_ref, total = refs[3 * calls :]
-    join = lambda pieces: jnp.concatenate(pieces, -1)
-    d_query = join([dq[...] for dq, _, _ in parts])
-    d_keys = join([own[0] + got[0].astype(jnp.float32) for _, own, got in parts])
-    d_values = join([own[1] + got[1].astype(jnp.float32) for _, own, got in parts])
-    cosine, sine = cos_ref[...], -sin_ref[...]
-    low = jnp.bfloat16
-    d_projected = join(
-        [turn(d_query, cosine, sine).astype(low), turn(d_keys, cosine, sine).astype(low), d_values.astype(low)]
-    )
-    dproj_ref[...] = d_projected
-    new = dotf(x_ref[...], d_projected, TN)
-
-    @pl.when(pl.program_id(0) == 0)
-    def _():
-        total[...] = new
-
-    @pl.when(pl.program_id(0) > 0)
-    def _():
-        total[...] += new
-
-    @pl.when(pl.program_id(0) == pl.num_programs(0) - 1)
-    def _():
-        halves(total[...], core_ref[0], keep_ref, send_ref)
-
-
-def grad_qkv(core, x, cosine, sine, parts, block=256):
-    rows, width = x.shape
-    row = lambda cols: pl.BlockSpec((block, cols), lambda i, c: (i, 0))
-    specs, arrays = [], []
-    for d_query, own, got in parts:
-        cols = d_query.shape[1]
-        pair = pl.BlockSpec((2, block, cols), lambda i, c: (0, i, 0))
-        specs += [row(cols), pair, pair]
-        arrays += [d_query, own, got]
-    half = pl.BlockSpec((width, 3 * width // 2), lambda i, c: (0, 0))
-    like = jax.ShapeDtypeStruct((width, 3 * width // 2), jnp.bfloat16)
-    return pl.pallas_call(
-        functools.partial(grad_qkv_kernel, len(parts)),
-        grid_spec=pltpu.PrefetchScalarGridSpec(
-            num_scalar_prefetch=1,
-            grid=(rows // block,),
-            in_specs=[row(width), row(128), row(128), *specs],
-            out_specs=[row(3 * width), half, half],
-            scratch_shapes=[pltpu.VMEM((width, 3 * width), jnp.float32)],
-        ),
-        out_shape=[jax.ShapeDtypeStruct((rows, 3 * width), jnp.bfloat16), like, like],
-        compiler_params=pltpu.CompilerParams(vmem_limit_bytes=56 << 20),
-        name="grad_qkv",
-    )(core, x, cosine, sine, *arrays)
-
-
-def grad_input_kernel(dproj_ref, wq_ref, wk_ref, wv_ref, dr_ref, dx_ref):
-    width = dr_ref.shape[1]
-    total = dr_ref[...]
-    for n, w_ref in enumerate((wq_ref, wk_ref, wv_ref)):
-        total = total + dotf(dproj_ref[:, n * width : (n + 1) * width], w_ref[...], NT)
-    dx_ref[...] = total.astype(jnp.bfloat16)
-
-
-def grad_input(d_projected, wide, first, d_resid, block=256):
-    rows, width = d_resid.shape
-    weight = lambda n: pl.BlockSpec((width, width), lambda i, n=n: (0, first + n))
-    row = lambda cols: pl.BlockSpec((block, cols), lambda i: (i, 0))
-    return pl.pallas_call(
-        grad_input_kernel,
-        grid=(rows // block,),
-        in_specs=[row(3 * width), weight(0), weight(1), weight(2), row(width)],
-        out_specs=row(width),
-        out_shape=jax.ShapeDtypeStruct((rows, width), jnp.bfloat16),
-        compiler_params=pltpu.CompilerParams(vmem_limit_bytes=48 << 20),
-        name="grad_input",
-    )(d_projected, wide, wide, wide, d_resid)
-
-
 NORM_COLS = 256
 PLAN = {1: ((0, 1),), 2: ((0, 2),), 4: ((0, 3), (1, 1)), 6: ((0, 0), (1, 2)), 8: ((1, 3), (2, 1)), 9: ((2, 2),), 10: ((1, 0),), 11: ((2, 3),)}
 AXES = ("seq", "fsdp")
@@ -1351,57 +1552,6 @@
 
 def pick(array, index, axis):
     return lax.dynamic_index_in_dim(array, index, axis, keepdims=False)
-
-
-def add_up(arrays):
-    return sum(array.astype(jnp.float32) for array in arrays)
-
-
-def reduce_scatter(shape, keep, away, downward):
-    seqs, chips = shape["seq"], shape["fsdp"] // 2
-    bits = chips.bit_length() - 1
-    z = lax.axis_index("seq")
-    f = lax.axis_index("fsdp")
-    core, chip = f % 2, f // 2
-    half = keep.shape[1]
-    rows = keep.shape[0] // (seqs * chips)
-    got = send(away, pairs_of(shape, lambda z, p, c: (z, p, 1 - c)))
-    whole = [array.reshape((seqs,) + (2,) * bits + (rows, half)) for array in (keep, got)]
-    left = list(reversed(range(bits)))
-    for b in left if downward else range(bits):
-        axis = 1 + sorted(left, reverse=True).index(b)
-        left = [n for n in left if n != b]
-        mine = (chip >> b) & 1
-        away = add_up([pick(array, 1 - mine, axis) for array in whole]).astype(jnp.bfloat16)
-        got = send(away, pairs_of(shape, lambda z, p, c: (z, p ^ (1 << b), c)))
-        whole = [pick(array, mine, axis) for array in whole] + [got]
-    terms = [add_up([pick(array, z, 0) for array in whole])]
-    for k in range(1, seqs):
-        away = add_up([pick(array, (z + k) % seqs, 0) for array in whole]).astype(jnp.bfloat16)
-        terms.append(send(away, pairs_of(shape, lambda z, p, c: ((z + k) % seqs, p, c))))
-    total = add_up(terms)
-    mine, away = jnp.where(core == 0, 0, rows // 2), jnp.where(core == 0, rows // 2, 0)
-    got = send(
-        lax.dynamic_slice_in_dim(total, away, rows // 2, 0), pairs_of(shape, lambda z, p, c: (z, p, 1 - c))
-    )
-    mine = lax.dynamic_slice_in_dim(total, mine, rows // 2, 0)
-    return jnp.where(core == 0, jnp.concatenate([mine, got], 1), jnp.concatenate([got, mine], 1))
-
-
-def sum_all(shape, value):
-    seqs, chips = shape["seq"], shape["fsdp"] // 2
-    moves = [lambda z, p, c: (z, p, 1 - c)]
-    b = 1
-    while b < chips:
-        moves.append(lambda z, p, c, b=b: (z, p ^ b, c))
-        b *= 2
-    b = 1
-    while b < seqs:
-        moves.append(lambda z, p, c, b=b: (z ^ b, p, c))
-        b *= 2
-    for move in moves:
-        value = value + send(value, pairs_of(shape, move))
-    return value
 
 
 def seg_codes(segments):
@@ -1437,18 +1587,11 @@
         return pairs_of(shape, move)
 
     out_pairs = [there(t) for t in range(seq_count)]
-    back_pairs = [[(to, at) for at, to in pairs] for pairs in out_pairs]
 
     def to_sequences(array):
         return jnp.concatenate(
             [send(pick(array, (z + t) % seq_count, 0), out_pairs[t]) for t in range(seq_count)], 0
         )
-
-    def from_sequences(array):
-        got = jnp.stack(
-            [send(array[t * local_len : (t + 1) * local_len], back_pairs[t]) for t in range(seq_count)]
-        )
-        return jnp.roll(got, z % seq_count, 0)
 
     x = to_sequences(tokens)
     segments = to_sequences(segment_ids)
@@ -1480,10 +1623,8 @@
     (
         result, d_resid_one, d_branch, d_attended, hidden_low, mixed, d_gate, d_up, d_ff, sums,
     ) = middle(x, attended, dy, wide, down, norms)
-    output = from_sequences(result)
 
     core_id = core.astype(jnp.int32).reshape(1)
-    scatter = functools.partial(reduce_scatter, shape)
     own_rows = w_gate.shape[0]
     half_tall, half_wide, half_out = units * width // 2 // width, units // 2, (width + NORM_COLS) // 2
     cols = half_tall + 2 * half_wide + half_out
@@ -1491,57 +1632,19 @@
     held = grad_wide(core_id, hidden_low, d_gate, held, half_tall)
     held = grad_wide(core_id, hidden_low, d_up, held, half_tall + half_wide)
     held = grad_out(core_id, attended, d_branch, sums, held, half_tall + 2 * half_wide)
-    d_query, d_own, d_got, reduced_sums = attend_back_pallas(
-        shape, query, own, sib, probs, attended, inverse_sums, d_attended, *held, PLAN
-    )
-    parts = [(d_query, d_own, d_got)]
-    columns = lambda first, count: jnp.concatenate([reduced_sums[n, :, first : first + count] for n in range(2)], 1)
-    red_down = jnp.concatenate(
-        [
-            reduced_sums[n, :, :half_tall].reshape(own_rows, -1, width // 2).transpose(1, 0, 2).reshape(-1, width // 2)
-            for n in range(2)
-        ],
-        1,
-    )
-    red_gate = columns(half_tall, half_wide)
-    red_up = columns(half_tall + half_wide, half_wide)
-    red_out = columns(half_tall + 2 * half_wide, half_out)
-    red_norms = red_out[:, width : width + norm_params.shape[0]].T
-    red_out = red_out[:, :width]
-
-    d_projected, keep, away = grad_qkv(core_id, x, cosine, sine, parts)
-    red_qkv = scatter(keep, away, True)
-    d_x = grad_input(d_projected, wide, first_block, d_resid_one)
-    input_grad = from_sequences(d_x).astype(jnp.float32)
-
-    reduced = (red_qkv, red_out, red_gate, red_up, red_down, red_norms)
-    squares = sum(jnp.sum(grad * grad) for grad in reduced)
-    grad_norm = jnp.sqrt(sum_all(shape, squares.reshape(1))[0])
-    clip_factor = jnp.minimum(1.0, MAX_NORM / (grad_norm + 1e-06))
-    weights = (w_qkv, w_out, w_gate, w_up, w_down, norm_params)
-    firsts = (first_qkv, first_out, first_gate, first_up, first_down, first_norms)
-    seconds = (second_qkv, second_out, second_gate, second_up, second_down, second_norms)
-    updated = [
-        adam_update(
-            weight,
-            grad,
-            first,
-            second,
-            0.0 if weight is norm_params else WEIGHT_DECAY,
-            NORM_RATE if weight is norm_params else LEARN_RATE,
-            clip_factor,
-        )
-        for weight, grad, first, second in zip(weights, reduced, firsts, seconds)
-    ]
-    return (
-        output,
-        input_grad,
-        *reduced,
-        *(new for new, _, _ in updated),
-        *(new for _, new, _ in updated),
-        *(new for _, _, new in updated),
-        grad_norm,
-    )
+    d_query, d_own, d_got, reduced_sums, output = attend_back_pallas(
+        shape, query, own, sib, probs, attended, inverse_sums, d_attended, *held, result, seq_count, PLAN
+    )
+    back, qkv_sums, squares = tail(
+        shape, cosine, sine, d_query, d_own, d_got, wide, first_block, d_resid_one, x, reduced_sums, seq_count
+    )
+    states = (
+        w_qkv, w_out, w_gate, w_up, w_down, norm_params,
+        first_qkv, first_out, first_gate, first_up, first_down, first_norms,
+        second_qkv, second_out, second_gate, second_up, second_down, second_norms,
+    )
+    *updated, input_grad, grad_norm = adam(reduced_sums, qkv_sums, squares, back, states)
+    return (output, input_grad, *updated, grad_norm.reshape(()))
 
 
 def device_program(shape, *arrays):

time: 560 us -> 495 us (0.88)
  Pallas kernels: 384 us -> 434 us
  waiting for transfers between devices: 51.6 us -> 8.76 us
  starting transfers between devices: 48.5 us -> 20.1 us
  other arithmetic: 33.4 us -> 7.42 us
  between operations: 9.91 us -> 1.45 us
  local copies, waits for them, and re-layouts: 24.3 us -> 16.3 us
    pallas_call x2, Pallas kernels: 21.7 us -> 75.3 us  [the longest x1 68.7 us: tail(): pl.pallas_call(functools.partial(tail_kernel, seqs, bits, pieces), grid=(...]
    ppermute x23 -> x7, waiting for transfers between devices: 51.6 us -> 8.76 us  [send(): return lax.ppermute(array, AXES, pairs)]
    ppermute x23 -> x7, starting transfers between devices: 48.5 us -> 20.1 us  [send(): return lax.ppermute(array, AXES, pairs)]
    convert_element_type x4 -> x0, other arithmetic: 9.52 us -> none  [the longest x1 4.54 us: two_to_a_sequence(): input_grad = from_sequences(d_x).astype(jnp.float32)]
    sub x6 -> x0, other arithmetic: 6.75 us -> none  [adam_update(): return (weight - step_rate * direction, first_new, second_new)]
    reduce_sum x6 -> x0, other arithmetic: 5.77 us -> none  [two_to_a_sequence(): squares = sum((jnp.sum(grad * grad) for grad in reduced))]
    pallas_call x1, Pallas kernels: 101 us -> 95.5 us  [gather_all(): pl.pallas_call(functools.partial(gather_kernel, seqs, bits, pieces), out_...]
  transfers between devices with their start and end apart: 23 -> 7, of which waited for: 9 -> 1; matrix products, arithmetic and copies ran while one was open for 8% -> 3% of each run, Pallas kernels for 20% -> 20%
where the time goes in v3:
time: 495 us; the launch traced here: 488 us
  Pallas kernels  434 us (88%)
  starting transfers between devices  20.1 us (4%)
  local copies, waits for them, and re-layouts  16.3 us (3%)
  waiting for transfers between devices  8.76 us (2%)
  other arithmetic  7.42 us (1%)
    pallas_call x1, Pallas kernels, attend_back_pallas(): pl.pallas_call(functools.partial(attend_back_kernel, seqs, bits, pieces,...  121 us
    pallas_call x1, Pallas kernels, gather_all(): pl.pallas_call(functools.partial(gather_kernel, seqs, bits, pieces), out_...  95.5 us
    pallas_call x1, Pallas kernels, tail(): pl.pallas_call(functools.partial(tail_kernel, seqs, bits, pieces), grid=(...  68.7 us
    pallas_call x1, Pallas kernels, middle(): pl.pallas_call(middle_kernel, grid=(rows // block,), in_specs=[row(width)...  52.9 us
    pallas_call x1, Pallas kernels, attend_pallas(): pl.pallas_call(functools.partial(attend_kernel, unit, chunk), grid=(pairs...  47.2 us
    pallas_call x2, Pallas kernels, grad_wide(): pl.pallas_call(functools.partial(grad_wide_kernel, tiles), grid_spec=pltp...  20.3 us
    ppermute x7, starting transfers between devices, send(): return lax.ppermute(array, AXES, pairs)  20.1 us
    pallas_call x1, Pallas kernels, grad_tall(): pl.pallas_call(functools.partial(grad_tall_kernel, rows), grid_spec=pltpu...  10.8 us
  transfers between devices with their start and end apart: 7, of which 1 were waited for; matrix products, arithmetic and copies ran while one was open for 3% of the time, Pallas kernels for 20%

profile of v3, /device:TPU:0, one launch (start us, length us, event | category | flops | bytes accessed | tf_op | source)
XLA Modules:
  0.0 488.3 jit_solution(10153708303216587855)
XLA Ops:
  0.7 0.8 constant_dynamic-slice_fusion.1
  1.5 3.0 collective-permute-start.3
  4.5 0.8 collective-permute-start.2
  5.3 2.6 dynamic-slice_bitcast_fusion.2
  8.0 7.4 %collective-permute-start = (bf16[512,768]{1,0:T(8,128)(2,1)}, bf16[512,768]{1,0:T(8,128)(2,1)}, u32[]{:S(2)}, u32[]{:S(2)}) collective-permute-start(bf16[512,768]{1,0:T(8,128)(2,1)} %get-tuple-element.148), channel_id=1, source_target_pairs={{0,0},{1,16},{2,2},{3,18},{4,4},{5,20},{6,6},{7,22},{8,8},{9,24},{... | collective-permute-start | bytes 2359304 | tf_op jit(solution)/shard_map/ppermute | solution.py:1550
  15.5 1.9 fusion.1
  18.5 95.5 %gather_parameters.1 = (bf16[4,4,48,9472]{3,2,1,0:T(8,128)(2,1)}, bf16[4,4,192,768]{3,2,1,0:T(8,128)(2,1)S(1)}) custom-call(f32[24,3072]{1,0:T(8,128)S(1)} %copy-done.9, f32[24,3072]{1,0:T(8,128)S(1)} %copy-done.10, f32[24,2304]{1,0:T(8,128)S(1)} %copy-done.12, f32[24,768]{1,0:T(8,128)S(1)} %copy-done.13, f32[24,256]{1,0:T(8,128)S(1)} %pad.10.refs_4_, ...), custom_call_target="tpu_custom_call" | custom-call | tf_op jit(solution)/shard_map/gather_parameters/pallas_call | solution.py:580
  114.0 2.1 copy-done.6
  116.4 1.2 constant_dynamic-update-slice_fusion.1
  117.7 8.4 %project.1 = (bf16[1024,768]{1,0:T(8,128)(2,1)S(1)}, bf16[1024,1664]{1,0:T(8,128)(2,1)}) custom-call(bf16[1024,768]{1,0:T(8,128)(2,1)S(1)} %constant_dynamic-update-slice_fusion.x_ref, bf16[768,9472]{1,0:T(8,128)(2,1)} %bitcast.20, bf16[768,9472]{1,0:T(8,128)(2,1)} %bitcast.21, bf16[768,9472]{1,0:T(8,128)(2,1)} %bitcast.22, ...), custom_call_target="tpu_custom_call" | custom-call | tf_op jit(solution)/shard_map/project/pallas_call | solution.py:1229
  126.1 1.1 copy-done.3
  127.6 1.3 dynamic-slice_bitcast_fusion.1
  128.9 7.9 %collective-permute-start.5 = (bf16[512,768]{1,0:T(8,128)(2,1)}, bf16[512,768]{1,0:T(8,128)(2,1)}, u32[]{:S(2)}, u32[]{:S(2)}) collective-permute-start(bf16[512,768]{1,0:T(8,128)(2,1)} %get-tuple-element.145), channel_id=1, source_target_pairs={{0,0},{1,16},{2,2},{3,18},{4,4},{5,20},{6,6},{7,22},{8,8},{9,24},{... | collective-permute-start | bytes 2359304 | tf_op jit(solution)/shard_map/ppermute | solution.py:1550
  136.8 0.5 collective-permute-start.6
  137.3 0.9 slice_bitcast_fusion
  138.3 0.8 pad_convert_fusion
  139.1 1.7 copy.58.norms_ref
  140.8 0.9 select_convert_fusion.qc_ref
  141.7 8.7 %collective-permute-done.6 = bf16[512,768]{1,0:T(8,128)(2,1)} collective-permute-done((bf16[512,768]{1,0:T(8,128)(2,1)}, bf16[512,768]{1,0:T(8,128)(2,1)}, u32[]{:S(2)}, u32[]{:S(2)}) %collective-permute-start.6) | collective-permute-done | bytes 786464 | tf_op jit(solution)/shard_map/ppermute | solution.py:1550
  150.4 2.6 pad_maximum_fusion.cot_ref
  153.1 1.7 copy-done.15
  154.8 47.2 %attend.1 = (bf16[12,2048,1024]{2,1,0:T(8,128)(2,1)}, bf16[1024,768]{1,0:T(8,128)(2,1)}, f32[1024,768]{1,0:T(8,128)}) custom-call(bf16[1024,768]{1,0:T(8,128)(2,1)} %copy-done.3, bf16[1024,128]{1,0:T(8,128)(2,1)} %select_convert_fusion.qc_ref, bf16[1024,1664]{1,0:T(8,128)(2,1)} %get-tuple-element.88.k0.kc0.v0, ...), custom_call_target="tpu_custom_call" | custom-call | tf_op jit(solution)/shard_map/attend/pallas_call | solution.py:1298
  201.9 52.9 %middle.1 = (bf16[1024,768]{1,0:T(8,128)(2,1)}, f32[1024,768]{1,0:T(8,128)}, bf16[1024,768]{1,0:T(8,128)(2,1)}, bf16[1024,768]{1,0:T(8,128)(2,1)}, bf16[1024,768...) custom-call(bf16[1024,768]{1,0:T(8,128)(2,1)} %copy-done, ...), custom_call_target="tpu_custom_call" | custom-call | tf_op jit(solution)/shard_map/middle/pallas_call | solution.py:1383
  254.9 1.4 copy-done.8
  256.3 10.8 %grad_tall.1 = (bf16[768,5120]{1,0:T(8,128)(2,1)}, bf16[768,5120]{1,0:T(8,128)(2,1)}) custom-call(s32[1]{0:T(128)} %bitcast.10.core_ref, bf16[1024,3072]{1,0:T(8,128)(2,1)} %get-tuple-element.99.left_ref, bf16[1024,768]{1,0:T(8,128)(2,1)S(1)} %copy-done.8), custom_call_target="tpu_custom_call" | custom-call | tf_op jit(solution)/shard_map/grad_tall/pallas_call | solution.py:1488
  267.1 10.0 %grad_wide.2 = (bf16[768,5120]{1,0:T(8,128)(2,1)}, bf16[768,5120]{1,0:T(8,128)(2,1)}) custom-call(s32[1]{0:T(128)} %bitcast.10.core_ref, bf16[1024,768]{1,0:T(8,128)(2,1)S(1)} %copy-done.2, bf16[1024,3072]{1,0:T(8,128)(2,1)} %get-tuple-element.98.right_ref, ...), custom_call_target="tpu_custom_call", output_to_operand_aliasing={{0}: (3, {}), {1}: (4, {})} | custom-call | tf_op jit(solution)/shard_map/grad_wide/pallas_call | solution.py:1425
  277.1 10.3 %grad_wide.3 = (bf16[768,5120]{1,0:T(8,128)(2,1)}, bf16[768,5120]{1,0:T(8,128)(2,1)}) custom-call(s32[1]{0:T(128)} %bitcast.10.core_ref, bf16[1024,768]{1,0:T(8,128)(2,1)S(1)} %copy-done.2, bf16[1024,3072]{1,0:T(8,128)(2,1)} %get-tuple-element.97.right_ref, ...), custom_call_target="tpu_custom_call", output_to_operand_aliasing={{0}: (3, {}), {1}: (4, {})} | custom-call | tf_op jit(solution)/shard_map/grad_wide/pallas_call | solution.py:1425
  287.5 2.7 grad_out.1
  290.2 121.2 %attend_back.1 = (f32[1024,768]{1,0:T(8,128)}, f32[2,1024,768]{2,1,0:T(8,128)}, bf16[2,1024,768]{2,1,0:T(8,128)(2,1)}, f32[2,24,5120]{2,1,0:T(8,128)}, bf16[2,512,768]{2,1,0:T(8,128)(2,1)}) custom-call(bf16[1024,768]{1,0:T(8,128)(2,1)} %copy-done.3, bf16[1024,1664]{1,0:T(8,128)(2,1)} %get-tuple-element.88.k0.kc0.v0, ...), custom_call_target="tpu_custom_call" | custom-call | tf_op jit(solution)/shard_map/attend_back/pallas_call | solution.py:961
  411.4 68.7 %tail.1 = (bf16[2,512,768]{2,1,0:T(8,128)(2,1)}, f32[2,24,1152]{2,1,0:T(8,128)}, f32[8,128]{1,0:T(8,128)}) custom-call(f32[1024,128]{1,0:T(8,128)} %copy-done.5, f32[1024,128]{1,0:T(8,128)} %copy-done.4, f32[1024,768]{1,0:T(8,128)} %get-tuple-element.112.dq_ref, f32[2,1024,768]{2,1,0:T(8,128)} %get-tuple-element.113.own_ref, ...), custom_call_target="tpu_custom_call" | custom-call | tf_op jit(solution)/shard_map/tail/pallas_call | solution.py:1107
  480.1 6.6 %adam.1 = (f32[24,2304]{1,0:T(8,128)}, f32[24,768]{1,0:T(8,128)}, f32[24,3072]{1,0:T(8,128)}, f32[24,3072]{1,0:T(8,128)}, f32[96,768]{1,0:T(8,128)}, /*index=5*/...) custom-call(f32[2,24,5120]{2,1,0:T(8,128)} %get-tuple-element.111.su, ...), custom_call_target="tpu_custom_call" | custom-call | tf_op jit(solution)/shard_map/adam/pallas_call | solution.py:1187
  486.7 1.1 copy.67
  (55 shorter events, 1.9 us)
Async XLA Ops:
  1.5 114.7 %collective-permute-start.3 = (s32[512]{0:T(512)S(1)}, s32[512]{0:T(512)S(1)}, u32[]{:S(2)}, u32[]{:S(2)}) collective-permute-start(s32[512]{0:T(512)S(1)} %bitcast.34), channel_id=1, source_target_pairs={{0,8},{1,24},{2,10},{3,26},{4,12},{5,28},{6,14},{7,30},{8,0},{9,16... | collective-permute-start | bytes 6152 | tf_op jit(solution)/shard_map/ppermute | solution.py:1550
  4.5 13.9 %copy-start.18 = (f32[4,24]{1,0:T(4,128)S(1)}, f32[4,24]{1,0:T(4,128)}, u32[]{:S(2)}) copy-start(f32[4,24]{1,0:T(4,128)} %refs_5_.3) | copy-start | bytes 1156
  4.5 14.0 %copy-start.9 = (f32[24,3072]{1,0:T(8,128)S(1)}, f32[24,3072]{1,0:T(8,128)}, u32[]{:S(2)}) copy-start(f32[24,3072]{1,0:T(8,128)} %refs_2_.3) | copy-start | bytes 884740
  4.5 14.0 %copy-start.10 = (f32[24,3072]{1,0:T(8,128)S(1)}, f32[24,3072]{1,0:T(8,128)}, u32[]{:S(2)}) copy-start(f32[24,3072]{1,0:T(8,128)} %refs_3_.3) | copy-start | bytes 884740
  4.5 14.0 %copy-start.11 = (f32[96,768]{1,0:T(8,128)S(1)}, f32[96,768]{1,0:T(8,128)}, u32[]{:S(2)}) copy-start(f32[96,768]{1,0:T(8,128)} %refs_4_.1) | copy-start | bytes 884740
  4.5 14.0 %copy-start.12 = (f32[24,2304]{1,0:T(8,128)S(1)}, f32[24,2304]{1,0:T(8,128)}, u32[]{:S(2)}) copy-start(f32[24,2304]{1,0:T(8,128)} %refs_0_.3) | copy-start | bytes 663556
  4.5 14.0 %copy-start.13 = (f32[24,768]{1,0:T(8,128)S(1)}, f32[24,768]{1,0:T(8,128)}, u32[]{:S(2)}) copy-start(f32[24,768]{1,0:T(8,128)} %refs_1_.3) | copy-start | bytes 221188
  4.5 111.7 %collective-permute-start.2 = (s32[512]{0:T(512)S(1)}, s32[512]{0:T(512)S(1)}, u32[]{:S(2)}, u32[]{:S(2)}) collective-permute-start(s32[512]{0:T(512)S(1)} %bitcast.33), channel_id=1, source_target_pairs={{0,0},{1,16},{2,2},{3,18},{4,4},{5,20},{6,6},{7,22},{8,8},{9,24},{... | collective-permute-start | bytes 6152 | tf_op jit(solution)/shard_map/ppermute | solution.py:1550
  8.0 109.7 %collective-permute-start.1 = (bf16[512,768]{1,0:T(8,128)(2,1)}, bf16[512,768]{1,0:T(8,128)(2,1)S(1)}, u32[]{:S(2)}, u32[]{:S(2)}) collective-permute-start(bf16[512,768]{1,0:T(8,128)(2,1)} %get-tuple-element.147), channel_id=1, source_target_pairs={{0,8},{1,24},{2,10},{3,26},{4,12},{5,28},{6,14},{7,30},{8,0},{9,16... | collective-permute-start | bytes 2359304 | tf_op jit(solution)/shard_map/ppermute | solution.py:1550
  8.0 108.4 %collective-permute-start = (bf16[512,768]{1,0:T(8,128)(2,1)}, bf16[512,768]{1,0:T(8,128)(2,1)}, u32[]{:S(2)}, u32[]{:S(2)}) collective-permute-start(bf16[512,768]{1,0:T(8,128)(2,1)} %get-tuple-element.148), channel_id=1, source_target_pairs={{0,0},{1,16},{2,2},{3,18},{4,4},{5,20},{6,6},{7,22},{8,8},{9,24},{... | collective-permute-start | bytes 2359304 | tf_op jit(solution)/shard_map/ppermute | solution.py:1550
  17.8 108.3 %copy-start.5 = (f32[1024,128]{1,0:T(8,128)}, f32[1024,128]{1,0:T(8,128)S(1)}, u32[]{:S(2)}) copy-start(f32[1024,128]{1,0:T(8,128)S(1)} %pad_maximum_fusion.1.cos_ref) | copy-start | bytes 1572868
  18.3 107.8 %copy-start.4 = (f32[1024,128]{1,0:T(8,128)}, f32[1024,128]{1,0:T(8,128)S(1)}, u32[]{:S(2)}) copy-start(f32[1024,128]{1,0:T(8,128)S(1)} %pad_maximum_fusion.2.sin_ref) | copy-start | bytes 1572868
  114.0 2.2 copy-start.6
  117.7 8.4 %copy-start = (bf16[1024,768]{1,0:T(8,128)(2,1)}, bf16[1024,768]{1,0:T(8,128)(2,1)S(1)}, u32[]{:S(2)}) copy-start(bf16[1024,768]{1,0:T(8,128)(2,1)S(1)} %constant_dynamic-update-slice_fusion.x_ref) | copy-start | bytes 4718596
  117.7 9.9 %copy-start.16 = (bf16[2,512,768]{2,1,0:T(8,128)(2,1)S(1)}, bf16[2,512,768]{2,1,0:T(8,128)(2,1)}, u32[]{:S(2)}) copy-start(bf16[2,512,768]{2,1,0:T(8,128)(2,1)} %param.23) | copy-start | bytes 4718596
  126.1 1.1 copy-start.3
  127.3 25.8 %collective-permute-start.4 = (bf16[1024,1664]{1,0:T(8,128)(2,1)}, bf16[1024,1664]{1,0:T(8,128)(2,1)S(1)}, u32[]{:S(2)}, u32[]{:S(2)}) collective-permute-start(bf16[1024,1664]{1,0:T(8,128)(2,1)} %get-tuple-element.88.k0.kc0.v0), channel_id=1, source_target_pairs={{0,1},{1,0},{2,3},{3,2},{4,5},{5,4},{6,7},{7,6},{8,9},{9,8},{10,11... | collective-permute-start | bytes 10223624 | tf_op jit(solution)/shard_map/ppermute | solution.py:1550
  128.9 12.8 %collective-permute-start.5 = (bf16[512,768]{1,0:T(8,128)(2,1)}, bf16[512,768]{1,0:T(8,128)(2,1)}, u32[]{:S(2)}, u32[]{:S(2)}) collective-permute-start(bf16[512,768]{1,0:T(8,128)(2,1)} %get-tuple-element.145), channel_id=1, source_target_pairs={{0,0},{1,16},{2,2},{3,18},{4,4},{5,20},{6,6},{7,22},{8,8},{9,24},{... | collective-permute-start | bytes 2359304 | tf_op jit(solution)/shard_map/ppermute | solution.py:1550
  136.8 13.6 %collective-permute-start.6 = (bf16[512,768]{1,0:T(8,128)(2,1)}, bf16[512,768]{1,0:T(8,128)(2,1)}, u32[]{:S(2)}, u32[]{:S(2)}) collective-permute-start(bf16[512,768]{1,0:T(8,128)(2,1)} %get-tuple-element.146), channel_id=1, source_target_pairs={{0,8},{1,24},{2,10},{3,26},{4,12},{5,28},{6,14},{7,30},{8,0},{9,16... | collective-permute-start | bytes 2359304 | tf_op jit(solution)/shard_map/ppermute | solution.py:1550
  153.1 1.7 copy-start.15
  254.9 1.4 copy-start.8
  256.3 10.8 %copy-start.2 = (bf16[1024,768]{1,0:T(8,128)(2,1)S(1)}, bf16[1024,768]{1,0:T(8,128)(2,1)}, u32[]{:S(2)}) copy-start(bf16[1024,768]{1,0:T(8,128)(2,1)} %get-tuple-element.96.left_ref) | copy-start | bytes 4718596
  277.1 10.4 %copy-start.1 = (bf16[1024,768]{1,0:T(8,128)(2,1)S(1)}, bf16[1024,768]{1,0:T(8,128)(2,1)}, u32[]{:S(2)}) copy-start(bf16[1024,768]{1,0:T(8,128)(2,1)} %get-tuple-element.90.att_ref.left_ref.o_ref) | copy-start | bytes 4718596
  277.1 10.4 %copy-start.7 = (bf16[1024,768]{1,0:T(8,128)(2,1)S(1)}, bf16[1024,768]{1,0:T(8,128)(2,1)}, u32[]{:S(2)}) copy-start(bf16[1024,768]{1,0:T(8,128)(2,1)} %get-tuple-element.94.right_ref) | copy-start | bytes 4718596
  277.1 10.4 %copy-start.14 = (f32[8,768]{1,0:T(8,128)S(1)}, f32[8,768]{1,0:T(8,128)}, u32[]{:S(2)}) copy-start(f32[8,768]{1,0:T(8,128)} %get-tuple-element.95.sums_ref) | copy-start | bytes 73732
  480.1 6.7 %copy-start.17 = (bf16[2,512,768]{2,1,0:T(8,128)(2,1)S(1)}, bf16[2,512,768]{2,1,0:T(8,128)(2,1)}, u32[]{:S(2)}) copy-start(bf16[2,512,768]{2,1,0:T(8,128)(2,1)} %get-tuple-element.183) | copy-start | bytes 4718596

commit v4 on v3

--- a/solution.py
+++ b/solution.py
@@ -375,236 +375,6 @@
     return lax.dot_general(left, right, dims, preferred_element_type=jnp.float32)
 
 
-def gather_kernel(seqs, bits, pieces, *refs):
-    gate, up, qkv, out, norm, down = refs[:6]
-    wide_all, down_all = refs[6:8]
-    wide_two, down_two, wide_chip, down_chip = refs[8:12]
-    core_send, core_recv, own_sem, line_send, line_recv, hop_send, hop_recv, swap_send, swap_recv = refs[12:]
-    z = lax.axis_index("seq")
-    f = lax.axis_index("fsdp")
-    core = lax.rem(f, 2)
-    chip = lax.div(f, 2)
-    sibling = {"fsdp": f + 1 - 2 * core}
-
-    def chip_at(mask):
-        at = chip
-        for b in range(bits):
-            if mask & (1 << b):
-                at = at + (1 - 2 * lax.rem(lax.div(chip, 1 << b), 2)) * (1 << b)
-        return at
-
-    def partner(b):
-        return {"fsdp": 2 * chip_at(1 << b) + core}
-
-    barrier = pltpu.get_barrier_semaphore()
-    pl.semaphore_signal(barrier, inc=1, device_id=sibling, device_id_type=MESH_ID)
-    for b in range(bits):
-        pl.semaphore_signal(barrier, inc=1, device_id=partner(b), device_id_type=MESH_ID)
-
-    for way in (1, seqs - 1):
-        pl.semaphore_signal(barrier, inc=1, device_id={"seq": lax.rem(z + way, seqs)}, device_id_type=MESH_ID)
-    rows = gate.shape[0]
-    at = 0
-    for part in (gate, up, qkv, out, norm):
-        wide_two[core, :, at : at + part.shape[1]] = part[...]
-        at += part.shape[1]
-    down_two[core] = down[...]
-    pl.semaphore_wait(barrier, 3 + bits)
-
-    first = [
-        pltpu.make_async_remote_copy(
-            two.at[core], two.at[core], core_send.at[i], core_recv.at[i], device_id=sibling, device_id_type=MESH_ID
-        )
-        for i, two in enumerate((wide_two, down_two))
-    ]
-    for copy in first:
-        copy.start()
-    for copy in first:
-        copy.wait()
-    wide_chip[...] = wide_two[...].reshape(wide_chip.shape).astype(jnp.bfloat16)
-    down_chip[...] = down_two[...].reshape(down_chip.shape).astype(jnp.bfloat16)
-    own = [
-        pltpu.make_async_copy(wide_chip, wide_all.at[z, chip], own_sem.at[0]),
-        pltpu.make_async_copy(down_chip, down_all.at[z, chip], own_sem.at[1]),
-    ]
-    for copy in own:
-        copy.start()
-
-    def columns(p):
-        source, offset, width, _ = pieces[p]
-        half = (down_all if source else wide_all).shape[-1] // 2
-        return pl.ds(pl.multiple_of(core * half + offset, 128), width)
-
-    def block(p, zz, mask):
-        return (down_all if pieces[p][0] else wide_all).at[zz, chip_at(mask), :, columns(p)]
-
-    def own_block(p):
-        return (down_chip if pieces[p][0] else wide_chip).at[:, columns(p)]
-
-    def line_copy(p, zz, way, mine):
-        return pltpu.make_async_remote_copy(
-            own_block(p) if mine else block(p, zz, 0),
-            block(p, zz, 0),
-            line_send.at[p, way, zz],
-            line_recv.at[p, zz],
-            device_id={"seq": z + (1 if way else -1)},
-            device_id_type=MESH_ID,
-        )
-
-    def hop_copy(p, zz, mask, b, mine):
-        return pltpu.make_async_remote_copy(
-            own_block(p) if mine else block(p, zz, mask),
-            block(p, zz, mask),
-            hop_send.at[p, zz, mask | (1 << b)],
-            hop_recv.at[p, zz, mask | (1 << b)],
-            device_id=partner(b),
-            device_id_type=MESH_ID,
-        )
-
-    def swap_copy(p, zz, mask):
-        return pltpu.make_async_remote_copy(
-            block(p, zz, mask),
-            block(p, zz, mask),
-            swap_send.at[p, zz, mask],
-            swap_recv.at[p, zz, mask],
-            device_id=sibling,
-            device_id_type=MESH_ID,
-        )
-
-    def level(p, mask):
-        return max([i for i, b in enumerate(pieces[p][3]) if mask & (1 << b)], default=-1)
-
-    def masks(p):
-        return sorted(range(1 << bits), key=lambda mask: (level(p, mask), mask))
-
-    def pass_on(p, zz, mask, mine=False):
-        for b in pieces[p][3][level(p, mask) + 1 :]:
-            hop_copy(p, zz, mask, b, mine).start()
-        if not mine:
-            swap_copy(p, zz, mask).start()
-
-    def arrived(p, zz, mask):
-        b = pieces[p][3][level(p, mask)]
-        hop_copy(p, zz, mask & ~(1 << b), b, False).wait_recv()
-
-    count = len(pieces)
-    for p in range(count):
-
-        @pl.when(z > 0)
-        def _():
-            line_copy(p, z, 0, True).start()
-
-        @pl.when(z < seqs - 1)
-        def _():
-            line_copy(p, z, 1, True).start()
-
-        pass_on(p, z, 0, True)
-
-    def hops(zz):
-        for level_at in range(bits):
-            for p in range(count):
-                for mask in masks(p):
-                    if level(p, mask) == level_at:
-                        arrived(p, zz, mask)
-                        pass_on(p, zz, mask)
-
-    for distance in range(1, seqs):
-        for way in (1, 0):
-            zz = z - distance if way else z + distance
-
-            @pl.when((zz >= 0) & (zz < seqs))
-            def _():
-                for p in range(count):
-                    line_copy(p, zz, way, False).wait_recv()
-
-                    @pl.when((z < seqs - 1) if way else (z > 0))
-                    def _():
-                        line_copy(p, zz, way, False).start()
-
-                    pass_on(p, zz, 0)
-
-        for way in (1, 0):
-            zz = z - distance + 1 if way else z + distance - 1
-            if distance > 1 or way:
-
-                @pl.when((zz >= 0) & (zz < seqs))
-                def _():
-                    hops(zz)
-
-    for way in (1, 0):
-        zz = z - seqs + 1 if way else z + seqs - 1
-
-        @pl.when((zz >= 0) & (zz < seqs))
-        def _():
-            hops(zz)
-
-    def finish(zz):
-        for p in range(count):
-
-            @pl.when((zz <= z) & (z < seqs - 1))
-            def _():
-                line_copy(p, zz, 1, False).wait_send()
-
-            @pl.when((zz >= z) & (z > 0))
-            def _():
-                line_copy(p, zz, 0, False).wait_send()
-
-            for mask in masks(p):
-                for b in pieces[p][3][level(p, mask) + 1 :]:
-                    hop_copy(p, zz, mask, b, False).wait_send()
-                if mask:
-                    swap_copy(p, zz, mask).wait()
-
-            @pl.when(zz != z)
-            def _():
-                swap_copy(p, zz, 0).wait()
-
-    lax.fori_loop(0, seqs, lambda zz, _: (finish(zz), 0)[1], 0)
-    for copy in own:
-        copy.wait()
-
-
-def gather_all(mesh_shape, gate, up, qkv, out, norm, down):
-    seqs, chips = mesh_shape["seq"], mesh_shape["fsdp"] // 2
-    bits = chips.bit_length() - 1
-    rows, rows_down = gate.shape[0], down.shape[0]
-    wide = sum(part.shape[1] for part in (gate, up, qkv, out, norm))
-    upward, downward = tuple(range(bits)), tuple(reversed(range(bits)))
-    down_load = down.shape[1] // 2 * rows_down // rows
-    cut = max(0, (wide // 2 + down_load) // 2 - down_load) // 128 * 128 + 128
-    pieces = ((0, 0, cut, upward), (1, 0, down.shape[1] // 2, upward), (0, cut, wide // 2 - cut, downward))
-    count = len(pieces)
-    dma = pltpu.SemaphoreType.DMA
-    any_space = pl.BlockSpec(memory_space=pl.ANY)
-    vmem = pl.BlockSpec(memory_space=pltpu.VMEM)
-    return pl.pallas_call(
-        functools.partial(gather_kernel, seqs, bits, pieces),
-        out_shape=[
-            jax.ShapeDtypeStruct((seqs, chips, 2 * rows, wide), jnp.bfloat16),
-            jax.ShapeDtypeStruct((seqs, chips, 2 * rows_down, down.shape[1]), jnp.bfloat16),
-        ],
-        in_specs=[vmem] * 6,
-        out_specs=[any_space] * 2,
-        scratch_shapes=[
-            pltpu.VMEM((2, rows, wide), jnp.float32),
-            pltpu.VMEM((2, rows_down, down.shape[1]), jnp.float32),
-            pltpu.VMEM((2 * rows, wide), jnp.bfloat16),
-            pltpu.VMEM((2 * rows_down, down.shape[1]), jnp.bfloat16),
-            dma((2,)),
-            dma((2,)),
-            dma((2,)),
-            dma((count, 2, seqs)),
-            dma((count, seqs)),
-            dma((count, seqs, chips)),
-            dma((count, seqs, chips)),
-            dma((count, seqs, chips)),
-            dma((count, seqs, chips)),
-        ],
-        compiler_params=pltpu.CompilerParams(collective_id=0, has_side_effects=True, vmem_limit_bytes=48 << 20),
-        name="gather_parameters",
-    )(gate, up, qkv, out, norm, down)
-
-
 def place():
     f = lax.axis_index("fsdp")
     return lax.axis_index("seq"), lax.div(f, 2), lax.rem(f, 2)
@@ -639,6 +409,61 @@
 def sum_peers(bits):
     z, chip, core = place()
     return [{"fsdp": 2 * chip + 1 - core}] + [{"fsdp": 2 * chip_at(chip, 1 << b) + core} for b in range(bits)]
+
+
+def departs(seqs, seq_count, source, target, sems, subs=1):
+    z, chip, core = place()
+    group = seqs // seq_count
+
+    def copies(s, sub):
+        at = (core * seq_count + s) * group + lax.div(z, seq_count)
+        to_z, to_core = lax.div(at, 2), lax.rem(at, 2)
+        n = lax.rem(z, seq_count) * subs + sub
+        remote = pltpu.make_async_remote_copy(
+            source(s, sub), target(n), sems.at[0, s * subs + sub], sems.at[1, n],
+            device_id={"seq": to_z, "fsdp": 2 * chip + to_core}, device_id_type=MESH_ID,
+        )
+        return (to_z == z) & (to_core == core), remote, pltpu.make_async_copy(source(s, sub), target(n), sems.at[2, n])
+
+    def begin():
+        for sub in range(subs):
+            for s in range(seq_count):
+                mine, remote, local = copies(s, sub)
+
+                @pl.when(mine)
+                def _():
+                    local.start()
+
+                @pl.when(jnp.logical_not(mine))
+                def _():
+                    remote.start()
+
+    def came(n):
+        at = z * 2 + core
+        from_z = lax.rem(at, group) * seq_count + lax.div(n, subs)
+        mine = (from_z == z) & (lax.div(lax.div(at, group), seq_count) == core)
+
+        @pl.when(mine)
+        def _():
+            pltpu.make_async_copy(source(0, 0), target(n), sems.at[2, n]).wait()
+
+        @pl.when(jnp.logical_not(mine))
+        def _():
+            pltpu.make_async_remote_copy(
+                source(0, 0), target(n), sems.at[0, 0], sems.at[1, n],
+                device_id={"seq": z, "fsdp": 2 * chip + 1 - core}, device_id_type=MESH_ID,
+            ).wait_recv()
+
+    def sent():
+        for sub in range(subs):
+            for s in range(seq_count):
+                mine, remote, _ = copies(s, sub)
+
+                @pl.when(jnp.logical_not(mine))
+                def _():
+                    remote.wait_send()
+
+    return begin, came, sent
 
 
 def returns(seqs, seq_count, source, target, sems, rows):
@@ -653,7 +478,7 @@
 
     def copies(n):
         t, sub = divmod(n, subs)
-        to_z = lax.rem(at, group) * seq_count + lax.rem(slot - t + seq_count, seq_count)
+        to_z = lax.rem(at, group) * seq_count + t
         mine = (to_z == z) & (to_core == core)
         here = target.at[slot, pl.ds(sub * rows, rows)]
         remote = pltpu.make_async_remote_copy(
@@ -699,6 +524,256 @@
                     ).wait_recv()
 
     return begin, end
+
+
+def line_peers(seqs):
+    z = lax.axis_index("seq")
+    return [{"seq": lax.rem(z + way, seqs)} for way in (1, seqs - 1)]
+
+
+def gatherer_scratch(seqs, bits, count):
+    dma = pltpu.SemaphoreType.DMA
+    chips = 1 << bits
+    return [
+        dma((count, 2, seqs)),
+        dma((count, seqs)),
+        dma((count, seqs, chips)),
+        dma((count, seqs, chips)),
+        dma((count, seqs, chips)),
+        dma((count, seqs, chips)),
+    ]
+
+
+def gatherer(seqs, bits, pieces, wholes, line_send, line_recv, hop_send, hop_recv, swap_send, swap_recv):
+    z, chip, core = place()
+
+    def block(p, zz, mask):
+        which, offset, width, _ = pieces[p]
+        half = wholes[which].shape[-1] // 2
+        return wholes[which].at[zz, chip_at(chip, mask), :, pl.ds(pl.multiple_of(core * half + offset, 128), width)]
+
+    def line_copy(p, zz, way):
+        return pltpu.make_async_remote_copy(
+            block(p, zz, 0), block(p, zz, 0), line_send.at[p, way, zz], line_recv.at[p, zz],
+            device_id={"seq": z + (1 if way else -1)}, device_id_type=MESH_ID,
+        )
+
+    def hop_copy(p, zz, mask, b):
+        to = mask | (1 << b)
+        return pltpu.make_async_remote_copy(
+            block(p, zz, mask), block(p, zz, mask), hop_send.at[p, zz, to], hop_recv.at[p, zz, to],
+            device_id={"fsdp": 2 * chip_at(chip, 1 << b) + core}, device_id_type=MESH_ID,
+        )
+
+    def swap_copy(p, zz, mask):
+        return pltpu.make_async_remote_copy(
+            block(p, zz, mask), block(p, zz, mask), swap_send.at[p, zz, mask], swap_recv.at[p, zz, mask],
+            device_id={"fsdp": 2 * chip + 1 - core}, device_id_type=MESH_ID,
+        )
+
+    def level(p, mask):
+        return max([i for i, b in enumerate(pieces[p][3]) if mask & (1 << b)], default=-1)
+
+    def later(p, mask):
+        return pieces[p][3][level(p, mask) + 1 :]
+
+    masks = range(1 << bits)
+
+    def pass_on(p, zz, mask, mine=False):
+        for b in later(p, mask):
+            hop_copy(p, zz, mask, b).start()
+        if not mine:
+            swap_copy(p, zz, mask).start()
+
+    def own_line(which):
+        for p in which:
+
+            @pl.when(z > 0)
+            def _():
+                line_copy(p, z, 0).start()
+
+            @pl.when(z < seqs - 1)
+            def _():
+                line_copy(p, z, 1).start()
+
+    def own_hops(which):
+        for p in which:
+            pass_on(p, z, 0, True)
+
+    def both(distance, task):
+        for way in (1, 0) if distance else (1,):
+            zz = z - distance if way else z + distance
+            pl.when((zz >= 0) & (zz < seqs))(functools.partial(task, zz, way))
+
+    def line(which, distance):
+        def task(zz, way):
+            for p in which:
+                line_copy(p, zz, way).wait_recv()
+
+                @pl.when((z < seqs - 1) if way else (z > 0))
+                def _():
+                    line_copy(p, zz, way).start()
+
+                pass_on(p, zz, 0)
+
+        both(distance, task)
+
+    def hops(which, distance, levels=range(bits)):
+        def task(zz, way):
+            for at in levels:
+                for p in which:
+                    for mask in masks:
+                        if level(p, mask) == at:
+                            b = pieces[p][3][at]
+                            hop_copy(p, zz, mask & ~(1 << b), b).wait_recv()
+                            pass_on(p, zz, mask)
+
+        both(distance, task)
+
+    def finish_line(which):
+        def task(zz, _):
+            for p in which:
+
+                @pl.when((zz <= z) & (z < seqs - 1))
+                def _():
+                    line_copy(p, zz, 1).wait_send()
+
+                @pl.when((zz >= z) & (z > 0))
+                def _():
+                    line_copy(p, zz, 0).wait_send()
+
+            return 0
+
+        lax.fori_loop(0, seqs, task, 0)
+
+    def finish_hops(which, distance):
+        def task(zz, _):
+            for p in which:
+                for mask in masks:
+                    for b in later(p, mask):
+                        hop_copy(p, zz, mask, b).wait_send()
+                    if mask or distance:
+                        swap_copy(p, zz, mask).wait()
+
+        both(distance, task)
+
+    return own_line, own_hops, line, hops, finish_line, finish_hops
+
+
+def first_gather_kernel(seqs, bits, pieces, early, *refs):
+    tokens, segments, gate, up, qkv, out, norm, down = refs[:8]
+    x_out, segments_out, qkv_all, rest_all, down_all = refs[8:13]
+    qkv_two, rest_two, down_two, qkv_chip, rest_chip, down_chip, core_sem, own_sem, token_sem, segment_sem = refs[13:23]
+    z, chip, core = place()
+    wholes = (qkv_all, rest_all, down_all)
+    chips = (qkv_chip, rest_chip, down_chip)
+    own_line, own_hops, line, hops, finish_line, finish_hops = gatherer(seqs, bits, pieces, wholes, *refs[23:])
+    seq_count = tokens.shape[0]
+    token_begin, token_came, token_sent = departs(
+        seqs, seq_count, lambda s, _: tokens.at[s], lambda n: x_out.at[n], token_sem
+    )
+    segment_begin, segment_came, segment_sent = departs(
+        seqs, seq_count, lambda s, _: segments.at[s], lambda n: segments_out.at[n], segment_sem
+    )
+    greet(sum_peers(bits) + column_peers(seqs))
+    segment_begin()
+    at = 0
+    for part in (gate, up, out, norm):
+        rest_two[core, :, at : at + part.shape[1]] = part[...]
+        at += part.shape[1]
+    qkv_two[core] = qkv[...]
+    down_two[core] = down[...]
+    twos = (qkv_two, rest_two, down_two)
+    first = [
+        pltpu.make_async_remote_copy(
+            two.at[core], two.at[core], core_sem.at[0, i], core_sem.at[1, i],
+            device_id={"fsdp": 2 * chip + 1 - core}, device_id_type=MESH_ID,
+        )
+        for i, two in enumerate(twos)
+    ]
+    for copy in first:
+        copy.start()
+    own = [
+        pltpu.make_async_copy(chip_ref, whole.at[z, chip], own_sem.at[i])
+        for i, (chip_ref, whole) in enumerate(zip(chips, wholes))
+    ]
+    for i, copy in enumerate(first):
+        copy.wait()
+        chips[i][...] = twos[i][...].reshape(chips[i].shape).astype(jnp.bfloat16)
+        own[i].start()
+    rest = [p for p in range(len(pieces)) if p not in early]
+    own[0].wait()
+    own_line(early)
+    own_hops(early)
+    own[1].wait()
+    own[2].wait()
+    own_hops(rest)
+    for distance in range(1, seqs):
+        line(early, distance)
+        if distance == seqs - 2:
+            token_begin()
+        hops(early, distance - 1)
+    hops(rest, 0)
+    hops(early, seqs - 1)
+    finish_line(early)
+    for distance in range(seqs):
+        finish_hops(early, distance)
+    finish_hops(rest, 0)
+    for n in range(seq_count):
+        token_came(n)
+        segment_came(n)
+    token_sent()
+    segment_sent()
+
+
+def gather_pieces(bits, qkv, rest, down, rows):
+    upward, downward = tuple(range(bits)), tuple(reversed(range(bits)))
+    cut = qkv // 512 * 128
+    load = down.shape[1] // 2 * down.shape[0] // rows
+    other = max(128, ((rest // 2 + load) // 2 - load) // 128 * 128)
+    return (
+        (0, 0, cut, upward),
+        (0, cut, qkv // 2 - cut, downward),
+        (1, 0, other, upward),
+        (2, 0, down.shape[1] // 2, upward),
+        (1, other, rest // 2 - other, downward),
+    )
+
+
+def first_gather(shape, tokens, segments, gate, up, qkv, out, norm, down):
+    seqs, chips = shape["seq"], shape["fsdp"] // 2
+    bits = chips.bit_length() - 1
+    rows, rows_down = gate.shape[0], down.shape[0]
+    rest = sum(part.shape[1] for part in (gate, up, out, norm))
+    pieces = gather_pieces(bits, qkv.shape[1], rest, down, rows)
+    seq_count = tokens.shape[0]
+    dma = pltpu.SemaphoreType.DMA
+    low = jnp.bfloat16
+    any_space = pl.BlockSpec(memory_space=pl.ANY)
+    vmem = pl.BlockSpec(memory_space=pltpu.VMEM)
+    forms = ((rows, qkv.shape[1]), (rows, rest), (rows_down, down.shape[1]))
+    *outs, = pl.pallas_call(
+        functools.partial(first_gather_kernel, seqs, bits, pieces, (0, 1)),
+        out_shape=[
+            jax.ShapeDtypeStruct(tokens.shape, low),
+            jax.ShapeDtypeStruct(segments.shape, jnp.int32),
+            *(jax.ShapeDtypeStruct((seqs, chips, 2 * n, cols), low) for n, cols in forms),
+        ],
+        in_specs=[any_space, any_space, *[vmem] * 6],
+        out_specs=[any_space] * 5,
+        scratch_shapes=[
+            *(pltpu.VMEM((2, *form), jnp.float32) for form in forms),
+            *(pltpu.VMEM((2 * n, cols), low) for n, cols in forms),
+            dma((2, 3)),
+            dma((3,)),
+            dma((3, seq_count)),
+            dma((3, seq_count)),
+            *gatherer_scratch(seqs, bits, len(pieces)),
+        ],
+        compiler_params=pltpu.CompilerParams(collective_id=0, has_side_effects=True, vmem_limit_bytes=48 << 20),
+        name="first_gather",
+    )(tokens, segments, gate, up, qkv, out, norm, down)
+    return outs, pieces[2:]
 
 
 def hop_masks(order, stage):
@@ -953,8 +1028,8 @@
     pieces = halves_of(sum_cols, bits)
     row = pl.BlockSpec((unit, 128), lambda j, i: (i, j))
     kv = [
-        pl.BlockSpec((part, 128), lambda j, i: (0, j)),
-        pl.BlockSpec((part, 128), lambda j, i: (0, j + pairs)),
+        pl.BlockSpec((part, 128), lambda j, i: (0, 2 * j)),
+        pl.BlockSpec((part, 128), lambda j, i: (0, 2 * j + 1)),
     ]
     any_space = pl.BlockSpec(memory_space=pl.ANY)
     dma = pltpu.SemaphoreType.DMA
@@ -1217,8 +1292,11 @@
     width = x.shape[-1]
     query = turn(dotf(x, wq_ref[...]), cosine, sine).astype(jnp.bfloat16)
     q_ref[...] = query * jnp.bfloat16(1.0 / math.sqrt(HEAD_DIM))
-    kv_ref[:, :width] = turn(dotf(x, wk_ref[...]), cosine, sine).astype(jnp.bfloat16)
-    kv_ref[:, width : 2 * width] = dotf(x, wv_ref[...]).astype(jnp.bfloat16)
+    keys = turn(dotf(x, wk_ref[...]), cosine, sine).astype(jnp.bfloat16)
+    values = dotf(x, wv_ref[...]).astype(jnp.bfloat16)
+    for at in range(0, width, 128):
+        kv_ref[:, 2 * at : 2 * at + 128] = keys[:, at : at + 128]
+        kv_ref[:, 2 * at + 128 : 2 * at + 256] = values[:, at : at + 128]
     kv_ref[:, 2 * width :] = code_ref[...]
 
 
@@ -1240,19 +1318,72 @@
     )(x, wide, wide, wide, cosine, sine, code)
 
 
-def attend_kernel(unit, chunk, q_ref, qc_ref, k0, kc0, v0, k1, kc1, v1, p_ref, o_ref, inv_ref, ka, vt, st_ref):
-    part = k0.shape[0]
+def attend_kernel(seqs, bits, pieces, plan, unit, chunk, q_ref, qc_ref, own_ref, code_ref, own_hbm, *refs):
+    p_ref, o_ref, inv_ref, sib_hbm, rest_all, down_all = refs[2:8]
+    ka, vt, st_ref, sib, kv_sem, keep_sem = refs[8:14]
+    own_line, own_hops, line, hops, finish_line, finish_hops = gatherer(
+        seqs, bits, pieces, (None, rest_all, down_all), *refs[14:]
+    )
+    z, chip, core = place()
+    part, rows = own_ref.shape[0], q_ref.shape[0]
     keys = 2 * part
-    rows = q_ref.shape[0]
+    j, pairs = pl.program_id(0), pl.num_programs(0)
+    step = j * pl.num_programs(1) + pl.program_id(1)
+    which = range(len(pieces))
+
+    def kv_copy(first, count, n):
+        cols = pl.ds(pl.multiple_of(first, 128), count)
+        return pltpu.make_async_remote_copy(
+            own_hbm.at[:, cols], sib.at[:, cols], kv_sem.at[0, n], kv_sem.at[1, n],
+            device_id={"fsdp": 2 * chip + 1 - core}, device_id_type=MESH_ID,
+        )
+
+    code_copy = kv_copy(256 * pairs, 128, pairs)
+    pair_copy = lambda n: kv_copy(256 * n, 256, n)
+
+    def carry(distance, level=None):
+        if level is None:
+            line(which, distance)
+        else:
+            hops(which, distance, (level,))
+
+    @pl.when(step == 0)
+    def _():
+        greet(sum_peers(bits) + line_peers(seqs))
+        code_copy.start()
+        pair_copy(0).start()
+        own_line(which)
+        lax.fori_loop(1, pairs, lambda n, _: (pair_copy(n).start(), 0)[1], 0)
+        code_copy.wait_recv()
+
+    for at in [at for at in plan if at is not None]:
+
+        @pl.when(step == at)
+        def _():
+            for task in plan[at]:
+                carry(*task)
+
     low_k = lax.broadcasted_iota(jnp.int32, (part, 128), 1) < HEAD_DIM
-    for i, (k_ref, kc_ref, v_ref) in enumerate(((k0, kc0, v0), (k1, kc1, v1))):
-        k, kc, v = k_ref[...], kc_ref[...], v_ref[...]
-        one = jnp.ones_like(v)
-        here = slice(i * part, (i + 1) * part)
-        ka[0, here] = jnp.where(low_k, k, kc)
-        ka[1, here] = jnp.where(low_k, kc, k)
-        vt[0, :, here] = jnp.where(low_k, v, one).T
-        vt[1, :, here] = jnp.where(low_k, one, v).T
+
+    @pl.when(pl.program_id(1) == 0)
+    def _():
+        pair_copy(j).wait_recv()
+        sides = (
+            (own_ref[:, :128], code_ref[...], own_ref[:, 128:]),
+            (
+                sib[:, pl.ds(pl.multiple_of(256 * j, 128), 128)],
+                sib[:, sib.shape[1] - 128 :],
+                sib[:, pl.ds(pl.multiple_of(256 * j + 128, 128), 128)],
+            ),
+        )
+        for i, (k, kc, v) in enumerate(sides):
+            one = jnp.ones_like(v)
+            here = slice(i * part, (i + 1) * part)
+            ka[0, here] = jnp.where(low_k, k, kc)
+            ka[1, here] = jnp.where(low_k, kc, k)
+            vt[0, :, here] = jnp.where(low_k, v, one).T
+            vt[1, :, here] = jnp.where(low_k, one, v).T
+
     low_q = lax.broadcasted_iota(jnp.int32, (unit, 128), 1) < HEAD_DIM
     units = [(h, b) for b in range(rows // unit) for h in range(2)]
     results, before = {}, None
@@ -1284,35 +1415,65 @@
         inv_ref[b * unit : (b + 1) * unit] = inv
         o_ref[b * unit : (b + 1) * unit] = (jnp.where(low_q, r0, r1) * inv).astype(jnp.bfloat16)
 
-
-def attend_pallas(q, qc, own, sib, unit=512, chunk=512):
+    @pl.when(step == pairs * pl.num_programs(1) - 1)
+    def _():
+        keep = pltpu.make_async_copy(sib, sib_hbm, keep_sem)
+        keep.start()
+        for task in plan[None]:
+            carry(*task)
+        finish_line(which)
+        for distance in range(1, seqs):
+            finish_hops(which, distance)
+        code_copy.wait_send()
+        lax.fori_loop(0, pairs, lambda n, _: (pair_copy(n).wait_send(), 0)[1], 0)
+        keep.wait()
+
+
+def attend_pallas(shape, pieces, plan, q, qc, own, rest_all, down_all, unit=512, chunk=512, block=512):
+    seqs, bits = shape["seq"], (shape["fsdp"] // 2).bit_length() - 1
     rows, width = q.shape
     pairs = width // 128
     part = own.shape[0]
-    row = pl.BlockSpec((rows, 128), lambda j: (0, j))
-    kv = [
-        pl.BlockSpec((part, 128), lambda j: (0, j)),
-        pl.BlockSpec((part, 128), lambda j: (0, 2 * pairs)),
-        pl.BlockSpec((part, 128), lambda j: (0, pairs + j)),
-    ]
+    low = jnp.bfloat16
+    row = pl.BlockSpec((block, 128), lambda j, i: (i, j))
+    any_space = pl.BlockSpec(memory_space=pl.ANY)
+    dma = pltpu.SemaphoreType.DMA
+    like = lambda array: jax.ShapeDtypeStruct(array.shape, array.dtype)
+
     return pl.pallas_call(
-        functools.partial(attend_kernel, unit, chunk),
-        grid=(pairs,),
-        in_specs=[row, pl.BlockSpec((rows, 128), lambda j: (0, 0)), *kv, *kv],
-        out_specs=[pl.BlockSpec((2, 2 * part, rows), lambda j: (j, 0, 0)), row, row],
+        functools.partial(attend_kernel, seqs, bits, pieces, plan, unit, chunk),
+        grid=(pairs, rows // block),
+        in_specs=[
+            row,
+            pl.BlockSpec((block, 128), lambda j, i: (i, 0)),
+            pl.BlockSpec((part, 256), lambda j, i: (0, j)),
+            pl.BlockSpec((part, 128), lambda j, i: (0, 2 * pairs)),
+            any_space,
+            any_space,
+            any_space,
+        ],
+        out_specs=[pl.BlockSpec((2, 2 * part, block), lambda j, i: (j, 0, i)), row, row, any_space, any_space, any_space],
         out_shape=[
-            jax.ShapeDtypeStruct((2 * pairs, 2 * part, rows), jnp.bfloat16),
-            jax.ShapeDtypeStruct((rows, width), jnp.bfloat16),
+            jax.ShapeDtypeStruct((2 * pairs, 2 * part, rows), low),
+            jax.ShapeDtypeStruct((rows, width), low),
             jax.ShapeDtypeStruct((rows, width), jnp.float32),
+            like(own),
+            like(rest_all),
+            like(down_all),
         ],
+        input_output_aliases={5: 4, 6: 5},
         scratch_shapes=[
-            pltpu.VMEM((2, 2 * part, 128), jnp.bfloat16),
-            pltpu.VMEM((2, 128, 2 * part), jnp.bfloat16),
+            pltpu.VMEM((2, 2 * part, 128), low),
+            pltpu.VMEM((2, 128, 2 * part), low),
             pltpu.VMEM((2, 2 * part, unit), jnp.float32),
+            pltpu.VMEM(own.shape, low),
+            dma((2, pairs + 1)),
+            dma,
+            *gatherer_scratch(seqs, bits, len(pieces)),
         ],
-        compiler_params=pltpu.CompilerParams(vmem_limit_bytes=56 << 20),
+        compiler_params=pltpu.CompilerParams(collective_id=3, has_side_effects=True, vmem_limit_bytes=58 << 20),
         name="attend",
-    )(q, qc, own, own, own, sib, sib, sib)
+    )(q, qc, own, own, own, rest_all, down_all)
 
 
 def mean_row(field):
@@ -1320,10 +1481,21 @@
 
 
 def middle_kernel(
-    x_ref, att_ref, cot_ref, wo_ref, wg_ref, wu_ref, wd_ref, norms_ref,
+    seqs, seq_count, x_ref, att_ref, cot_hbm, wo_ref, wg_ref, wu_ref, wd_ref, norms_ref,
     out_ref, dr_ref, branch_ref, datt_ref, hid_ref, mixed_ref, dgate_ref, dup_ref, dff_ref, sums_ref,
-    silu_s, slope_s,
+    silu_s, slope_s, dy_s, dy_sem,
 ):
+    blocks, block = dy_s.shape[:2]
+    subs = blocks // seq_count
+    begin, came, sent = departs(
+        seqs, seq_count, lambda s, sub: cot_hbm.at[s, pl.ds(sub * block, block)], lambda n: dy_s.at[n], dy_sem, subs
+    )
+
+    @pl.when(pl.program_id(0) == 0)
+    def _():
+        greet(column_peers(seqs))
+        begin()
+
     gain_one, shift_one, gain_two, shift_two = (norms_ref[n : n + 1] for n in range(4))
     resid_one = x_ref[...].astype(jnp.float32) + dotf(att_ref[...], wo_ref[...])
     hidden, normed_one, inv_one = normalize(resid_one, gain_one, shift_one)
@@ -1345,7 +1517,9 @@
         resid_two = resid_two + dotf(mixed, wd_ref[cut, :])
     result, normed_two, inv_two = normalize(resid_two, gain_two, shift_two)
     out_ref[...] = result.astype(jnp.bfloat16)
-    dy = cot_ref[...].astype(jnp.float32)
+    now = row_order(seq_count, subs, pl.program_id(0))
+    came(now)
+    dy = dy_s[now].astype(jnp.float32)
     d_two = normalize_back(dy, normed_two, inv_two, gain_two)
     d_ff = d_two.astype(jnp.bfloat16)
     dff_ref[...] = d_ff
@@ -1370,22 +1544,31 @@
     for n, term in enumerate((d_hidden * normed_one, d_hidden, dy * normed_two, dy)):
         sums_ref[n : n + 1] += jnp.sum(term, 0, keepdims=True)
 
-
-def middle(x, attended, cotangent, wide, down, norms, block=256):
+    @pl.when(pl.program_id(0) == blocks - 1)
+    def _():
+        sent()
+
+
+def row_order(seq_count, subs, step):
+    return lax.rem(step, seq_count) * subs + lax.div(step, seq_count)
+
+
+def middle(shape, x, attended, cotangent, rest, down, norms, block=256):
     rows, width = x.shape
     units = down.shape[0]
-    row = lambda cols: pl.BlockSpec((block, cols), lambda i: (i, 0))
+    seq_count, local_len = cotangent.shape[:2]
+    subs = local_len // block
+    row = lambda cols: pl.BlockSpec((block, cols), lambda i: (row_order(seq_count, subs, i), 0))
     once = pl.Buffered(1)
     weight = lambda shape, n: pl.BlockSpec(shape, lambda i: (0, n), pipeline_mode=once)
     like = lambda cols, dtype: jax.ShapeDtypeStruct((rows, cols), dtype)
     low = jnp.bfloat16
-    first_out = (2 * units + 3 * width) // width
     return pl.pallas_call(
-        middle_kernel,
+        functools.partial(middle_kernel, shape["seq"], seq_count),
         grid=(rows // block,),
         in_specs=[
-            row(width), row(width), row(width),
-            weight((width, width), first_out), weight((width, units), 0), weight((width, units), 1),
+            row(width), row(width), pl.BlockSpec(memory_space=pl.ANY),
+            weight((width, width), 2 * units // width), weight((width, units), 0), weight((width, units), 1),
             weight((units, width), 0), weight((8, width), 0),
         ],
         out_specs=[
@@ -1397,10 +1580,15 @@
             like(units, low), like(units, low), like(units, low), like(width, low),
             jax.ShapeDtypeStruct((8, width), jnp.float32),
         ],
-        scratch_shapes=[pltpu.VMEM((block, units), jnp.float32), pltpu.VMEM((block, units), jnp.float32)],
-        compiler_params=pltpu.CompilerParams(vmem_limit_bytes=60 << 20),
+        scratch_shapes=[
+            pltpu.VMEM((block, units), jnp.float32),
+            pltpu.VMEM((block, units), jnp.float32),
+            pltpu.VMEM((rows // block, block, width), low),
+            pltpu.SemaphoreType.DMA((3, rows // block)),
+        ],
+        compiler_params=pltpu.CompilerParams(collective_id=4, has_side_effects=True, vmem_limit_bytes=61 << 20),
         name="middle",
-    )(x, attended, cotangent, wide, wide, wide, down, norms)
+    )(x, attended, cotangent, rest, rest, rest, down, norms)
 
 
 def grad_wide_kernel(tiles, core_ref, left_ref, right_ref, *refs):
@@ -1533,25 +1721,7 @@
 
 NORM_COLS = 256
 PLAN = {1: ((0, 1),), 2: ((0, 2),), 4: ((0, 3), (1, 1)), 6: ((0, 0), (1, 2)), 8: ((1, 3), (2, 1)), 9: ((2, 2),), 10: ((1, 0),), 11: ((2, 3),)}
-AXES = ("seq", "fsdp")
-
-
-def pairs_of(shape, move):
-    seqs, line = shape["seq"], shape["fsdp"]
-    found = []
-    for z in range(seqs):
-        for f in range(line):
-            to_z, to_chip, to_core = move(z, f // 2, f % 2)
-            found.append((z * line + f, to_z * line + 2 * to_chip + to_core))
-    return found
-
-
-def send(array, pairs):
-    return lax.ppermute(array, AXES, pairs)
-
-
-def pick(array, index, axis):
-    return lax.dynamic_index_in_dim(array, index, axis, keepdims=False)
+GATHER_PLAN = {3: ((1,),), 5: ((1, 0),), 6: ((2,),), 7: ((1, 1),), 8: ((2, 0),), 9: ((3,),), 10: ((2, 1),), 11: ((3, 0),), None: ((3, 1),)}
 
 
 def seg_codes(segments):
@@ -1576,32 +1746,16 @@
     group = seqs // seq_count
     units = w_gate.shape[1]
     z = lax.axis_index("seq")
-    f = lax.axis_index("fsdp")
-    core = f % 2
-
-    def there(turn_at):
-        def move(z, p, c):
-            at = (c * seq_count + (z + turn_at) % seq_count) * group + z // seq_count
-            return (at // 2, p, at % 2)
-
-        return pairs_of(shape, move)
-
-    out_pairs = [there(t) for t in range(seq_count)]
-
-    def to_sequences(array):
-        return jnp.concatenate(
-            [send(pick(array, (z + t) % seq_count, 0), out_pairs[t]) for t in range(seq_count)], 0
-        )
-
-    x = to_sequences(tokens)
-    segments = to_sequences(segment_ids)
-    dy = to_sequences(cotangent)
-    q_code, k_code = seg_codes(segments)
-    at = z * 2 + core
-    within = jnp.concatenate(
-        [((at // group - t) % seq_count) * local_len + jnp.arange(local_len) for t in range(seq_count)]
-    )
-    positions = ((at % group) * rows + within).astype(jnp.float32)
+    core = lax.axis_index("fsdp") % 2
+
+    norm_rows = jnp.pad(norm_params.T, ((0, 0), (0, NORM_COLS - norm_params.shape[0])))
+    (x, segments, qkv_all, rest_all, down_all), pieces = first_gather(
+        shape, tokens, segment_ids.reshape(seq_count, 1, local_len), w_gate, w_up, w_qkv, w_out, norm_rows, w_down
+    )
+    x = x.reshape(rows, width)
+    w_all = qkv_all.reshape(width, 3 * width)
+    q_code, k_code = seg_codes(segments.reshape(rows))
+    positions = ((z * 2 + core) % group * rows + jnp.arange(rows)).astype(jnp.float32)
     half_dim = HEAD_DIM // 2
     inverse = jnp.exp(jnp.arange(half_dim, dtype=jnp.float32) * (-2.0 * math.log(ROPE_BASE) / HEAD_DIM))
     angles = positions[:, None] * inverse[None, :]
@@ -1609,20 +1763,16 @@
     cosine = jnp.concatenate([cosine] * 4, 1)
     sine = jnp.concatenate([-sine, sine, -sine, sine], 1)
 
-    norm_rows = jnp.pad(norm_params.T, ((0, 0), (0, NORM_COLS - norm_params.shape[0])))
-    wide, down = gather_all(shape, w_gate, w_up, w_qkv, w_out, norm_rows, w_down)
-    wide = wide.reshape(width, wide.shape[-1])
-    down = down.reshape(units, width)
-    norms = jnp.pad(wide[:, -NORM_COLS : 4 - NORM_COLS].T.astype(jnp.float32), ((0, 4), (0, 0)))
-    first_block = 2 * units // width
-
-    sibling = pairs_of(shape, lambda z, p, c: (z, p, 1 - c))
-    query, own = project(x, wide, first_block, cosine, sine, k_code)
-    sib = send(own, sibling)
-    probs, attended, inverse_sums = attend_pallas(query, q_code, own, sib)
+    query, own = project(x, w_all, 0, cosine, sine, k_code)
+    probs, attended, inverse_sums, sib, rest_all, down_all = attend_pallas(
+        shape, pieces, GATHER_PLAN, query, q_code, own, rest_all, down_all
+    )
+    rest = rest_all.reshape(width, rest_all.shape[-1])
+    down = down_all.reshape(units, width)
+    norms = jnp.pad(rest[:, -NORM_COLS : 4 - NORM_COLS].T.astype(jnp.float32), ((0, 4), (0, 0)))
     (
         result, d_resid_one, d_branch, d_attended, hidden_low, mixed, d_gate, d_up, d_ff, sums,
-    ) = middle(x, attended, dy, wide, down, norms)
+    ) = middle(shape, x, attended, cotangent, rest, down, norms)
 
     core_id = core.astype(jnp.int32).reshape(1)
     own_rows = w_gate.shape[0]
@@ -1636,7 +1786,7 @@
         shape, query, own, sib, probs, attended, inverse_sums, d_attended, *held, result, seq_count, PLAN
     )
     back, qkv_sums, squares = tail(
-        shape, cosine, sine, d_query, d_own, d_got, wide, first_block, d_resid_one, x, reduced_sums, seq_count
+        shape, cosine, sine, d_query, d_own, d_got, w_all, 0, d_resid_one, x, reduced_sums, seq_count
     )
     states = (
         w_qkv, w_out, w_gate, w_up, w_down, norm_params,

time: 495 us -> 451 us (0.911)
  starting transfers between devices: 20.1 us -> 0 us
  local copies, waits for them, and re-layouts: 16.3 us -> 6.33 us
  waiting for transfers between devices: 8.76 us -> 0 us
    ppermute x7 -> x0, starting transfers between devices: 20.1 us -> none  [send(): return lax.ppermute(array, AXES, pairs)]
    pallas_call x3, Pallas kernels: 196 us -> 207 us  [the longest x1 77.5 us: attend_pallas(): pl.pallas_call(functools.partial(attend_kernel, seqs, bits, pieces, plan,...]
    pallas_call x1, Pallas kernels: 121 us -> 111 us  [attend_back_pallas(): pl.pallas_call(functools.partial(attend_back_kernel, seqs, bits, pieces,...]
    ppermute x7 -> x0, waiting for transfers between devices: 8.76 us -> none  [send(): return lax.ppermute(array, AXES, pairs)]
  transfers between devices with their start and end apart: 7 -> 0, of which waited for: 1 -> 0; matrix products, arithmetic and copies ran while one was open for 3% -> 0% of each run, Pallas kernels for 20% -> 0%
where the time goes in v4:
time: 451 us; the launch traced here: 447 us
  Pallas kernels  435 us (96%)
  local copies, waits for them, and re-layouts  6.33 us (1%)
  other arithmetic  4.74 us (1%)
    pallas_call x1, Pallas kernels, attend_back_pallas(): pl.pallas_call(functools.partial(attend_back_kernel, seqs, bits, pieces,...  111 us
    pallas_call x1, Pallas kernels, attend_pallas(): pl.pallas_call(functools.partial(attend_kernel, seqs, bits, pieces, plan,...  77.5 us
    pallas_call x1, Pallas kernels, first_gather(): pl.pallas_call(functools.partial(first_gather_kernel, seqs, bits, pieces,...  69 us
    pallas_call x1, Pallas kernels, tail(): pl.pallas_call(functools.partial(tail_kernel, seqs, bits, pieces), grid=(...  67.8 us
    pallas_call x1, Pallas kernels, middle(): pl.pallas_call(functools.partial(middle_kernel, shape['seq'], seq_count),...  60.9 us
    pallas_call x2, Pallas kernels, grad_wide(): pl.pallas_call(functools.partial(grad_wide_kernel, tiles), grid_spec=pltp...  20.4 us
    pallas_call x1, Pallas kernels, grad_tall(): pl.pallas_call(functools.partial(grad_tall_kernel, rows), grid_spec=pltpu...  10.8 us

profile of v4, /device:TPU:0, one launch (start us, length us, event | category | flops | bytes accessed | tf_op | source)
XLA Modules:
  0.0 447.1 jit_solution(2831136028699527429)
XLA Ops:
  0.7 0.0 copy-start.11
  0.7 0.0 copy-start.10
  0.7 0.0 copy-start.9
  0.7 0.0 copy-start.13
  0.7 0.0 copy-start.12
  0.8 0.8 reshape.106.refs_1_
  1.6 0.8 copy.63
  2.3 1.9 fusion.1
  4.2 0.9 pad_maximum_fusion
  5.2 69.0 %first_gather.1 = (bf16[2,512,768]{2,1,0:T(8,128)(2,1)S(1)}, s32[2,1,512]{2,1,0:T(1,128)S(1)}, bf16[4,4,48,2304]{3,2,1,0:T(8,128)(2,1)}, bf16[4,4,48,7168]{3,2,1,0:T(8,128)(2,1)}, bf16[4,4,192,768]{3,2,1,0:T(8,128)(2,1)}) custom-call(bf16[2,512,768]{2,1,0:T(8,128)(2,1)S(1)} %copy-done.7, s32[2,1,512]{2,1,0:T(1,128)S(1)} %reshape.106.refs_1_, ...), custom_call_target="tpu_custom_call" | custom-call | tf_op jit(solution)/shard_map/first_gather/pallas_call | solution.py:755
  74.2 0.0 copy-start
  74.2 1.1 select_convert_fusion.qc_ref
  75.3 0.2 multiply_convert_fusion.code_ref
  75.5 7.8 %project.1 = (bf16[1024,768]{1,0:T(8,128)(2,1)S(1)}, bf16[1024,1664]{1,0:T(8,128)(2,1)}) custom-call(bf16[1024,768]{1,0:T(8,128)(2,1)S(1)} %bitcast.11, bf16[768,2304]{1,0:T(8,128)(2,1)} %bitcast.20, bf16[768,2304]{1,0:T(8,128)(2,1)} %bitcast.21, bf16[768,2304]{1,0:T(8,128)(2,1)} %bitcast.22, f32[1024,128]{1,0:T(8,128)S(1)} %get-tuple-element.160.cos_ref, ...), custom_call_target="tpu_custom_call" | custom-call | tf_op jit(solution)/shard_map/project/pallas_call | solution.py:1307
  83.3 0.0 copy-start.3
  83.3 1.1 copy-done.3
  84.4 77.5 %attend.1 = (bf16[12,2048,1024]{2,1,0:T(8,128)(2,1)}, bf16[1024,768]{1,0:T(8,128)(2,1)}, f32[1024,768]{1,0:T(8,128)}, bf16[1024,1664]{1,0:T(8,128)(2,1)}, bf16[4...) custom-call(bf16[1024,768]{1,0:T(8,128)(2,1)} %copy-done.3, ...), custom_call_target="tpu_custom_call", output_to_operand_aliasing={{4}: (5, {}), {5}: (6, {})} | custom-call | tf_op jit(solution)/shard_map/attend/pallas_call | solution.py:1443
  161.9 0.9 slice.4
  162.9 0.1 copy.66
  163.0 0.6 pad_convert_fusion.norms_ref
  163.7 60.9 %middle.1 = (bf16[1024,768]{1,0:T(8,128)(2,1)}, f32[1024,768]{1,0:T(8,128)}, bf16[1024,768]{1,0:T(8,128)(2,1)}, bf16[1024,768]{1,0:T(8,128)(2,1)}, bf16[1024,768...) custom-call(bf16[1024,768]{1,0:T(8,128)(2,1)} %bitcast.12, ...), custom_call_target="tpu_custom_call" | custom-call | tf_op jit(solution)/shard_map/middle/pallas_call | solution.py:1566
  224.6 1.4 copy-done.8
  226.0 10.8 %grad_tall.1 = (bf16[768,5120]{1,0:T(8,128)(2,1)}, bf16[768,5120]{1,0:T(8,128)(2,1)}) custom-call(s32[1]{0:T(128)} %bitcast.7.core_ref, bf16[1024,3072]{1,0:T(8,128)(2,1)} %get-tuple-element.111.left_ref, bf16[1024,768]{1,0:T(8,128)(2,1)S(1)} %copy-done.8), custom_call_target="tpu_custom_call" | custom-call | tf_op jit(solution)/shard_map/grad_tall/pallas_call | solution.py:1676
  236.8 0.0 copy-done.2
  236.8 10.0 %grad_wide.2 = (bf16[768,5120]{1,0:T(8,128)(2,1)}, bf16[768,5120]{1,0:T(8,128)(2,1)}) custom-call(s32[1]{0:T(128)} %bitcast.7.core_ref, bf16[1024,768]{1,0:T(8,128)(2,1)S(1)} %copy-done.2, bf16[1024,3072]{1,0:T(8,128)(2,1)} %get-tuple-element.110.right_ref, ...), custom_call_target="tpu_custom_call", output_to_operand_aliasing={{0}: (3, {}), {1}: (4, {})} | custom-call | tf_op jit(solution)/shard_map/grad_wide/pallas_call | solution.py:1613
  246.7 10.4 %grad_wide.3 = (bf16[768,5120]{1,0:T(8,128)(2,1)}, bf16[768,5120]{1,0:T(8,128)(2,1)}) custom-call(s32[1]{0:T(128)} %bitcast.7.core_ref, bf16[1024,768]{1,0:T(8,128)(2,1)S(1)} %copy-done.2, bf16[1024,3072]{1,0:T(8,128)(2,1)} %get-tuple-element.109.right_ref, ...), custom_call_target="tpu_custom_call", output_to_operand_aliasing={{0}: (3, {}), {1}: (4, {})} | custom-call | tf_op jit(solution)/shard_map/grad_wide/pallas_call | solution.py:1613
  257.1 0.0 copy-done.14
  257.1 2.7 grad_out.1
  259.8 111.4 %attend_back.1 = (f32[1024,768]{1,0:T(8,128)}, f32[2,1024,768]{2,1,0:T(8,128)}, bf16[2,1024,768]{2,1,0:T(8,128)(2,1)}, f32[2,24,5120]{2,1,0:T(8,128)}, bf16[2,512,768]{2,1,0:T(8,128)(2,1)}) custom-call(bf16[1024,768]{1,0:T(8,128)(2,1)} %copy-done.3, bf16[1024,1664]{1,0:T(8,128)(2,1)} %get-tuple-element.96.own_ref.code_ref.own_hbm.k0.v0, ...), custom_call_target="tpu_custom_call" | custom-call | tf_op jit(solution)/shard_map/attend_back/pallas_call | solution.py:1036
  371.3 67.8 %tail.1 = (bf16[2,512,768]{2,1,0:T(8,128)(2,1)}, f32[2,24,1152]{2,1,0:T(8,128)}, f32[8,128]{1,0:T(8,128)}) custom-call(f32[1024,128]{1,0:T(8,128)} %copy-done.4, f32[1024,128]{1,0:T(8,128)} %copy-done.5, f32[1024,768]{1,0:T(8,128)} %get-tuple-element.124.dq_ref, f32[2,1024,768]{2,1,0:T(8,128)} %get-tuple-element.125.own_ref, ...), custom_call_target="tpu_custom_call" | custom-call | tf_op jit(solution)/shard_map/tail/pallas_call | solution.py:1182
  439.0 6.6 %adam.1 = (f32[24,2304]{1,0:T(8,128)}, f32[24,768]{1,0:T(8,128)}, f32[24,3072]{1,0:T(8,128)}, f32[24,3072]{1,0:T(8,128)}, f32[96,768]{1,0:T(8,128)}, /*index=5*/...) custom-call(f32[2,24,5120]{2,1,0:T(8,128)} %get-tuple-element.123.su, ...), custom_call_target="tpu_custom_call" | custom-call | tf_op jit(solution)/shard_map/adam/pallas_call | solution.py:1262
  445.7 1.1 copy.76
  (26 shorter events, 0.1 us)
Async XLA Ops:
  0.7 4.5 %copy-start.11 = (f32[96,768]{1,0:T(8,128)S(1)}, f32[96,768]{1,0:T(8,128)}, u32[]{:S(2)}) copy-start(f32[96,768]{1,0:T(8,128)} %refs_4_.3) | copy-start | bytes 884740
  0.7 4.5 %copy-start.10 = (f32[24,3072]{1,0:T(8,128)S(1)}, f32[24,3072]{1,0:T(8,128)}, u32[]{:S(2)}) copy-start(f32[24,3072]{1,0:T(8,128)} %refs_3_.3) | copy-start | bytes 884740
  0.7 4.5 %copy-start.9 = (f32[24,3072]{1,0:T(8,128)S(1)}, f32[24,3072]{1,0:T(8,128)}, u32[]{:S(2)}) copy-start(f32[24,3072]{1,0:T(8,128)} %refs_2_.3) | copy-start | bytes 884740
  0.7 4.5 %copy-start.13 = (f32[24,768]{1,0:T(8,128)S(1)}, f32[24,768]{1,0:T(8,128)}, u32[]{:S(2)}) copy-start(f32[24,768]{1,0:T(8,128)} %refs_1_.1) | copy-start | bytes 221188
  0.7 4.5 %copy-start.12 = (f32[24,2304]{1,0:T(8,128)S(1)}, f32[24,2304]{1,0:T(8,128)}, u32[]{:S(2)}) copy-start(f32[24,2304]{1,0:T(8,128)} %refs_0_.3) | copy-start | bytes 663556
  2.3 2.9 copy-start.7
  5.1 78.1 %copy-start.4 = (f32[1024,128]{1,0:T(8,128)}, f32[1024,128]{1,0:T(8,128)S(1)}, u32[]{:S(2)}) copy-start(f32[1024,128]{1,0:T(8,128)S(1)} %get-tuple-element.160.cos_ref) | copy-start | bytes 1572868
  5.1 78.1 %copy-start.5 = (f32[1024,128]{1,0:T(8,128)}, f32[1024,128]{1,0:T(8,128)S(1)}, u32[]{:S(2)}) copy-start(f32[1024,128]{1,0:T(8,128)S(1)} %get-tuple-element.161.sin_ref) | copy-start | bytes 1572868
  74.2 9.1 %copy-start = (bf16[2,512,768]{2,1,0:T(8,128)(2,1)}, bf16[2,512,768]{2,1,0:T(8,128)(2,1)S(1)}, u32[]{:S(2)}) copy-start(bf16[2,512,768]{2,1,0:T(8,128)(2,1)S(1)} %get-tuple-element.92) | copy-start | bytes 4718596
  83.3 1.1 copy-start.3
  224.6 1.4 copy-start.8
  226.0 10.8 %copy-start.2 = (bf16[1024,768]{1,0:T(8,128)(2,1)S(1)}, bf16[1024,768]{1,0:T(8,128)(2,1)}, u32[]{:S(2)}) copy-start(bf16[1024,768]{1,0:T(8,128)(2,1)} %get-tuple-element.108.left_ref) | copy-start | bytes 4718596
  246.7 10.4 %copy-start.1 = (bf16[1024,768]{1,0:T(8,128)(2,1)S(1)}, bf16[1024,768]{1,0:T(8,128)(2,1)}, u32[]{:S(2)}) copy-start(bf16[1024,768]{1,0:T(8,128)(2,1)} %get-tuple-element.101.att_ref.left_ref.o_ref) | copy-start | bytes 4718596
  246.7 10.4 %copy-start.6 = (bf16[1024,768]{1,0:T(8,128)(2,1)S(1)}, bf16[1024,768]{1,0:T(8,128)(2,1)}, u32[]{:S(2)}) copy-start(bf16[1024,768]{1,0:T(8,128)(2,1)} %get-tuple-element.106.right_ref) | copy-start | bytes 4718596
  246.7 10.4 %copy-start.14 = (f32[8,768]{1,0:T(8,128)S(1)}, f32[8,768]{1,0:T(8,128)}, u32[]{:S(2)}) copy-start(f32[8,768]{1,0:T(8,128)} %get-tuple-element.107.sums_ref) | copy-start | bytes 73732
  439.0 6.7 %copy-start.15 = (bf16[2,512,768]{2,1,0:T(8,128)(2,1)S(1)}, bf16[2,512,768]{2,1,0:T(8,128)(2,1)}, u32[]{:S(2)}) copy-start(bf16[2,512,768]{2,1,0:T(8,128)(2,1)} %get-tuple-element.191) | copy-start | bytes 4718596

commit v5 on v4

--- a/solution.py
+++ b/solution.py
@@ -710,7 +710,7 @@
     own_hops(rest)
     for distance in range(1, seqs):
         line(early, distance)
-        if distance == seqs - 2:
+        if distance == 1:
             token_begin()
         hops(early, distance - 1)
     hops(rest, 0)
@@ -785,175 +785,372 @@
     return [m ^ (1 << order[stage]) for m in hop_masks(order, stage)].index(mask)
 
 
-def reducer_scratch(seqs, bits, pieces, rows, width):
+def z_low(zm):
+    return (zm & -zm).bit_length() - 1
+
+
+def span(pieces, group):
+    return pieces[group[0]][0], sum(pieces[p][1] for p in group)
+
+
+def reducer_scratch(seqs, bits, pieces, groups, rows, width):
     dma = pltpu.SemaphoreType.DMA
-    chips = 1 << bits
     low = jnp.bfloat16
+    line_bits = seqs.bit_length() - 1
     hops = [
         pltpu.VMEM((seqs, len(hop_masks(order, stage)), rows, cols), low)
         for _, cols, order in pieces
         for stage in range(bits)
     ]
-    most = max(1, chips // 2)
+    lines = [
+        pltpu.VMEM((seqs >> (k + 1), rows, span(pieces, group)[1]), low) for group in groups for k in range(line_bits)
+    ]
+    most = 1 << (bits - 1)
     return [
-        pltpu.VMEM((seqs, chips, rows, width), low),
-        pltpu.VMEM((seqs, rows, width), low),
         pltpu.VMEM((2, rows // 2, width), jnp.float32),
         pltpu.VMEM((rows // 2, width), jnp.float32),
-        dma((2, seqs, chips)),
+        dma((2, seqs, 1 << bits)),
         dma((2, len(pieces), bits, seqs, most)),
-        dma((2, seqs)),
+        dma((2, len(groups), line_bits, seqs)),
         dma((2,)),
         *hops,
+        *lines,
     ]
 
 
-def reducer(seqs, bits, pieces, away, keep, got, line, halves_ref, swapped, core_sem, hop_sem, line_sem, swap_sem, *hops):
+def reducer(seqs, bits, pieces, groups, away, keep, got, halves_ref, swapped, core_sem, hop_sem, line_sem, swap_sem, *buffers):
     z, chip, core = place()
     rows = keep.shape[2]
     half = rows // 2
+    line_bits = seqs.bit_length() - 1
     sibling = {"fsdp": 2 * chip + 1 - core}
     masks = range(1 << bits)
-    hop = lambda p, stage: hops[p * bits + stage]
+    hop = lambda p, stage: buffers[p * bits + stage]
+    line = lambda g, k: buffers[len(pieces) * bits + g * line_bits + k]
 
     def remote(source, target, sems, index, device):
         return pltpu.make_async_remote_copy(
             source, target, sems.at[(0, *index)], sems.at[(1, *index)], device_id=device, device_id_type=MESH_ID
         )
 
-    def core_copy(zz, mask):
-        at = chip_at(chip, mask)
-        return remote(away.at[zz, at], got.at[zz, at], core_sem, (zz, at), sibling)
-
-    def hop_copy(p, stage, zz, mask):
-        start, cols, order = pieces[p]
+    def core_copy(zm, mask):
+        at = (chip_at(z, zm), chip_at(chip, mask))
+        return remote(away.at[at], got.at[at], core_sem, (zm, mask), sibling)
+
+    def hop_copy(p, stage, zm, mask):
+        first, cols, order = pieces[p]
         slot = hop_slot(order, stage, mask ^ (1 << order[stage]))
         return remote(
-            got.at[zz, chip_at(chip, mask), :, pl.ds(start, cols)],
-            hop(p, stage).at[zz, slot],
+            got.at[chip_at(z, zm), chip_at(chip, mask), :, pl.ds(first, cols)],
+            hop(p, stage).at[zm, slot],
             hop_sem,
-            (p, stage, zz, slot),
+            (p, stage, zm, slot),
             {"fsdp": 2 * chip_at(chip, 1 << order[stage]) + core},
         )
 
-    def line_copy(zz, source):
-        return remote(got.at[zz, chip], line.at[source], line_sem, (source,), {"seq": zz})
-
-    def total(p, zz, mask, stages):
-        start, cols, order = pieces[p]
-        at = chip_at(chip, mask)
-        where = (zz, at, slice(None), pl.ds(start, cols))
+    def line_copy(g, zm):
+        k = z_low(zm)
+        slot = zm >> (k + 1)
+        return remote(
+            got.at[chip_at(z, zm), chip, :, pl.ds(*span(pieces, groups[g]))],
+            line(g, k).at[slot],
+            line_sem,
+            (g, k, slot),
+            {"seq": chip_at(z, 1 << k)},
+        )
+
+    def total(p, zm, mask, stages, lines=0):
+        first, cols, order = pieces[p]
+        where = (chip_at(z, zm), chip_at(chip, mask), slice(None), pl.ds(first, cols))
         value = keep[where].astype(jnp.float32) + got[where].astype(jnp.float32)
         for stage in range(stages):
-            value = value + hop(p, stage)[zz, hop_slot(order, stage, mask)].astype(jnp.float32)
+            value = value + hop(p, stage)[zm, hop_slot(order, stage, mask)].astype(jnp.float32)
+        if lines:
+            g = [n for n, group in enumerate(groups) if p in group][0]
+            here = pl.ds(first - span(pieces, groups[g])[0], cols)
+            for k in range(lines):
+                value = value + line(g, k)[zm >> (k + 1), :, here].astype(jnp.float32)
         return value
 
+    def come(g, stage, zm):
+        for p in groups[g]:
+            for mask in hop_masks(pieces[p][2], stage):
+                hop_copy(p, stage, zm, mask).wait_recv()
+
+    def come_line(g, zm, lines):
+        for k in range(lines):
+            line_copy(g, zm | (1 << k)).wait_recv()
+
     def start():
-        for k in range(1, seqs + 1):
-            zz = lax.rem(z + k, seqs)
+        for zm in (*range(1, seqs), 0):
             for mask in reversed(masks):
-                core_copy(zz, mask).start()
-
-    def come(p, stage, zz):
-        for mask in hop_masks(pieces[p][2], stage):
-            hop_copy(p, stage, zz, mask).wait_recv()
-
-    def stage_of(stage, zz):
-        if stage == 0:
+                core_copy(zm, mask).start()
+
+    def hop_task(g, stage, zm):
+        if stage:
+            come(g, stage - 1, zm)
+        elif away is not None:
             for mask in masks:
-                core_copy(zz, mask).wait_recv()
-        for p, (first, cols, order) in enumerate(pieces):
-            if stage:
-                come(p, stage - 1, zz)
+                core_copy(zm, mask).wait_recv()
+        for p in groups[g]:
+            first, cols, order = pieces[p]
             for mask in hop_masks(order, stage):
-                got[zz, chip_at(chip, mask), :, pl.ds(first, cols)] = total(p, zz, mask, stage).astype(jnp.bfloat16)
-                hop_copy(p, stage, zz, mask).start()
-
-    def line_of(zz):
-        for p, (first, cols, _) in enumerate(pieces):
-            come(p, bits - 1, zz)
-            got[zz, chip, :, pl.ds(first, cols)] = total(p, zz, 0, bits).astype(jnp.bfloat16)
-        line_copy(zz, z).start()
+                got[chip_at(z, zm), chip_at(chip, mask), :, pl.ds(first, cols)] = total(p, zm, mask, stage).astype(
+                    jnp.bfloat16
+                )
+                hop_copy(p, stage, zm, mask).start()
+
+    def line_task(g, zm):
+        k = z_low(zm)
+        come(g, bits - 1, zm)
+        come_line(g, zm, k)
+        for p in groups[g]:
+            first, cols, _ = pieces[p]
+            got[chip_at(z, zm), chip, :, pl.ds(first, cols)] = total(p, zm, 0, bits, k).astype(jnp.bfloat16)
+        line_copy(g, zm).start()
+
+    def task(g, kind, zm):
+        if kind == bits:
+            line_task(g, zm)
+        else:
+            hop_task(g, kind, zm)
 
     def finish():
-        for p in range(len(pieces)):
-            come(p, bits - 1, z)
-        for k in range(1, seqs):
-            source = lax.rem(z + k, seqs)
-            line_copy(z, source).wait_recv()
-        for p, (first, cols, _) in enumerate(pieces):
-            value = total(p, z, 0, bits)
-            for k in range(1, seqs):
-                value = value + line[lax.rem(z + k, seqs), :, pl.ds(first, cols)].astype(jnp.float32)
-            halves_ref[0, :, pl.ds(first, cols)] = value[:half]
-            halves_ref[1, :, pl.ds(first, cols)] = value[half:]
+        for g, group in enumerate(groups):
+            come(g, bits - 1, 0)
+            come_line(g, 0, line_bits)
+            for p in group:
+                first, cols, _ = pieces[p]
+                value = total(p, 0, 0, bits, line_bits)
+                halves_ref[0, :, pl.ds(first, cols)] = value[:half]
+                halves_ref[1, :, pl.ds(first, cols)] = value[half:]
         swap = remote(halves_ref.at[1 - core], swapped, swap_sem, (), sibling)
         swap.start()
-        for zz in range(seqs):
-            for mask in masks:
-                core_copy(zz, mask).wait_send()
+        for zm in range(seqs):
+            if away is not None:
+                for mask in masks:
+                    core_copy(zm, mask).wait_send()
             for p, (_, _, order) in enumerate(pieces):
                 for stage in range(bits):
                     for mask in hop_masks(order, stage):
-                        hop_copy(p, stage, zz, mask).wait_send()
-        for k in range(1, seqs):
-            line_copy(lax.rem(z + k, seqs), z).wait_send()
+                        hop_copy(p, stage, zm, mask).wait_send()
+            if zm:
+                for g in range(len(groups)):
+                    line_copy(g, zm).wait_send()
         swap.wait()
 
-    def own(k):
-        return lax.rem(z + k, seqs)
-
-    return start, stage_of, line_of, finish, own
-
-
-def attend_back_kernel(
-    seqs, bits, pieces, plan,
-    q_ref, k0, v0, k1, v1, p_ref, o_ref, inv_ref, do_ref, keep_hbm, away_hbm, result_hbm,
+    return start, task, finish
+
+
+GROUPS = ((0, 1), (2, 3))
+
+
+def sum_pieces(units, tall, out, bits):
+    upward, downward = tuple(range(bits)), tuple(reversed(range(bits)))
+    cut = (tall + out) // 256 * 128
+    half = units // 2
+    return (
+        (0, half, upward),
+        (half, half, downward),
+        (units, cut, upward),
+        (units + cut, tall + out - cut, downward),
+    )
+
+
+def back_kernel(
+    seqs, bits, pieces, plan, tiles, talls, fold, turns,
+    hid_ref, att_ref, branch_ref, dff_ref, sums_ref, mixed_ref, dgate_ref, dup_ref,
+    q_ref, k0, v0, k1, v1, p_ref, inv_ref, do_ref, result_hbm,
     dq_ref, own_ref, sib_ref, sum_ref, output_hbm,
-    kt, va, dk, dv, sib, sib_sem, keep, keep_sem, back_sem, *shared,
+    keep, got, away_wide, away_tall, away_sem, kt, va, dk, dv, sib, sib_sem, back_sem, *shared,
+):
+    z, chip, core = place()
+    sibling = {"fsdp": 2 * chip + 1 - core}
+    step = pl.program_id(0)
+    last = pl.num_programs(0) - 1
+    rows = keep.shape[2]
+    chips = seqs << bits
+    low = jnp.bfloat16
+    width = att_ref.shape[1]
+    tile = dgate_ref.shape[1]
+    tall = fold * width // 2
+    out_cols = (width + NORM_COLS) // 2
+    units = 2 * tiles * tile
+    first_steps = 4 * tiles + talls + 1
+    per_z = 1 << bits
+    _, sum_task, finish = reducer(seqs, bits, pieces, GROUPS, None, keep, got, *shared)
+    seq_count, local_len = output_hbm.shape[:2]
+    back_begin, back_end = returns(
+        seqs, seq_count, lambda n: result_hbm.at[pl.ds(n * local_len, local_len)], output_hbm, back_sem, local_len
+    )
+
+    def wide_copy(n, slot):
+        at = n * tile if n is not None else units + tall
+        cols = pl.ds(pl.multiple_of(at, 128), tile)
+        return pltpu.make_async_remote_copy(
+            away_wide.at[slot], got.at[:, :, :, cols],
+            away_sem.at[0, n if n is not None else 2 * tiles], away_sem.at[1, n if n is not None else 2 * tiles],
+            device_id=sibling, device_id_type=MESH_ID,
+        )
+
+    def tall_copy(n):
+        count = chips // talls
+        at = n * count
+        index = 2 * tiles + 1 + n
+        return pltpu.make_async_remote_copy(
+            away_tall.at[lax.rem(n, 2)],
+            got.at[lax.div(at, per_z), pl.ds(lax.rem(at, per_z), count), :, pl.ds(units, tall)],
+            away_sem.at[0, index], away_sem.at[1, index],
+            device_id=sibling, device_id_type=MESH_ID,
+        )
+
+    @pl.when(step == 0)
+    def _():
+        greet(sum_peers(bits) + column_peers(seqs))
+        for n in range(seq_count):
+            back_begin(n)
+
+    for n, ref in enumerate((dgate_ref, dup_ref)):
+
+        @pl.when((step >= n * tiles) & (step < (n + 1) * tiles))
+        def _():
+            slot = lax.rem(step, 2)
+
+            @pl.when(step >= 2)
+            def _():
+                wide_copy(step - 2, slot).wait_send()
+
+            away_wide[slot] = dotf(hid_ref[...], ref[...]).astype(low).reshape(away_wide.shape[1:])
+            wide_copy(step, slot).start()
+
+        @pl.when((step >= (2 + n) * tiles) & (step < (3 + n) * tiles))
+        def _():
+            cols = pl.ds(pl.multiple_of((step - 2 * tiles) * tile, 128), tile)
+            keep[:, :, :, cols] = dotf(hid_ref[...], ref[...]).astype(low).reshape(away_wide.shape[1:])
+
+    n_tall = step - 4 * tiles
+
+    def sides(halves, mine, other):
+        for side, value in enumerate(halves):
+
+            @pl.when(core == side)
+            def _():
+                mine(value)
+
+            @pl.when(core != side)
+            def _():
+                other(value)
+
+    @pl.when((n_tall >= 0) & (n_tall < talls))
+    def _():
+        @pl.when(n_tall >= 2)
+        def _():
+            tall_copy(n_tall - 2).wait_send()
+
+        value = dotf(mixed_ref[...], dff_ref[...], TN)
+        own = rows // 2
+        count = chips // talls
+        at = n_tall * count
+
+        def folded(part):
+            return jnp.concatenate(
+                [
+                    jnp.concatenate([part[(b * fold + a) * own : (b * fold + a + 1) * own] for a in range(fold)], 1)
+                    for b in range(part.shape[0] // (fold * own))
+                ],
+                0,
+            ).astype(low).reshape(count, rows, tall)
+
+        def mine(value):
+            keep[lax.div(at, per_z), pl.ds(lax.rem(at, per_z), count), :, units : units + tall] = value
+
+        def other(value):
+            away_tall[lax.rem(n_tall, 2)] = value
+
+        sides([folded(value[:, : width // 2]), folded(value[:, width // 2 :])], mine, other)
+        tall_copy(n_tall).start()
+
+    @pl.when(n_tall == talls)
+    def _():
+        wide_copy(2 * tiles - 2, 0).wait_send()
+        value = dotf(att_ref[...], branch_ref[...], TN)
+        pad = jnp.zeros((NORM_COLS - sums_ref.shape[0], width), jnp.float32)
+        value = jnp.concatenate([value, jnp.concatenate([sums_ref[...], pad], 0).T], 1).astype(low)
+
+        def mine(value):
+            keep[:, :, :, units + tall :] = value
+
+        def other(value):
+            away_wide[0] = value
+
+        sides(
+            [value[:, n * out_cols : (n + 1) * out_cols].reshape(away_wide.shape[1:]) for n in range(2)], mine, other
+        )
+        wide_copy(None, 0).start()
+
+    @pl.when(step == 4 * tiles)
+    def _():
+        for n in range(2 * tiles):
+            wide_copy(n, n % 2).wait_recv()
+
+    @pl.when(step == first_steps)
+    def _():
+        wide_copy(2 * tiles - 1, 1).wait_send()
+        wide_copy(None, 0).wait()
+        for n in range(talls):
+            tall_copy(n).wait_recv()
+        for n in (talls - 2, talls - 1):
+            tall_copy(n).wait_send()
+
+    for at, tasks in plan.items():
+
+        @pl.when(step == at)
+        def _():
+            for one in tasks:
+                sum_task(*one)
+
+    attention = step - first_steps
+
+    @pl.when(attention >= 0)
+    def _():
+        attend_back_block(
+            turns, lax.div(attention, turns), lax.rem(attention, turns),
+            q_ref, k0, v0, k1, v1, p_ref, att_ref, inv_ref, do_ref, dq_ref, own_ref, sib_ref, kt, va, dk, dv, sib, sib_sem,
+        )
+
+    @pl.when(step == last)
+    def _():
+        finish()
+        back_end()
+        halves_ref, swapped = shared[0], shared[1]
+        sum_ref[core] = halves_ref[core]
+        sum_ref[1 - core] = swapped[...]
+        pairs = width // 128
+        for pair in range(pairs):
+            if pair >= pairs - 2:
+                sib_copy(sib, sib_ref, sib_sem, pair).wait_send()
+            sib_copy(sib, sib_ref, sib_sem, pair).wait_recv()
+
+
+def sib_copy(sib, sib_ref, sib_sem, pair):
+    z, chip, core = place()
+    return pltpu.make_async_remote_copy(
+        sib.at[lax.rem(pair, 2)],
+        sib_ref.at[:, :, pl.ds(pl.multiple_of(pair * 128, 128), 128)],
+        sib_sem.at[0, pair],
+        sib_sem.at[1, pair],
+        device_id={"fsdp": 2 * chip + 1 - core},
+        device_id_type=MESH_ID,
+    )
+
+
+def attend_back_block(
+    turns, j, i,
+    q_ref, k0, v0, k1, v1, p_ref, att_ref, inv_ref, do_ref, dq_ref, own_ref, sib_ref, kt, va, dk, dv, sib, sib_sem,
 ):
     part = k0.shape[0]
     unit = q_ref.shape[0]
-    j, i = pl.program_id(0), pl.program_id(1)
-    count = pl.num_programs(1)
-    step = j * count + i
-    z, chip, core = place()
     lane_k = lax.broadcasted_iota(jnp.int32, (part, 128), 1)
-    start, stage_of, line_of, finish, own = reducer(seqs, bits, pieces, away_hbm, keep, *shared)
-    keep_copy = pltpu.make_async_copy(keep_hbm, keep, keep_sem)
-    seq_count, local_len = output_hbm.shape[:2]
-    back_begin, back_end = returns(
-        seqs, seq_count, lambda n: result_hbm.at[pl.ds(n * local_len, local_len)], output_hbm, back_sem, local_len
-    )
-
-    def sib_copy(pair):
-        return pltpu.make_async_remote_copy(
-            sib.at[lax.rem(pair, 2)],
-            sib_ref.at[:, :, pl.ds(pl.multiple_of(pair * 128, 128), 128)],
-            sib_sem.at[0, pair],
-            sib_sem.at[1, pair],
-            device_id={"fsdp": 2 * chip + 1 - core},
-            device_id_type=MESH_ID,
-        )
-
-    @pl.when(step == 0)
-    def _():
-        keep_copy.start()
-        greet(sum_peers(bits) + column_peers(seqs))
-        start()
-        for n in range(seq_count):
-            back_begin(n)
-        keep_copy.wait()
-
-    for at, tasks in plan.items():
-
-        @pl.when(step == at)
-        def _():
-            for kind, k in tasks:
-                if kind < bits:
-                    stage_of(kind, own(k))
-                else:
-                    line_of(own(k))
 
     @pl.when(i == 0)
     def _():
@@ -970,8 +1167,9 @@
 
     lane = lax.broadcasted_iota(jnp.int32, (unit, 128), 1)
     q = q_ref[...]
+    o = att_ref[pl.ds(pl.multiple_of(i * unit, unit), unit), pl.ds(pl.multiple_of(j * 128, 128), 128)]
     dof = do_ref[...].astype(jnp.float32) * inv_ref[...]
-    prod = dof * o_ref[...].astype(jnp.float32)
+    prod = dof * o.astype(jnp.float32)
     dob = dof.astype(jnp.bfloat16)
     zero = jnp.zeros_like(dob)
     turned = None
@@ -993,91 +1191,116 @@
         turned = new if turned is None else turned + new
     dq_ref[...] = turned.T * (1.0 / math.sqrt(HEAD_DIM))
 
-    @pl.when(i == count - 1)
+    @pl.when(i == turns - 1)
     def _():
         @pl.when(j >= 2)
         def _():
-            sib_copy(j - 2).wait_send()
+            sib_copy(sib, sib_ref, sib_sem, j - 2).wait_send()
 
         for n, total in enumerate((dk, dv)):
             own_ref[n] = total[:part]
             sib[lax.rem(j, 2), n] = total[part:].astype(jnp.bfloat16)
-        sib_copy(j).start()
-
-    @pl.when(step == pl.num_programs(0) * count - 1)
-    def _():
-        finish()
-        back_end()
-        halves_ref, swapped = shared[2], shared[3]
-        sum_ref[core] = halves_ref[core]
-        sum_ref[1 - core] = swapped[...]
-        pairs = pl.num_programs(0)
-        for back in (1, 0):
-            sib_copy(pairs - 1 - back).wait_send()
-        lax.fori_loop(0, pairs, lambda pair, _: (sib_copy(pair).wait_recv(), 0)[1], 0)
-
-
-def attend_back_pallas(shape, q, own, sib, p, o, inv, do, keep, away, result, seq_count, plan, unit=512):
+        sib_copy(sib, sib_ref, sib_sem, j).start()
+
+
+def backward(
+    shape, plan, hidden_t, attended, branch, d_ff, sums, mixed, d_gate, d_up, q, own, sib, p, inv, do, result, seq_count,
+    tiles=3, talls=8, unit=256,
+):
     seqs, bits = shape["seq"], (shape["fsdp"] // 2).bit_length() - 1
-    rows, width = q.shape
-    pairs = width // 128
-    part = own.shape[0]
+    chips = seqs << bits
+    rows, width = attended.shape
+    units = mixed.shape[1]
+    fold = units // width
+    tile = units // 2 // tiles
+    tall, out_cols = fold * width // 2, (width + NORM_COLS) // 2
+    cols = units + tall + out_cols
+    pieces = sum_pieces(units, tall, out_cols, bits)
+    sum_rows = width // chips
+    pairs, turns, part = width // 128, rows // unit, own.shape[0]
+    first_steps, second_steps = 4 * tiles + talls + 1, pairs * turns
+    steps = first_steps + second_steps
     low = jnp.bfloat16
-    keep, away = (array.reshape(seqs, 1 << bits, -1, array.shape[1]) for array in (keep, away))
-    sum_rows, sum_cols = keep.shape[2:]
-    pieces = halves_of(sum_cols, bits)
-    row = pl.BlockSpec((unit, 128), lambda j, i: (i, j))
+    once = pl.Buffered(1)
+    full = lambda array: pl.BlockSpec(array.shape, lambda s: (0, 0), pipeline_mode=once)
+
+    def later(s):
+        return lax.div(s + second_steps, steps)
+
+    def pair_of(s):
+        return lax.div((s - first_steps) * later(s), turns)
+
+    def turn_of(s):
+        return lax.rem((s - first_steps) * later(s), turns)
+
+    def reached(s, first, count):
+        return sum(lax.div(s + steps - first - k, steps) for k in range(1, count))
+
+    def half_tile(away_at, keep_at):
+        def at(s):
+            core = lax.rem(lax.axis_index("fsdp"), 2)
+            kept = lax.div(s + steps - keep_at, steps)
+            t = reached(s, away_at, tiles) * (1 - kept) + reached(s, keep_at, tiles) * kept
+            return (0, (1 - core + (2 * core - 1) * kept) * tiles + t)
+
+        return pl.BlockSpec((rows, tile), at)
+
+    row = pl.BlockSpec((unit, 128), lambda s: (turn_of(s), pair_of(s)))
     kv = [
-        pl.BlockSpec((part, 128), lambda j, i: (0, 2 * j)),
-        pl.BlockSpec((part, 128), lambda j, i: (0, 2 * j + 1)),
+        pl.BlockSpec((part, 128), lambda s: (0, 2 * pair_of(s))),
+        pl.BlockSpec((part, 128), lambda s: (0, 2 * pair_of(s) + 1)),
     ]
     any_space = pl.BlockSpec(memory_space=pl.ANY)
     dma = pltpu.SemaphoreType.DMA
+    form = (seqs, 1 << bits, sum_rows)
     return pl.pallas_call(
-        functools.partial(attend_back_kernel, seqs, bits, pieces, plan),
-        grid=(pairs, rows // unit),
+        functools.partial(back_kernel, seqs, bits, pieces, plan, tiles, talls, fold, turns),
+        grid=(steps,),
         in_specs=[
-            row, *kv, *kv, pl.BlockSpec((2, 2 * part, unit), lambda j, i: (j, 0, i)), row, row, row,
-            any_space, any_space, any_space,
+            full(hidden_t), full(attended), full(branch), full(d_ff), full(sums),
+            pl.BlockSpec((rows, units // talls), lambda s: (0, reached(s, 4 * tiles, talls))),
+            half_tile(0, 2 * tiles), half_tile(tiles, 3 * tiles),
+            row, *kv, *kv, pl.BlockSpec((2, 2 * part, unit), lambda s: (pair_of(s), 0, turn_of(s))), row, row, any_space,
         ],
         out_specs=[
             row,
-            pl.BlockSpec((2, part, 128), lambda j, i: (0, 0, j)),
+            pl.BlockSpec((2, part, 128), lambda s: (0, 0, pair_of(s))),
             any_space,
-            pl.BlockSpec((2, sum_rows // 2, sum_cols), lambda j, i: (0, 0, 0)),
+            pl.BlockSpec((2, sum_rows // 2, cols), lambda s: (0, 0, 0)),
             any_space,
         ],
         out_shape=[
             jax.ShapeDtypeStruct((rows, width), jnp.float32),
             jax.ShapeDtypeStruct((2, part, width), jnp.float32),
             jax.ShapeDtypeStruct((2, part, width), low),
-            jax.ShapeDtypeStruct((2, sum_rows // 2, sum_cols), jnp.float32),
+            jax.ShapeDtypeStruct((2, sum_rows // 2, cols), jnp.float32),
             jax.ShapeDtypeStruct((seq_count, rows // seq_count, width), low),
         ],
         scratch_shapes=[
+            pltpu.VMEM((*form, cols), low),
+            pltpu.VMEM((*form, cols), low),
+            pltpu.VMEM((2, *form, tile), low),
+            pltpu.VMEM((2, chips // talls, sum_rows, tall), low),
+            dma((2, 2 * tiles + 1 + talls)),
             pltpu.VMEM((2, 128, 2 * part), low),
             pltpu.VMEM((2, 2 * part, 128), low),
             pltpu.VMEM((2 * part, 128), jnp.float32),
             pltpu.VMEM((2 * part, 128), jnp.float32),
             pltpu.VMEM((2, 2, part, 128), low),
             dma((2, pairs)),
-            pltpu.VMEM(keep.shape, low),
-            dma,
             dma((3, seq_count)),
-            *reducer_scratch(seqs, bits, pieces, sum_rows, sum_cols),
+            *reducer_scratch(seqs, bits, pieces, GROUPS, sum_rows, cols),
         ],
-        compiler_params=pltpu.CompilerParams(
-            collective_id=1, has_side_effects=True, vmem_limit_bytes=62 << 20
-        ),
-        name="attend_back",
-    )(q, own, own, sib, sib, p, o, inv, do, keep, away, result)
+        compiler_params=pltpu.CompilerParams(collective_id=1, has_side_effects=True, vmem_limit_bytes=63 << 20),
+        name="backward",
+    )(hidden_t, attended, branch, d_ff, sums, mixed, d_gate, d_up, q, own, own, sib, sib, p, inv, do, result)
 
 
 def tail_kernel(
     seqs, bits, pieces,
     cos_ref, sin_ref, dq_ref, own_ref, got_ref, wq_ref, wk_ref, wv_ref, dr_ref, x_ref, sum_ref,
     back_ref, qsum_ref, square_ref,
-    dproj, dx, keep, away, plane, line_sum, back_sem, plane_sem, total_sem, *shared,
+    dproj, dx, keep, got, away, plane, line_sum, back_sem, plane_sem, total_sem, *shared,
 ):
     z, chip, core = place()
     f = 2 * chip + core
@@ -1086,7 +1309,7 @@
     i = pl.program_id(0)
     blocks = dx.shape[0]
     low = jnp.bfloat16
-    start, stage_of, line_of, finish, own = reducer(seqs, bits, pieces, away, keep, *shared)
+    start, sum_task, finish = reducer(seqs, bits, pieces, ((0, 1),), away, keep, got, *shared)
     back_begin, back_end = returns(seqs, back_ref.shape[0], lambda n: dx.at[n], back_ref, back_sem, block)
 
     @pl.when(i == 0)
@@ -1122,16 +1345,10 @@
                 target[:, :, :, n * tile : (n + 1) * tile] = grad.reshape(target.shape[:3] + (tile,))
             if target is away:
                 start()
-        order = [*range(1, seqs), 0]
-        for k in order:
-            stage_of(0, own(k))
-        for stage in range(1, bits):
-            for k in order:
-                stage_of(stage, own(k))
-        for k in order[:-1]:
-            line_of(own(k))
+        for task in sum_plan(seqs, bits):
+            sum_task(0, *task)
         finish()
-        halves_ref, swapped = shared[2], shared[3]
+        halves_ref, swapped = shared[0], shared[1]
         qsum_ref[core] = halves_ref[core]
         qsum_ref[1 - core] = swapped[...]
         squares = jnp.sum(jnp.square(sum_ref[...])) + jnp.sum(jnp.square(qsum_ref[...]))
@@ -1200,14 +1417,13 @@
         scratch_shapes=[
             pltpu.VMEM((rows, 3 * width), low),
             pltpu.VMEM((blocks, block, width), low),
-            pltpu.VMEM((seqs, 1 << bits, sum_rows, sum_cols), low),
-            pltpu.VMEM((seqs, 1 << bits, sum_rows, sum_cols), low),
+            *[pltpu.VMEM((seqs, 1 << bits, sum_rows, sum_cols), low)] * 3,
             pltpu.VMEM((line, 8, 128), jnp.float32),
             pltpu.VMEM((seqs, 8, 128), jnp.float32),
             dma((3, blocks)),
             dma((2, line)),
             dma((2, seqs)),
-            *reducer_scratch(seqs, bits, pieces, sum_rows, sum_cols),
+            *reducer_scratch(seqs, bits, pieces, ((0, 1),), sum_rows, sum_cols),
         ],
         compiler_params=pltpu.CompilerParams(collective_id=2, has_side_effects=True, vmem_limit_bytes=60 << 20),
         name="tail",
@@ -1223,20 +1439,20 @@
     clip = jnp.minimum(1.0, MAX_NORM / (norm + 1e-06))
     rows, units = states[2].shape
     width = states[1].shape[1]
-    tall, wide, out = units // 2, units // 2, (width + NORM_COLS) // 2
-    at = tall + 2 * wide
+    out = (width + NORM_COLS) // 2
     take = lambda first, count: jnp.concatenate([sum_ref[n, :, first : first + count] for n in range(2)], 1)
     fold = states[4].shape[0] // rows
-    red_out = take(at, out)
+    tall = fold * width // 2
+    red_out = take(units + tall, out)
     norms = red_out[:, width : width + 128].T[: states[5].shape[0]]
     grads = (
         jnp.concatenate([qsum_ref[0], qsum_ref[1]], 1),
         red_out[:, :width],
-        take(tall, wide),
-        take(tall + wide, wide),
+        take(0, units // 2),
+        take(units // 2, units // 2),
         jnp.concatenate(
             [
-                jnp.concatenate([sum_ref[n, :, a * (width // 2) : (a + 1) * (width // 2)] for n in range(2)], 1)
+                jnp.concatenate([sum_ref[n, :, units + a * (width // 2) : units + (a + 1) * (width // 2)] for n in range(2)], 1)
                 for a in range(fold)
             ],
             0,
@@ -1267,6 +1483,16 @@
         compiler_params=pltpu.CompilerParams(vmem_limit_bytes=56 << 20),
         name="adam",
     )(sums, qsums, squares, back, *states)
+
+
+def sum_plan(seqs, bits):
+    order = sorted(range(seqs), key=lambda zm: (z_low(zm) if zm else seqs, zm))
+    found = []
+    for n in range(seqs + bits):
+        for stage in reversed(range(bits + 1)):
+            if 0 <= n - stage < seqs and (stage < bits or order[n - stage]):
+                found.append((stage, order[n - stage]))
+    return found
 
 
 def halves_of(cols, bits):
@@ -1328,7 +1554,6 @@
     part, rows = own_ref.shape[0], q_ref.shape[0]
     keys = 2 * part
     j, pairs = pl.program_id(0), pl.num_programs(0)
-    step = j * pl.num_programs(1) + pl.program_id(1)
     which = range(len(pieces))
 
     def kv_copy(first, count, n):
@@ -1347,7 +1572,7 @@
         else:
             hops(which, distance, (level,))
 
-    @pl.when(step == 0)
+    @pl.when(j == 0)
     def _():
         greet(sum_peers(bits) + line_peers(seqs))
         code_copy.start()
@@ -1356,38 +1581,38 @@
         lax.fori_loop(1, pairs, lambda n, _: (pair_copy(n).start(), 0)[1], 0)
         code_copy.wait_recv()
 
-    for at in [at for at in plan if at is not None]:
-
-        @pl.when(step == at)
-        def _():
-            for task in plan[at]:
-                carry(*task)
+    def slot(n):
+        for at in [at for at in plan if at is not None and at % SLOTS == n]:
+
+            @pl.when(j == at // SLOTS)
+            def _():
+                for task in plan[at]:
+                    carry(*task)
 
     low_k = lax.broadcasted_iota(jnp.int32, (part, 128), 1) < HEAD_DIM
 
-    @pl.when(pl.program_id(1) == 0)
-    def _():
-        pair_copy(j).wait_recv()
-        sides = (
-            (own_ref[:, :128], code_ref[...], own_ref[:, 128:]),
-            (
-                sib[:, pl.ds(pl.multiple_of(256 * j, 128), 128)],
-                sib[:, sib.shape[1] - 128 :],
-                sib[:, pl.ds(pl.multiple_of(256 * j + 128, 128), 128)],
-            ),
-        )
-        for i, (k, kc, v) in enumerate(sides):
-            one = jnp.ones_like(v)
-            here = slice(i * part, (i + 1) * part)
-            ka[0, here] = jnp.where(low_k, k, kc)
-            ka[1, here] = jnp.where(low_k, kc, k)
-            vt[0, :, here] = jnp.where(low_k, v, one).T
-            vt[1, :, here] = jnp.where(low_k, one, v).T
-
+    pair_copy(j).wait_recv()
+    sides = (
+        (own_ref[:, :128], code_ref[...], own_ref[:, 128:]),
+        (
+            sib[:, pl.ds(pl.multiple_of(256 * j, 128), 128)],
+            sib[:, sib.shape[1] - 128 :],
+            sib[:, pl.ds(pl.multiple_of(256 * j + 128, 128), 128)],
+        ),
+    )
+    for i, (k, kc, v) in enumerate(sides):
+        one = jnp.ones_like(v)
+        here = slice(i * part, (i + 1) * part)
+        ka[0, here] = jnp.where(low_k, k, kc)
+        ka[1, here] = jnp.where(low_k, kc, k)
+        vt[0, :, here] = jnp.where(low_k, v, one).T
+        vt[1, :, here] = jnp.where(low_k, one, v).T
     low_q = lax.broadcasted_iota(jnp.int32, (unit, 128), 1) < HEAD_DIM
     units = [(h, b) for b in range(rows // unit) for h in range(2)]
     results, before = {}, None
     for u, now in enumerate([*units, None]):
+        if u < SLOTS:
+            slot(u)
         if now is not None:
             h, b = now
             q, qc = q_ref[b * unit : (b + 1) * unit], qc_ref[b * unit : (b + 1) * unit]
@@ -1415,7 +1640,7 @@
         inv_ref[b * unit : (b + 1) * unit] = inv
         o_ref[b * unit : (b + 1) * unit] = (jnp.where(low_q, r0, r1) * inv).astype(jnp.bfloat16)
 
-    @pl.when(step == pairs * pl.num_programs(1) - 1)
+    @pl.when(j == pairs - 1)
     def _():
         keep = pltpu.make_async_copy(sib, sib_hbm, keep_sem)
         keep.start()
@@ -1429,30 +1654,30 @@
         keep.wait()
 
 
-def attend_pallas(shape, pieces, plan, q, qc, own, rest_all, down_all, unit=512, chunk=512, block=512):
+def attend_pallas(shape, pieces, plan, q, qc, own, rest_all, down_all, unit=512, chunk=512):
     seqs, bits = shape["seq"], (shape["fsdp"] // 2).bit_length() - 1
     rows, width = q.shape
     pairs = width // 128
     part = own.shape[0]
     low = jnp.bfloat16
-    row = pl.BlockSpec((block, 128), lambda j, i: (i, j))
+    row = pl.BlockSpec((rows, 128), lambda j: (0, j))
     any_space = pl.BlockSpec(memory_space=pl.ANY)
     dma = pltpu.SemaphoreType.DMA
     like = lambda array: jax.ShapeDtypeStruct(array.shape, array.dtype)
 
     return pl.pallas_call(
         functools.partial(attend_kernel, seqs, bits, pieces, plan, unit, chunk),
-        grid=(pairs, rows // block),
+        grid=(pairs,),
         in_specs=[
             row,
-            pl.BlockSpec((block, 128), lambda j, i: (i, 0)),
-            pl.BlockSpec((part, 256), lambda j, i: (0, j)),
-            pl.BlockSpec((part, 128), lambda j, i: (0, 2 * pairs)),
+            pl.BlockSpec((rows, 128), lambda j: (0, 0)),
+            pl.BlockSpec((part, 256), lambda j: (0, j)),
+            pl.BlockSpec((part, 128), lambda j: (0, 2 * pairs)),
             any_space,
             any_space,
             any_space,
         ],
-        out_specs=[pl.BlockSpec((2, 2 * part, block), lambda j, i: (j, 0, i)), row, row, any_space, any_space, any_space],
+        out_specs=[pl.BlockSpec((2, 2 * part, rows), lambda j: (j, 0, 0)), row, row, any_space, any_space, any_space],
         out_shape=[
             jax.ShapeDtypeStruct((2 * pairs, 2 * part, rows), low),
             jax.ShapeDtypeStruct((rows, width), low),
@@ -1481,9 +1706,9 @@
 
 
 def middle_kernel(
-    seqs, seq_count, x_ref, att_ref, cot_hbm, wo_ref, wg_ref, wu_ref, wd_ref, norms_ref,
+    seqs, seq_count, x_ref, att_ref, cot_hbm, rest_hbm, down_hbm, norms_ref,
     out_ref, dr_ref, branch_ref, datt_ref, hid_ref, mixed_ref, dgate_ref, dup_ref, dff_ref, sums_ref,
-    silu_s, slope_s, dy_s, dy_sem,
+    silu_s, slope_s, dy_s, dy_sem, wo_s, wg_s, wu_s, wd_s, weight_sem,
 ):
     blocks, block = dy_s.shape[:2]
     subs = blocks // seq_count
@@ -1491,30 +1716,52 @@
         seqs, seq_count, lambda s, sub: cot_hbm.at[s, pl.ds(sub * block, block)], lambda n: dy_s.at[n], dy_sem, subs
     )
 
+    units, width = wd_s.shape
+    step = 768
+    cuts = [slice(n, n + step) for n in range(0, units, step)]
+    out_at = 2 * units
+    loads = [pltpu.make_async_copy(rest_hbm.at[:, pl.ds(out_at, width)], wo_s, weight_sem.at[0])]
+    for n, cut in enumerate(cuts):
+        for m, (source, target) in enumerate(
+            (
+                (rest_hbm.at[:, pl.ds(cut.start, step)], wg_s.at[:, pl.ds(cut.start, step)]),
+                (rest_hbm.at[:, pl.ds(units + cut.start, step)], wu_s.at[:, pl.ds(cut.start, step)]),
+                (down_hbm.at[pl.ds(cut.start, step)], wd_s.at[pl.ds(cut.start, step)]),
+            )
+        ):
+            loads.append(pltpu.make_async_copy(source, target, weight_sem.at[1 + 3 * n + m]))
+
+    def ready(first, count):
+        @pl.when(pl.program_id(0) == 0)
+        def _():
+            for load in loads[first : first + count]:
+                load.wait()
+
     @pl.when(pl.program_id(0) == 0)
     def _():
+        for load in loads:
+            load.start()
         greet(column_peers(seqs))
         begin()
 
+    ready(0, 1)
     gain_one, shift_one, gain_two, shift_two = (norms_ref[n : n + 1] for n in range(4))
-    resid_one = x_ref[...].astype(jnp.float32) + dotf(att_ref[...], wo_ref[...])
+    resid_one = x_ref[...].astype(jnp.float32) + dotf(att_ref[...], wo_s[...])
     hidden, normed_one, inv_one = normalize(resid_one, gain_one, shift_one)
     hidden_low = hidden.astype(jnp.bfloat16)
-    hid_ref[...] = hidden_low
-    hidden_units = wd_ref.shape[0]
-    step = 768
-    cuts = [slice(n, n + step) for n in range(0, hidden_units, step)]
+    hid_ref[...] = hidden_low.T
     resid_two = hidden
-    for cut in cuts:
-        gate = dotf(hidden_low, wg_ref[:, cut])
-        up = dotf(hidden_low, wu_ref[:, cut])
+    for n, cut in enumerate(cuts):
+        ready(1 + 3 * n, 3)
+        gate = dotf(hidden_low, wg_s[:, cut])
+        up = dotf(hidden_low, wu_s[:, cut])
         sig = jax.nn.sigmoid(gate)
         silu = gate * sig
         mixed = (silu * up).astype(jnp.bfloat16)
         silu_s[:, cut] = silu
         slope_s[:, cut] = up * sig * (1.0 + gate * (1.0 - sig))
         mixed_ref[:, cut] = mixed
-        resid_two = resid_two + dotf(mixed, wd_ref[cut, :])
+        resid_two = resid_two + dotf(mixed, wd_s[cut, :])
     result, normed_two, inv_two = normalize(resid_two, gain_two, shift_two)
     out_ref[...] = result.astype(jnp.bfloat16)
     now = row_order(seq_count, subs, pl.program_id(0))
@@ -1525,17 +1772,17 @@
     dff_ref[...] = d_ff
     d_hidden = d_two
     for cut in cuts:
-        d_mixed = dotf(d_ff, wd_ref[cut, :], NT)
+        d_mixed = dotf(d_ff, wd_s[cut, :], NT)
         d_up = (d_mixed * silu_s[:, cut]).astype(jnp.bfloat16)
         d_gate = (d_mixed * slope_s[:, cut]).astype(jnp.bfloat16)
         dup_ref[:, cut] = d_up
         dgate_ref[:, cut] = d_gate
-        d_hidden = d_hidden + dotf(d_gate, wg_ref[:, cut], NT) + dotf(d_up, wu_ref[:, cut], NT)
+        d_hidden = d_hidden + dotf(d_gate, wg_s[:, cut], NT) + dotf(d_up, wu_s[:, cut], NT)
     d_one = normalize_back(d_hidden, normed_one, inv_one, gain_one)
     dr_ref[...] = d_one
     branch = d_one.astype(jnp.bfloat16)
     branch_ref[...] = branch
-    datt_ref[...] = dotf(branch, wo_ref[...], NT).astype(jnp.bfloat16)
+    datt_ref[...] = dotf(branch, wo_s[...], NT).astype(jnp.bfloat16)
 
     @pl.when(pl.program_id(0) == 0)
     def _():
@@ -1559,8 +1806,7 @@
     seq_count, local_len = cotangent.shape[:2]
     subs = local_len // block
     row = lambda cols: pl.BlockSpec((block, cols), lambda i: (row_order(seq_count, subs, i), 0))
-    once = pl.Buffered(1)
-    weight = lambda shape, n: pl.BlockSpec(shape, lambda i: (0, n), pipeline_mode=once)
+    any_space = pl.BlockSpec(memory_space=pl.ANY)
     like = lambda cols, dtype: jax.ShapeDtypeStruct((rows, cols), dtype)
     low = jnp.bfloat16
     return pl.pallas_call(
@@ -1568,15 +1814,17 @@
         grid=(rows // block,),
         in_specs=[
             row(width), row(width), pl.BlockSpec(memory_space=pl.ANY),
-            weight((width, width), 2 * units // width), weight((width, units), 0), weight((width, units), 1),
-            weight((units, width), 0), weight((8, width), 0),
+            any_space, any_space, pl.BlockSpec((8, width), lambda i: (0, 0)),
         ],
         out_specs=[
-            row(width), row(width), row(width), row(width), row(width), row(units), row(units), row(units), row(width),
+            row(width), row(width), row(width), row(width),
+            pl.BlockSpec((width, block), lambda i: (0, row_order(seq_count, subs, i))),
+            row(units), row(units), row(units), row(width),
             pl.BlockSpec((8, width), lambda i: (0, 0)),
         ],
         out_shape=[
-            like(width, low), like(width, jnp.float32), like(width, low), like(width, low), like(width, low),
+            like(width, low), like(width, jnp.float32), like(width, low), like(width, low),
+            jax.ShapeDtypeStruct((width, rows), low),
             like(units, low), like(units, low), like(units, low), like(width, low),
             jax.ShapeDtypeStruct((8, width), jnp.float32),
         ],
@@ -1585,143 +1833,29 @@
             pltpu.VMEM((block, units), jnp.float32),
             pltpu.VMEM((rows // block, block, width), low),
             pltpu.SemaphoreType.DMA((3, rows // block)),
+            pltpu.VMEM((width, width), low),
+            pltpu.VMEM((width, units), low),
+            pltpu.VMEM((width, units), low),
+            pltpu.VMEM((units, width), low),
+            pltpu.SemaphoreType.DMA((1 + 3 * (units // 768),)),
         ],
         compiler_params=pltpu.CompilerParams(collective_id=4, has_side_effects=True, vmem_limit_bytes=61 << 20),
         name="middle",
-    )(x, attended, cotangent, rest, rest, rest, down, norms)
-
-
-def grad_wide_kernel(tiles, core_ref, left_ref, right_ref, *refs):
-    keep_ref, send_ref = refs[-2:]
-    value = dotf(left_ref[...], right_ref[...], TN).astype(jnp.bfloat16)
-
-    @pl.when(pl.program_id(0) < tiles)
-    def _():
-        send_ref[...] = value
-
-    @pl.when(pl.program_id(0) >= tiles)
-    def _():
-        keep_ref[...] = value
-
-
-def grad_wide(core, left, right, held, offset, tile=512):
-    rows, width = left.shape
-    half = right.shape[1] // 2
-    tiles = half // tile
-    first = offset // tile
-    like = jax.ShapeDtypeStruct(held[0].shape, jnp.bfloat16)
-    return pl.pallas_call(
-        functools.partial(grad_wide_kernel, tiles),
-        grid_spec=pltpu.PrefetchScalarGridSpec(
-            num_scalar_prefetch=1,
-            grid=(2 * tiles,),
-            in_specs=[
-                pl.BlockSpec((rows, width), lambda i, c: (0, 0)),
-                pl.BlockSpec(
-                    (rows, tile), lambda i, c: (0, lax.rem(c[0] + 1 + lax.div(i, tiles), 2) * tiles + lax.rem(i, tiles))
-                ),
-                pl.BlockSpec(memory_space=pl.ANY),
-                pl.BlockSpec(memory_space=pl.ANY),
-            ],
-            out_specs=[
-                pl.BlockSpec((width, tile), lambda i, c: (0, first + jnp.maximum(i - tiles, 0))),
-                pl.BlockSpec((width, tile), lambda i, c: (0, first + jnp.minimum(i, tiles - 1))),
-            ],
-        ),
-        out_shape=[like, like],
-        input_output_aliases={3: 0, 4: 1},
-        compiler_params=pltpu.CompilerParams(vmem_limit_bytes=48 << 20),
-        name="grad_wide",
-    )(core, left, right, *held)
-
-
-def halves(value, core, keep_ref, send_ref):
-    half = value.shape[1] // 2
-    low, high = value[:, :half].astype(jnp.bfloat16), value[:, half:].astype(jnp.bfloat16)
-    keep_ref[...] = jnp.where(core == 0, low, high)
-    send_ref[...] = jnp.where(core == 0, high, low)
-
-
-def grad_tall_kernel(rows, core_ref, left_ref, right_ref, keep_ref, send_ref):
-    value = dotf(left_ref[...], right_ref[...], TN)
-    half = value.shape[1] // 2
-    turns = keep_ref.shape[1] // half
-    core = core_ref[0]
-    for n, part in enumerate((value[:, :half], value[:, half:])):
-        wide = jnp.concatenate(
-            [
-                jnp.concatenate([part[(b * turns + a) * rows : (b * turns + a + 1) * rows] for a in range(turns)], 1)
-                for b in range(part.shape[0] // (turns * rows))
-            ],
-            0,
-        ).astype(jnp.bfloat16)
-
-        @pl.when(core == n)
-        def _():
-            keep_ref[...] = wide
-
-        @pl.when(core != n)
-        def _():
-            send_ref[...] = wide
-
-
-def grad_tall(core, left, right, rows, cols, tile=384):
-    depth, height = left.shape
-    width = right.shape[1]
-    devices = height // (rows * (height // width))
-    fold = height // (devices * rows)
-    tile_rows = tile // fold
-    out = pl.BlockSpec((tile_rows, fold * width // 2), lambda i, c: (i, 0))
-    like = jax.ShapeDtypeStruct((height // fold, cols), jnp.bfloat16)
-    return pl.pallas_call(
-        functools.partial(grad_tall_kernel, rows),
-        grid_spec=pltpu.PrefetchScalarGridSpec(
-            num_scalar_prefetch=1,
-            grid=(height // tile,),
-            in_specs=[
-                pl.BlockSpec((depth, tile), lambda i, c: (0, i)),
-                pl.BlockSpec((depth, width), lambda i, c: (0, 0)),
-            ],
-            out_specs=[out, out],
-        ),
-        out_shape=[like, like],
-        compiler_params=pltpu.CompilerParams(vmem_limit_bytes=48 << 20),
-        name="grad_tall",
-    )(core, left, right)
-
-
-def grad_out_kernel(core_ref, left_ref, right_ref, sums_ref, _keep, _send, keep_ref, send_ref):
-    value = dotf(left_ref[...], right_ref[...], TN)
-    pad = jnp.zeros((NORM_COLS - sums_ref.shape[0], sums_ref.shape[1]), jnp.float32)
-    norms = jnp.concatenate([sums_ref[...], pad], 0).T
-    halves(jnp.concatenate([value, norms], 1), core_ref[0], keep_ref, send_ref)
-
-
-def grad_out(core, left, right, sums, held, offset):
-    width = left.shape[1]
-    full = lambda array: pl.BlockSpec(array.shape, lambda i, c: (0, 0))
-    half = (width + NORM_COLS) // 2
-    out = pl.BlockSpec((width, half), lambda i, c: (0, offset // half))
-    like = jax.ShapeDtypeStruct(held[0].shape, jnp.bfloat16)
-    any_space = pl.BlockSpec(memory_space=pl.ANY)
-    return pl.pallas_call(
-        grad_out_kernel,
-        grid_spec=pltpu.PrefetchScalarGridSpec(
-            num_scalar_prefetch=1,
-            grid=(1,),
-            in_specs=[full(left), full(right), full(sums), any_space, any_space],
-            out_specs=[out, out],
-        ),
-        out_shape=[like, like],
-        input_output_aliases={4: 0, 5: 1},
-        compiler_params=pltpu.CompilerParams(vmem_limit_bytes=48 << 20),
-        name="grad_out",
-    )(core, left, right, sums, *held)
+    )(x, attended, cotangent, rest, down, norms)
 
 
 NORM_COLS = 256
-PLAN = {1: ((0, 1),), 2: ((0, 2),), 4: ((0, 3), (1, 1)), 6: ((0, 0), (1, 2)), 8: ((1, 3), (2, 1)), 9: ((2, 2),), 10: ((1, 0),), 11: ((2, 3),)}
-GATHER_PLAN = {3: ((1,),), 5: ((1, 0),), 6: ((2,),), 7: ((1, 1),), 8: ((2, 0),), 9: ((3,),), 10: ((2, 1),), 11: ((3, 0),), None: ((3, 1),)}
+SLOTS = 4
+GATHER_PLAN = {
+    7: ((1,),), 10: ((1, 0),), 14: ((2,),), 15: ((1, 1),), 18: ((2, 0),), 20: ((3,),), 21: ((2, 1),), 23: ((3, 0),),
+    None: ((3, 1),),
+}
+PLAN = {
+    13: ((0, 0, 1),), 16: ((0, 0, 3),), 19: ((0, 0, 2),), 21: ((0, 1, 1),), 23: ((0, 0, 0),), 24: ((0, 1, 3),),
+    26: ((0, 2, 1), (1, 0, 1)), 28: ((0, 1, 2), (1, 0, 3)), 29: ((0, 2, 3),), 30: ((0, 1, 0), (1, 0, 2)),
+    32: ((0, 2, 2), (1, 0, 0)), 34: ((1, 1, 1),), 36: ((1, 1, 3),), 38: ((1, 2, 1), (1, 1, 2)), 40: ((1, 2, 3),),
+    41: ((1, 1, 0),), 43: ((1, 2, 2),),
+}
 
 
 def seg_codes(segments):
@@ -1774,16 +1908,9 @@
         result, d_resid_one, d_branch, d_attended, hidden_low, mixed, d_gate, d_up, d_ff, sums,
     ) = middle(shape, x, attended, cotangent, rest, down, norms)
 
-    core_id = core.astype(jnp.int32).reshape(1)
-    own_rows = w_gate.shape[0]
-    half_tall, half_wide, half_out = units * width // 2 // width, units // 2, (width + NORM_COLS) // 2
-    cols = half_tall + 2 * half_wide + half_out
-    held = grad_tall(core_id, mixed, d_ff, own_rows, cols)
-    held = grad_wide(core_id, hidden_low, d_gate, held, half_tall)
-    held = grad_wide(core_id, hidden_low, d_up, held, half_tall + half_wide)
-    held = grad_out(core_id, attended, d_branch, sums, held, half_tall + 2 * half_wide)
-    d_query, d_own, d_got, reduced_sums, output = attend_back_pallas(
-        shape, query, own, sib, probs, attended, inverse_sums, d_attended, *held, result, seq_count, PLAN
+    d_query, d_own, d_got, reduced_sums, output = backward(
+        shape, PLAN, hidden_low, attended, d_branch, d_ff, sums, mixed, d_gate, d_up,
+        query, own, sib, probs, inverse_sums, d_attended, result, seq_count,
     )
     back, qkv_sums, squares = tail(
         shape, cosine, sine, d_query, d_own, d_got, w_all, 0, d_resid_one, x, reduced_sums, seq_count
@@ -1803,8 +1930,8 @@
     seq_count, local_len, width = tokens.shape
     fits = (
         seqs == 2 * seq_count
-        and line & (line - 1) == 0
-        and line >= 4
+        and seqs == 4
+        and line == 8
         and (seq_count * local_len) % 512 == 0
         and w_gate.shape[0] % 8 == 0
         and w_down.shape[0] % 8 == 0

time: 451 us -> 429 us (0.951)
  Pallas kernels: 435 us -> 414 us
    pallas_call x1, Pallas kernels: 60.9 us -> 53 us  [middle(): pl.pallas_call(functools.partial(middle_kernel, shape['seq'], seq_count),...]
    pallas_call x1, Pallas kernels: 69 us -> 63.9 us  [first_gather(): pl.pallas_call(functools.partial(first_gather_kernel, seqs, bits, pieces,...]
    pallas_call x5 -> x1, Pallas kernels: 145 us -> 142 us  [backward(): pl.pallas_call(functools.partial(back_kernel, seqs, bits, pieces, plan, t...]
where the time goes in v5:
time: 429 us; the launch traced here: 425 us
  Pallas kernels  414 us (97%)
  local copies, waits for them, and re-layouts  4.9 us (1%)
  other arithmetic  4.75 us (1%)
    pallas_call x1, Pallas kernels, backward(): pl.pallas_call(functools.partial(back_kernel, seqs, bits, pieces, plan, t...  142 us
    pallas_call x1, Pallas kernels, attend_pallas(): pl.pallas_call(functools.partial(attend_kernel, seqs, bits, pieces, plan,...  77.6 us
    pallas_call x1, Pallas kernels, first_gather(): pl.pallas_call(functools.partial(first_gather_kernel, seqs, bits, pieces,...  63.9 us
    pallas_call x1, Pallas kernels, tail(): pl.pallas_call(functools.partial(tail_kernel, seqs, bits, pieces), grid=(...  63.7 us
    pallas_call x1, Pallas kernels, middle(): pl.pallas_call(functools.partial(middle_kernel, shape['seq'], seq_count),...  53 us

profile of v5, /device:TPU:0, one launch (start us, length us, event | category | flops | bytes accessed | tf_op | source)
XLA Modules:
  0.0 425.3 jit_solution(11634636032047884342)
XLA Ops:
  0.7 0.0 copy-start.6
  0.7 0.0 copy-start.5
  0.7 0.0 copy-start.9
  0.8 0.8 reshape.97.refs_1_
  1.5 0.8 copy.55
  2.3 1.9 fusion.1
  4.2 0.9 pad_maximum_fusion
  5.1 0.0 copy-start.2
  5.1 0.0 copy-start.3
  5.1 0.0 copy-done.6
  5.1 0.0 copy-done.5
  5.1 0.0 copy-done.9
  5.2 0.0 copy-done.4
  5.2 0.0 copy-done.7
  5.2 63.9 %first_gather.1 = (bf16[2,512,768]{2,1,0:T(8,128)(2,1)S(1)}, s32[2,1,512]{2,1,0:T(1,128)S(1)}, bf16[4,4,48,2304]{3,2,1,0:T(8,128)(2,1)}, bf16[4,4,48,7168]{3,2,1,0:T(8,128)(2,1)}, bf16[4,4,192,768]{3,2,1,0:T(8,128)(2,1)}) custom-call(bf16[2,512,768]{2,1,0:T(8,128)(2,1)S(1)} %copy-done.4, s32[2,1,512]{2,1,0:T(1,128)S(1)} %reshape.97.refs_1_, ...), custom_call_target="tpu_custom_call" | custom-call | tf_op jit(solution)/shard_map/first_gather/pallas_call | solution.py:755
  69.0 0.0 copy-start
  69.1 1.1 select_convert_fusion.qc_ref
  70.1 0.2 multiply_convert_fusion.code_ref
  70.4 7.7 %project.1 = (bf16[1024,768]{1,0:T(8,128)(2,1)S(1)}, bf16[1024,1664]{1,0:T(8,128)(2,1)}) custom-call(bf16[1024,768]{1,0:T(8,128)(2,1)S(1)} %bitcast.8, bf16[768,2304]{1,0:T(8,128)(2,1)} %bitcast.13, bf16[768,2304]{1,0:T(8,128)(2,1)} %bitcast.14, bf16[768,2304]{1,0:T(8,128)(2,1)} %bitcast.15, f32[1024,128]{1,0:T(8,128)S(1)} %get-tuple-element.144.cos_ref, ...), custom_call_target="tpu_custom_call" | custom-call | tf_op jit(solution)/shard_map/project/pallas_call | solution.py:1533
  78.1 0.0 copy-done.3
  78.1 0.0 copy-start.1
  78.1 1.1 copy-done.1
  79.3 77.6 %attend.1 = (bf16[12,2048,1024]{2,1,0:T(8,128)(2,1)}, bf16[1024,768]{1,0:T(8,128)(2,1)}, f32[1024,768]{1,0:T(8,128)}, bf16[1024,1664]{1,0:T(8,128)(2,1)}, bf16[4...) custom-call(bf16[1024,768]{1,0:T(8,128)(2,1)} %copy-done.1, ...), custom_call_target="tpu_custom_call", output_to_operand_aliasing={{4}: (5, {}), {5}: (6, {})} | custom-call | tf_op jit(solution)/shard_map/attend/pallas_call | solution.py:1668
  156.9 0.9 slice.4
  157.8 0.1 copy.58
  157.9 0.6 pad_convert_fusion.norms_ref
  158.6 53.0 %middle.1 = (bf16[1024,768]{1,0:T(8,128)(2,1)}, f32[1024,768]{1,0:T(8,128)}, bf16[1024,768]{1,0:T(8,128)(2,1)}, bf16[1024,768]{1,0:T(8,128)(2,1)}, bf16[768,1024...) custom-call(bf16[1024,768]{1,0:T(8,128)(2,1)} %bitcast.9, ...), custom_call_target="tpu_custom_call" | custom-call | tf_op jit(solution)/shard_map/middle/pallas_call | solution.py:1812
  211.6 141.9 %backward.1 = (f32[1024,768]{1,0:T(8,128)}, f32[2,1024,768]{2,1,0:T(8,128)}, bf16[2,1024,768]{2,1,0:T(8,128)(2,1)}, f32[2,24,5120]{2,1,0:T(8,128)}, bf16[2,512,768]{2,1,0:T(8,128)(2,1)}) custom-call(bf16[768,1024]{1,0:T(8,128)(2,1)} %get-tuple-element.94.hid_ref, bf16[1024,768]{1,0:T(8,128)(2,1)} %get-tuple-element.91.att_ref, ...), custom_call_target="tpu_custom_call" | custom-call | tf_op jit(solution)/shard_map/backward/pallas_call | solution.py:1256
  353.5 63.7 %tail.1 = (bf16[2,512,768]{2,1,0:T(8,128)(2,1)}, f32[2,24,1152]{2,1,0:T(8,128)}, f32[8,128]{1,0:T(8,128)}) custom-call(f32[1024,128]{1,0:T(8,128)} %copy-done.2, f32[1024,128]{1,0:T(8,128)} %copy-done.3, f32[1024,768]{1,0:T(8,128)} %get-tuple-element.108.dq_ref, f32[2,1024,768]{2,1,0:T(8,128)} %get-tuple-element.109.own_ref, ...), custom_call_target="tpu_custom_call" | custom-call | tf_op jit(solution)/shard_map/tail/pallas_call | solution.py:1399
  417.2 0.0 copy-start.10
  417.2 6.6 %adam.1 = (f32[24,2304]{1,0:T(8,128)}, f32[24,768]{1,0:T(8,128)}, f32[24,3072]{1,0:T(8,128)}, f32[24,3072]{1,0:T(8,128)}, f32[96,768]{1,0:T(8,128)}, /*index=5*/...) custom-call(f32[2,24,5120]{2,1,0:T(8,128)} %get-tuple-element.107.su, ...), custom_call_target="tpu_custom_call" | custom-call | tf_op jit(solution)/shard_map/adam/pallas_call | solution.py:1478
  423.8 1.1 copy.62
  (12 shorter events, 0.0 us)
Async XLA Ops:
  0.7 4.5 %copy-start.6 = (f32[24,3072]{1,0:T(8,128)S(1)}, f32[24,3072]{1,0:T(8,128)}, u32[]{:S(2)}) copy-start(f32[24,3072]{1,0:T(8,128)} %refs_3_.3) | copy-start | bytes 884740
  0.7 4.5 %copy-start.5 = (f32[24,3072]{1,0:T(8,128)S(1)}, f32[24,3072]{1,0:T(8,128)}, u32[]{:S(2)}) copy-start(f32[24,3072]{1,0:T(8,128)} %refs_2_.3) | copy-start | bytes 884740
  0.7 4.5 %copy-start.9 = (f32[24,768]{1,0:T(8,128)S(1)}, f32[24,768]{1,0:T(8,128)}, u32[]{:S(2)}) copy-start(f32[24,768]{1,0:T(8,128)} %refs_1_.1) | copy-start | bytes 221188
  2.3 2.9 copy-start.4
  2.3 2.9 copy-start.7
  2.3 2.9 copy-start.8
  5.1 73.0 %copy-start.2 = (f32[1024,128]{1,0:T(8,128)}, f32[1024,128]{1,0:T(8,128)S(1)}, u32[]{:S(2)}) copy-start(f32[1024,128]{1,0:T(8,128)S(1)} %get-tuple-element.144.cos_ref) | copy-start | bytes 1572868
  5.1 73.0 %copy-start.3 = (f32[1024,128]{1,0:T(8,128)}, f32[1024,128]{1,0:T(8,128)S(1)}, u32[]{:S(2)}) copy-start(f32[1024,128]{1,0:T(8,128)S(1)} %get-tuple-element.145.sin_ref) | copy-start | bytes 1572868
  69.0 9.1 %copy-start = (bf16[2,512,768]{2,1,0:T(8,128)(2,1)}, bf16[2,512,768]{2,1,0:T(8,128)(2,1)S(1)}, u32[]{:S(2)}) copy-start(bf16[2,512,768]{2,1,0:T(8,128)(2,1)S(1)} %get-tuple-element.84) | copy-start | bytes 4718596
  78.1 1.1 copy-start.1
  417.2 6.7 %copy-start.10 = (bf16[2,512,768]{2,1,0:T(8,128)(2,1)S(1)}, bf16[2,512,768]{2,1,0:T(8,128)(2,1)}, u32[]{:S(2)}) copy-start(bf16[2,512,768]{2,1,0:T(8,128)(2,1)} %get-tuple-element.175) | copy-start | bytes 4718596

commit v6 on v5

--- a/solution.py
+++ b/solution.py
@@ -3,6 +3,7 @@
 
 import jax
 import jax.numpy as jnp
+import numpy as np
 from jax import lax
 from jax.experimental import pallas as pl
 from jax.experimental.pallas import tpu as pltpu
@@ -663,11 +664,11 @@
 def first_gather_kernel(seqs, bits, pieces, early, *refs):
     tokens, segments, gate, up, qkv, out, norm, down = refs[:8]
     x_out, segments_out, qkv_all, rest_all, down_all = refs[8:13]
-    qkv_two, rest_two, down_two, qkv_chip, rest_chip, down_chip, core_sem, own_sem, token_sem, segment_sem = refs[13:23]
+    qkv_two, rest_two, down_two, qkv_chip, rest_chip, down_chip, core_sem, own_sem, token_sem, segment_sem, load_sem = refs[13:24]
     z, chip, core = place()
     wholes = (qkv_all, rest_all, down_all)
     chips = (qkv_chip, rest_chip, down_chip)
-    own_line, own_hops, line, hops, finish_line, finish_hops = gatherer(seqs, bits, pieces, wholes, *refs[23:])
+    own_line, own_hops, line, hops, finish_line, finish_hops = gatherer(seqs, bits, pieces, wholes, *refs[24:])
     seq_count = tokens.shape[0]
     token_begin, token_came, token_sent = departs(
         seqs, seq_count, lambda s, _: tokens.at[s], lambda n: x_out.at[n], token_sem
@@ -675,14 +676,21 @@
     segment_begin, segment_came, segment_sent = departs(
         seqs, seq_count, lambda s, _: segments.at[s], lambda n: segments_out.at[n], segment_sem
     )
+    loads = [
+        pltpu.make_async_copy(qkv, qkv_two.at[core], load_sem.at[0]),
+        pltpu.make_async_copy(down, down_two.at[core], load_sem.at[1]),
+    ]
+    at = 0
+    for n, part in enumerate((gate, up, out, norm)):
+        cols = part.shape[1]
+        loads.append(pltpu.make_async_copy(part, rest_two.at[core, :, pl.ds(at, cols)], load_sem.at[2 + n]))
+        at += cols
+    for load in loads:
+        load.start()
     greet(sum_peers(bits) + column_peers(seqs))
     segment_begin()
-    at = 0
-    for part in (gate, up, out, norm):
-        rest_two[core, :, at : at + part.shape[1]] = part[...]
-        at += part.shape[1]
-    qkv_two[core] = qkv[...]
-    down_two[core] = down[...]
+    for load in loads:
+        load.wait()
     twos = (qkv_two, rest_two, down_two)
     first = [
         pltpu.make_async_remote_copy(
@@ -750,7 +758,6 @@
     dma = pltpu.SemaphoreType.DMA
     low = jnp.bfloat16
     any_space = pl.BlockSpec(memory_space=pl.ANY)
-    vmem = pl.BlockSpec(memory_space=pltpu.VMEM)
     forms = ((rows, qkv.shape[1]), (rows, rest), (rows_down, down.shape[1]))
     *outs, = pl.pallas_call(
         functools.partial(first_gather_kernel, seqs, bits, pieces, (0, 1)),
@@ -759,7 +766,7 @@
             jax.ShapeDtypeStruct(segments.shape, jnp.int32),
             *(jax.ShapeDtypeStruct((seqs, chips, 2 * n, cols), low) for n, cols in forms),
         ],
-        in_specs=[any_space, any_space, *[vmem] * 6],
+        in_specs=[any_space] * 8,
         out_specs=[any_space] * 5,
         scratch_shapes=[
             *(pltpu.VMEM((2, *form), jnp.float32) for form in forms),
@@ -768,9 +775,10 @@
             dma((3,)),
             dma((3, seq_count)),
             dma((3, seq_count)),
+            dma((6,)),
             *gatherer_scratch(seqs, bits, len(pieces)),
         ],
-        compiler_params=pltpu.CompilerParams(collective_id=0, has_side_effects=True, vmem_limit_bytes=48 << 20),
+        compiler_params=pltpu.CompilerParams(collective_id=0, has_side_effects=True, vmem_limit_bytes=63 << 20),
         name="first_gather",
     )(tokens, segments, gate, up, qkv, out, norm, down)
     return outs, pieces[2:]
@@ -1383,7 +1391,7 @@
         back_end()
 
 
-def tail(shape, cosine, sine, d_query, own, got, wide, first, d_resid, x, sums, seq_count, block=256):
+def tail(shape, cosine, sine, d_query, own, got, wide, first, d_resid, x, sums, seq_count, group, block=256):
     seqs, line = shape["seq"], shape["fsdp"]
     bits = (line // 2).bit_length() - 1
     rows, width = x.shape
@@ -1396,11 +1404,12 @@
     once = pl.Buffered(1)
     weight = lambda n: pl.BlockSpec((width, width), lambda i, n=n: (0, first + n), pipeline_mode=once)
     blocks = rows // block
+    turned = pl.BlockSpec((block, 128), sequence_rows(group, blocks))
     return pl.pallas_call(
         functools.partial(tail_kernel, seqs, bits, pieces),
         grid=(blocks,),
         in_specs=[
-            row(128), row(128), row(width), pair, pair, weight(0), weight(1), weight(2), row(width),
+            turned, turned, row(width), pair, pair, weight(0), weight(1), weight(2), row(width),
             pl.BlockSpec(x.shape, lambda i: (0, 0), pipeline_mode=once),
             pl.BlockSpec(sums.shape, lambda i: (0, 0, 0), pipeline_mode=once),
         ],
@@ -1526,20 +1535,38 @@
     kv_ref[:, 2 * width :] = code_ref[...]
 
 
-def project(x, wide, first, cosine, sine, code, block=256):
+def sequence_rows(group, blocks):
+    def at(i):
+        part = lax.rem(2 * lax.axis_index("seq") + lax.rem(lax.axis_index("fsdp"), 2), group)
+        return (part * blocks + i, 0)
+
+    return at
+
+
+def rotary_tables(positions):
+    half_dim = HEAD_DIM // 2
+    inverse = np.exp(np.arange(half_dim, dtype=np.float32) * np.float32(-2.0 * math.log(ROPE_BASE) / HEAD_DIM))
+    angles = (np.arange(positions, dtype=np.float32)[:, None] * inverse[None, :]).astype(np.float64)
+    cosine, sine = np.cos(angles), np.sin(angles)
+    tables = np.concatenate([cosine] * 4, 1), np.concatenate([-sine, sine, -sine, sine], 1)
+    return tuple(jnp.asarray(table.astype(np.float32)) for table in tables)
+
+
+def project(x, wide, first, cosine, sine, code, group, block=256):
     rows, width = x.shape
+    turned = pl.BlockSpec((block, 128), sequence_rows(group, rows // block))
     weight = lambda n: pl.BlockSpec((width, width), lambda i, n=n: (0, first + n))
     row = lambda cols: pl.BlockSpec((block, cols), lambda i: (i, 0))
     return pl.pallas_call(
         project_kernel,
         grid=(rows // block,),
-        in_specs=[row(width), weight(0), weight(1), weight(2), row(128), row(128), row(128)],
+        in_specs=[row(width), weight(0), weight(1), weight(2), turned, turned, row(128)],
         out_specs=[row(width), row(2 * width + 128)],
         out_shape=[
             jax.ShapeDtypeStruct((rows, width), jnp.bfloat16),
             jax.ShapeDtypeStruct((rows, 2 * width + 128), jnp.bfloat16),
         ],
-        compiler_params=pltpu.CompilerParams(vmem_limit_bytes=48 << 20),
+        compiler_params=pltpu.CompilerParams(vmem_limit_bytes=63 << 20),
         name="project",
     )(x, wide, wide, wide, cosine, sine, code)
 
@@ -1696,7 +1723,7 @@
             dma,
             *gatherer_scratch(seqs, bits, len(pieces)),
         ],
-        compiler_params=pltpu.CompilerParams(collective_id=3, has_side_effects=True, vmem_limit_bytes=58 << 20),
+        compiler_params=pltpu.CompilerParams(collective_id=3, has_side_effects=True, vmem_limit_bytes=63 << 20),
         name="attend",
     )(q, qc, own, own, own, rest_all, down_all)
 
@@ -1706,9 +1733,9 @@
 
 
 def middle_kernel(
-    seqs, seq_count, x_ref, att_ref, cot_hbm, rest_hbm, down_hbm, norms_ref,
+    seqs, seq_count, x_ref, att_ref, cot_hbm, rest_hbm, down_hbm,
     out_ref, dr_ref, branch_ref, datt_ref, hid_ref, mixed_ref, dgate_ref, dup_ref, dff_ref, sums_ref,
-    silu_s, slope_s, dy_s, dy_sem, wo_s, wg_s, wu_s, wd_s, weight_sem,
+    silu_s, slope_s, dy_s, dy_sem, wo_s, wg_s, wu_s, wd_s, norm_s, norms, weight_sem,
 ):
     blocks, block = dy_s.shape[:2]
     subs = blocks // seq_count
@@ -1720,7 +1747,10 @@
     step = 768
     cuts = [slice(n, n + step) for n in range(0, units, step)]
     out_at = 2 * units
-    loads = [pltpu.make_async_copy(rest_hbm.at[:, pl.ds(out_at, width)], wo_s, weight_sem.at[0])]
+    loads = [
+        pltpu.make_async_copy(rest_hbm.at[:, pl.ds(out_at + width, 128)], norm_s, weight_sem.at[1 + 3 * len(cuts)]),
+        pltpu.make_async_copy(rest_hbm.at[:, pl.ds(out_at, width)], wo_s, weight_sem.at[0]),
+    ]
     for n, cut in enumerate(cuts):
         for m, (source, target) in enumerate(
             (
@@ -1744,15 +1774,20 @@
         greet(column_peers(seqs))
         begin()
 
-    ready(0, 1)
-    gain_one, shift_one, gain_two, shift_two = (norms_ref[n : n + 1] for n in range(4))
+    ready(0, 2)
+
+    @pl.when(pl.program_id(0) == 0)
+    def _():
+        norms[...] = norm_s[...].astype(jnp.float32).T[: norms.shape[0]]
+
+    gain_one, shift_one, gain_two, shift_two = (norms[n : n + 1] for n in range(4))
     resid_one = x_ref[...].astype(jnp.float32) + dotf(att_ref[...], wo_s[...])
     hidden, normed_one, inv_one = normalize(resid_one, gain_one, shift_one)
     hidden_low = hidden.astype(jnp.bfloat16)
     hid_ref[...] = hidden_low.T
     resid_two = hidden
     for n, cut in enumerate(cuts):
-        ready(1 + 3 * n, 3)
+        ready(2 + 3 * n, 3)
         gate = dotf(hidden_low, wg_s[:, cut])
         up = dotf(hidden_low, wu_s[:, cut])
         sig = jax.nn.sigmoid(gate)
@@ -1800,7 +1835,7 @@
     return lax.rem(step, seq_count) * subs + lax.div(step, seq_count)
 
 
-def middle(shape, x, attended, cotangent, rest, down, norms, block=256):
+def middle(shape, x, attended, cotangent, rest, down, block=256):
     rows, width = x.shape
     units = down.shape[0]
     seq_count, local_len = cotangent.shape[:2]
@@ -1814,7 +1849,7 @@
         grid=(rows // block,),
         in_specs=[
             row(width), row(width), pl.BlockSpec(memory_space=pl.ANY),
-            any_space, any_space, pl.BlockSpec((8, width), lambda i: (0, 0)),
+            any_space, any_space,
         ],
         out_specs=[
             row(width), row(width), row(width), row(width),
@@ -1837,11 +1872,13 @@
             pltpu.VMEM((width, units), low),
             pltpu.VMEM((width, units), low),
             pltpu.VMEM((units, width), low),
-            pltpu.SemaphoreType.DMA((1 + 3 * (units // 768),)),
+            pltpu.VMEM((width, 128), low),
+            pltpu.VMEM((8, width), jnp.float32),
+            pltpu.SemaphoreType.DMA((2 + 3 * (units // 768),)),
         ],
         compiler_params=pltpu.CompilerParams(collective_id=4, has_side_effects=True, vmem_limit_bytes=61 << 20),
         name="middle",
-    )(x, attended, cotangent, rest, down, norms)
+    )(x, attended, cotangent, rest, down)
 
 
 NORM_COLS = 256
@@ -1879,8 +1916,6 @@
     rows = seq_count * local_len
     group = seqs // seq_count
     units = w_gate.shape[1]
-    z = lax.axis_index("seq")
-    core = lax.axis_index("fsdp") % 2
 
     norm_rows = jnp.pad(norm_params.T, ((0, 0), (0, NORM_COLS - norm_params.shape[0])))
     (x, segments, qkv_all, rest_all, down_all), pieces = first_gather(
@@ -1889,31 +1924,24 @@
     x = x.reshape(rows, width)
     w_all = qkv_all.reshape(width, 3 * width)
     q_code, k_code = seg_codes(segments.reshape(rows))
-    positions = ((z * 2 + core) % group * rows + jnp.arange(rows)).astype(jnp.float32)
-    half_dim = HEAD_DIM // 2
-    inverse = jnp.exp(jnp.arange(half_dim, dtype=jnp.float32) * (-2.0 * math.log(ROPE_BASE) / HEAD_DIM))
-    angles = positions[:, None] * inverse[None, :]
-    cosine, sine = jnp.cos(angles), jnp.sin(angles)
-    cosine = jnp.concatenate([cosine] * 4, 1)
-    sine = jnp.concatenate([-sine, sine, -sine, sine], 1)
-
-    query, own = project(x, w_all, 0, cosine, sine, k_code)
+    cosine, sine = rotary_tables(rows * group)
+
+    query, own = project(x, w_all, 0, cosine, sine, k_code, group)
     probs, attended, inverse_sums, sib, rest_all, down_all = attend_pallas(
         shape, pieces, GATHER_PLAN, query, q_code, own, rest_all, down_all
     )
     rest = rest_all.reshape(width, rest_all.shape[-1])
     down = down_all.reshape(units, width)
-    norms = jnp.pad(rest[:, -NORM_COLS : 4 - NORM_COLS].T.astype(jnp.float32), ((0, 4), (0, 0)))
     (
         result, d_resid_one, d_branch, d_attended, hidden_low, mixed, d_gate, d_up, d_ff, sums,
-    ) = middle(shape, x, attended, cotangent, rest, down, norms)
+    ) = middle(shape, x, attended, cotangent, rest, down)
 
     d_query, d_own, d_got, reduced_sums, output = backward(
         shape, PLAN, hidden_low, attended, d_branch, d_ff, sums, mixed, d_gate, d_up,
         query, own, sib, probs, inverse_sums, d_attended, result, seq_count,
     )
     back, qkv_sums, squares = tail(
-        shape, cosine, sine, d_query, d_own, d_got, w_all, 0, d_resid_one, x, reduced_sums, seq_count
+        shape, cosine, sine, d_query, d_own, d_got, w_all, 0, d_resid_one, x, reduced_sums, seq_count, group
     )
     states = (
         w_qkv, w_out, w_gate, w_up, w_down, norm_params,

time: 429 us -> 431 us (level); the launches traced: 425 us -> 423 us
  no operation moved by 1% of the time
where the time goes in v6:
time: 431 us; the launch traced here: 423 us
  Pallas kernels  414 us (96%)
    pallas_call x1, Pallas kernels, backward(): pl.pallas_call(functools.partial(back_kernel, seqs, bits, pieces, plan, t...  142 us
    pallas_call x1, Pallas kernels, attend_pallas(): pl.pallas_call(functools.partial(attend_kernel, seqs, bits, pieces, plan,...  77.6 us
    pallas_call x1, Pallas kernels, tail(): pl.pallas_call(functools.partial(tail_kernel, seqs, bits, pieces), grid=(...  63.8 us
    pallas_call x1, Pallas kernels, first_gather(): pl.pallas_call(functools.partial(first_gather_kernel, seqs, bits, pieces,...  63.2 us
    pallas_call x1, Pallas kernels, middle(): pl.pallas_call(functools.partial(middle_kernel, shape['seq'], seq_count),...  53.1 us

profile of v6, /device:TPU:0, one launch (start us, length us, event | category | flops | bytes accessed | tf_op | source)
XLA Modules:
  0.0 422.5 jit_solution(17852386280249686693)
XLA Ops:
  0.7 1.3 reshape.87.refs_1_
  2.0 0.8 copy.52
  2.7 0.6 pad.4.refs_6_
  3.4 63.2 %first_gather.1 = (bf16[2,512,768]{2,1,0:T(8,128)(2,1)}, s32[2,1,512]{2,1,0:T(1,128)}, bf16[4,4,48,2304]{3,2,1,0:T(8,128)(2,1)}, bf16[4,4,48,7168]{3,2,1,0:T(8,128)(2,1)}, bf16[4,4,192,768]{3,2,1,0:T(8,128)(2,1)}) custom-call(bf16[2,512,768]{2,1,0:T(8,128)(2,1)} %refs_0_.2, s32[2,1,512]{2,1,0:T(1,128)} %reshape.87.refs_1_, f32[24,3072]{1,0:T(8,128)} %refs_2_.3, ...), custom_call_target="tpu_custom_call" | custom-call | tf_op jit(solution)/shard_map/first_gather/pallas_call | solution.py:762
  66.6 1.6 select_convert_fusion.qc_ref
  68.2 1.6 multiply_convert_fusion.code_ref
  69.8 8.3 %project.1 = (bf16[1024,768]{1,0:T(8,128)(2,1)}, bf16[1024,1664]{1,0:T(8,128)(2,1)}) custom-call(bf16[1024,768]{1,0:T(8,128)(2,1)} %bitcast.15, bf16[768,2304]{1,0:T(8,128)(2,1)} %bitcast.7, bf16[768,2304]{1,0:T(8,128)(2,1)} %bitcast.8, bf16[768,2304]{1,0:T(8,128)(2,1)} %bitcast.9, f32[2048,128]{1,0:T(8,128)} %constant.36.clone.cos_ref, ...), custom_call_target="tpu_custom_call" | custom-call | tf_op jit(solution)/shard_map/project/pallas_call | solution.py:1560
  78.1 77.6 %attend.1 = (bf16[12,2048,1024]{2,1,0:T(8,128)(2,1)}, bf16[1024,768]{1,0:T(8,128)(2,1)}, f32[1024,768]{1,0:T(8,128)}, bf16[1024,1664]{1,0:T(8,128)(2,1)}, bf16[4...) custom-call(bf16[1024,768]{1,0:T(8,128)(2,1)} %get-tuple-element.87.q_r, ...), custom_call_target="tpu_custom_call", output_to_operand_aliasing={{4}: (5, {}), {5}: (6, {})} | custom-call | tf_op jit(solution)/shard_map/attend/pallas_call | solution.py:1695
  155.7 53.1 %middle.1 = (bf16[1024,768]{1,0:T(8,128)(2,1)}, f32[1024,768]{1,0:T(8,128)}, bf16[1024,768]{1,0:T(8,128)(2,1)}, bf16[1024,768]{1,0:T(8,128)(2,1)}, bf16[768,1024...) custom-call(bf16[1024,768]{1,0:T(8,128)(2,1)} %bitcast.16, ...), custom_call_target="tpu_custom_call" | custom-call | tf_op jit(solution)/shard_map/middle/pallas_call | solution.py:1847
  208.7 141.8 %backward.1 = (f32[1024,768]{1,0:T(8,128)}, f32[2,1024,768]{2,1,0:T(8,128)}, bf16[2,1024,768]{2,1,0:T(8,128)(2,1)}, f32[2,24,5120]{2,1,0:T(8,128)}, bf16[2,512,768]{2,1,0:T(8,128)(2,1)}) custom-call(bf16[768,1024]{1,0:T(8,128)(2,1)} %get-tuple-element.94.hid_ref, bf16[1024,768]{1,0:T(8,128)(2,1)} %get-tuple-element.91.att_ref, ...), custom_call_target="tpu_custom_call" | custom-call | tf_op jit(solution)/shard_map/backward/pallas_call | solution.py:1264
  350.5 63.8 %tail.1 = (bf16[2,512,768]{2,1,0:T(8,128)(2,1)}, f32[2,24,1152]{2,1,0:T(8,128)}, f32[8,128]{1,0:T(8,128)}) custom-call(f32[2048,128]{1,0:T(8,128)} %constant.36.clone.cos_ref, f32[2048,128]{1,0:T(8,128)} %constant.37.clone.sin_ref, f32[1024,768]{1,0:T(8,128)} %get-tuple-element.108.dq_ref, f32[2,1024,768]{2,1,0:T(8,128)} %get-tuple-element.109.own_ref, ...), custom_call_target="tpu_custom_call" | custom-call | tf_op jit(solution)/shard_map/tail/pallas_call | solution.py:1408
  414.3 0.0 copy-start
  414.3 6.6 %adam.1 = (f32[24,2304]{1,0:T(8,128)}, f32[24,768]{1,0:T(8,128)}, f32[24,3072]{1,0:T(8,128)}, f32[24,3072]{1,0:T(8,128)}, f32[96,768]{1,0:T(8,128)}, /*index=5*/...) custom-call(f32[2,24,5120]{2,1,0:T(8,128)} %get-tuple-element.107.su, ...), custom_call_target="tpu_custom_call" | custom-call | tf_op jit(solution)/shard_map/adam/pallas_call | solution.py:1487
  420.9 0.0 copy-done
  421.0 1.1 copy.56
  (2 shorter events, 0.0 us)
Async XLA Ops:
  414.3 6.7 %copy-start = (bf16[2,512,768]{2,1,0:T(8,128)(2,1)S(1)}, bf16[2,512,768]{2,1,0:T(8,128)(2,1)}, u32[]{:S(2)}) copy-start(bf16[2,512,768]{2,1,0:T(8,128)(2,1)} %get-tuple-element.170) | copy-start | bytes 4718596
